TPU v7x, 32 devices: a whole 2x2x4 slice. The times are simulated.
32 devices in a mesh: clip: 4 (over y, x), py: 4 (over z), px: 2 (over core).
Axes of the slice: x: 2, y: 2, z: 4, core: 2. Of those that a mesh axis runs over, the one named last changes fastest.
Arguments:
- fsq_codes: int32 [6, 8, 64, 64], P(None, 'clip', 'py', 'px'), parts along dimension 1, may hold values from 0 to 7, as said below
- in_weight: bfloat16 [3, 3, 6, 512], replicated, may hold values from -0.875 to 0.875
- res_weight: bfloat16 [512, 3, 3, 512], P(('py', 'px')), may hold values from -0.09375 to 0.09375
- up_weight: bfloat16 [512, 4, 4, 512], P(('py', 'px')), may hold values from -0.125 to 0.125
- first_gain: float32 [512], replicated, may hold values from 0.1 to 1.9
- second_gain: float32 [512], replicated, may hold values from 0.1 to 1.9
Outputs:
- upsampled: bfloat16 [8, 128, 128, 512], P('clip', 'py', 'px'), parts along dimension 0
There are 4 independent parts, one for each index of `clip`. A program takes and returns all parts, laid end to end along the dimension named above; an argument that names none is the same for every part. Nothing has to cross between parts.
Inputs may be any that keep to these rules, and one draw needn't show every extreme that they name: `fsq_codes`: entry d of the first dimension is a level index of FSQ dimension d, below 8 for d = 0, 1, 2 and below 5 for d = 3, 4, 5.
All inputs are finite; a program needn't handle non-finite values.
Results may differ from a plain program's by a relative error of at most 0.0073.
Values may be sent and summed in bfloat16 or wider, within the bound.
No kernel may reach another device: no remote copies, remote signals or barrier semaphores. Data moves between devices by JAX's collectives and lax.ppermute only.
A program may use at most 128 MiB of HBM per device.

v0:
```python
import jax
import jax.numpy as jnp
from jax import lax
from jax.sharding import PartitionSpec as P

GROUPS = 32


fsq_levels = (8, 8, 8, 5, 5, 5)
epsilon = 1e-06
up_taps = (((1, 1), (3, 0)), ((0, 2), (2, 1)))


def with_halo(cells, sides, width):
    for axis, dim in sides:
        count = lax.axis_size(axis)
        ends = count - 1
        head = lax.slice_in_dim(cells, 0, width, axis=dim)
        tail = lax.slice_in_dim(cells, cells.shape[dim] - width, cells.shape[dim], axis=dim)
        cells = jnp.concatenate(
            [
                lax.ppermute(tail, axis, [(i, (i + 1) % count) for i in range(ends)]),
                cells,
                lax.ppermute(head, axis, [((i + 1) % count, i) for i in range(ends)]),
            ],
            axis=dim,
        )
    return cells


def code_values(fsq_codes):
    levels = jnp.array(fsq_levels, jnp.int32).reshape(-1, 1, 1, 1)
    half_range = levels // 2
    values = (fsq_codes - half_range).astype(jnp.float32) / half_range.astype(jnp.float32)
    return jnp.transpose(values, (1, 2, 3, 0)).astype(jnp.bfloat16)


def first_conv(padded, in_weight):
    out_rows = padded.shape[1] - 2
    out_cols = padded.shape[2] - 2
    windows = [
        padded[:, row_tap : row_tap + out_rows, col_tap : col_tap + out_cols, :]
        for row_tap in range(3)
        for col_tap in range(3)
    ]
    stacked = jnp.concatenate(windows, axis=3)
    flat_weight = in_weight.reshape(-1, in_weight.shape[3])
    return jnp.einsum(
        "fhwk,kd->fhwd", stacked, flat_weight, preferred_element_type=jnp.float32
    ).astype(jnp.bfloat16)


def group_norm(interior, region, gain_vec, cell_count):
    channels = interior.shape[3]
    grouped = interior.astype(jnp.float32).reshape(-1, GROUPS, channels // GROUPS)
    average = lax.psum(jnp.sum(grouped, axis=(0, 2)), ("py", "px")) / cell_count
    centred = grouped - average[None, :, None]
    spread = lax.psum(jnp.sum(centred * centred, axis=(0, 2)), ("py", "px")) / cell_count
    inv_std = lax.rsqrt(spread + epsilon)
    average_c = jnp.repeat(average, channels // GROUPS)
    scale_c = jnp.repeat(inv_std, channels // GROUPS)
    normed = (region.astype(jnp.float32) - average_c) * (scale_c * gain_vec)
    return jax.nn.silu(normed)


def feature_halo(source):
    return with_halo(source, (("py", 1), ("px", 2)), 1)


def conv_rows(carried, source, block_rows):
    out_rows = carried.shape[1]
    out_cols = carried.shape[2]
    for row_tap in range(3):
        for col_tap in range(3):
            window = source[:, row_tap : row_tap + out_rows, col_tap : col_tap + out_cols, :]
            carried = carried + jnp.einsum(
                "fhwc,cd->fhwd",
                window,
                block_rows[:, row_tap, col_tap, :],
                preferred_element_type=jnp.float32,
            )
    return carried


def upsample_rows(carried, source, block_rows):
    out_rows = carried[0].shape[1]
    out_cols = carried[0].shape[2]
    phases = []
    for row_phase in range(2):
        for col_phase in range(2):
            phase_sum = carried[2 * row_phase + col_phase]
            for row_kernel, row_offset in up_taps[row_phase]:
                for col_kernel, col_offset in up_taps[col_phase]:
                    window = source[
                        :, row_offset : row_offset + out_rows, col_offset : col_offset + out_cols, :
                    ]
                    phase_sum = phase_sum + jnp.einsum(
                        "fhwc,cd->fhwd",
                        window,
                        block_rows[:, row_kernel, col_kernel, :],
                        preferred_element_type=jnp.float32,
                    )
            phases.append(phase_sum)
    return tuple(phases)


def local(fsq_codes, in_weight, res_weight, up_weight, first_gain, second_gain):
    values = code_values(fsq_codes)
    frames = values.shape[0]
    tile_rows = values.shape[1]
    tile_cols = values.shape[2]
    channels = in_weight.shape[3]
    cell_count = float(
        frames
        * tile_rows
        * lax.axis_size("py")
        * tile_cols
        * lax.axis_size("px")
        * (channels // GROUPS)
    )
    margin = 1
    padded = with_halo(values, (("py", 1), ("px", 2)), margin)
    features = first_conv(padded, in_weight)
    res_slab, up_slab = (
        lax.all_gather(res_weight, "px", axis=0, tiled=True),
        lax.all_gather(up_weight, "px", axis=0, tiled=True),
    )
    active = group_norm(features, features, first_gain, cell_count)
    source = feature_halo(active.astype(jnp.bfloat16))
    start_sum = jnp.zeros(features.shape, jnp.float32)
    branch = conv_rows(start_sum, source, lax.all_gather(res_slab, "py", axis=0, tiled=True))
    hidden = (features.astype(jnp.float32) + branch).astype(jnp.bfloat16)
    upper = feature_halo(group_norm(hidden, hidden, second_gain, cell_count).astype(jnp.bfloat16))
    zero_phase = jnp.zeros((frames, tile_rows, tile_cols, channels), jnp.float32)
    start_phases = (zero_phase, zero_phase, zero_phase, zero_phase)
    phases = upsample_rows(start_phases, upper, lax.all_gather(up_slab, "py", axis=0, tiled=True))
    stacked = jnp.stack([phase.astype(jnp.bfloat16) for phase in phases]).reshape(
        2, 2, frames, tile_rows, tile_cols, channels
    )
    return jnp.transpose(stacked, (2, 3, 0, 4, 1, 5)).reshape(
        frames, 2 * tile_rows, 2 * tile_cols, channels
    )


def solution(mesh):
    placed = (
        P(None, "clip", "py", "px"),
        P(),
        P(("py", "px"), None, None, None),
        P(("py", "px"), None, None, None),
        P(),
        P(),
    )
    return jax.shard_map(
        local, mesh=mesh, in_specs=placed, out_specs=P("clip", "py", "px", None), check_vma=False
    )
```

profile of v0, /device:TPU:0, one launch (start us, length us, event | category | flops | bytes accessed | tf_op | source)
XLA Modules:
  0.0 317.2 jit_solution(9477323930279868848)
XLA Ops:
  7.3 2.8 copy.54
  10.2 10.7 %all-gather.5.cloned.1.call-done = bf16[128,3,3,512]{3,0,2,1:T(8,128)(2,1)} async-done(((bf16[64,3,3,512]{3,0,2,1:T(8,128)(2,1)}), bf16[128,3,3,512]{3,0,2,1:T(8,128)(2,1)}) %all-gather.5.cloned.1.call-update) | async-done | bytes 1179664 | tf_op jit(solution)/shard_map/all_gather | solution.py:125
  20.9 13.2 %all-gather.9.cloned.1.call-done = bf16[128,4,4,512]{3,0,2,1:T(8,128)(2,1)} async-done(((bf16[64,4,4,512]{3,0,2,1:T(8,128)(2,1)}), bf16[128,4,4,512]{3,0,2,1:T(8,128)(2,1)}) %all-gather.9.cloned.1.call-update) | async-done | bytes 2097168 | tf_op jit(solution)/shard_map/all_gather | solution.py:126
  34.3 3.6 %collective-permute-start = (bf16[2,1,32,6]{2,1,0,3:T(2,128)(2,1)S(1)}, bf16[2,1,32,6]{2,1,0,3:T(2,128)(2,1)S(1)}, u32[]{:S(2)}, u32[]{:S(2)}) collective-permute-start(bf16[2,1,32,6]{2,1,0,3:T(2,128)(2,1)S(1)} %get-tuple-element.29), channel_id=1, source_target_pairs={{0,2},{2,4},{4,6},{1,3},{3,5},{5,7},{8,10},{10,12},{12,14},{9,11},... | collective-permute-start | bytes 2312 | tf_op jit(solution)/shard_map/ppermute | solution.py:22
  39.4 4.1 %collective-permute-done.1 = bf16[2,1,32,6]{2,1,0,3:T(2,128)(2,1)S(1)} collective-permute-done((bf16[2,1,32,6]{2,1,0,3:T(2,128)(2,1)S(1)}, bf16[2,1,32,6]{2,1,0,3:T(2,128)(2,1)S(1)}, u32[]{:S(2)}, u32[]{:S(2)}) %collective-permute-start.1) | collective-permute-done | bytes 800 | tf_op jit(solution)/shard_map/ppermute | solution.py:24
  46.3 1.8 collective-permute-done.3
  49.7 15.5 %psum.28 = f32[32]{0:T(128)S(1)} all-reduce(f32[32]{0:T(128)S(1)} %reduce_sum.51), channel_id=1, replica_groups=mesh['clip'=4,'py'=4,'px'=2] {'py','px'}, use_global_device_ids=true, to_apply=%region_2.3 | all-reduce | flops 32 | bytes 256 | tf_op jit(solution)/shard_map/psum | solution.py:56
  65.9 14.2 %psum.29 = f32[32]{0:T(128)S(1)} all-reduce(f32[32]{0:T(128)S(1)} %reduce_sum.54), channel_id=1, replica_groups=mesh['clip'=4,'py'=4,'px'=2] {'py','px'}, use_global_device_ids=true, to_apply=%region_5.6 | all-reduce | flops 32 | bytes 256 | tf_op jit(solution)/shard_map/psum | solution.py:58
  83.8 2.2 collective-permute-done.4
  85.9 10.7 %collective-permute-done.5 = bf16[2,1,32,512]{3,2,1,0:T(8,128)(2,1)S(1)} collective-permute-done((bf16[2,1,32,512]{3,2,1,0:T(8,128)(2,1)S(1)}, bf16[2,1,32,512]{3,2,1,0:T(8,128)(2,1)S(1)}, u32[]{:S(2)}, u32[]{:S(2)}) %collective-permute-start.5) | collective-permute-done | bytes 65568 | tf_op jit(solution)/shard_map/ppermute | solution.py:24
  99.4 1.8 collective-permute-done.7
  101.2 2.0 pad_maximum_fusion.1
  103.2 25.0 %all-gather.7.cloned.1.call-done = bf16[512,3,3,512]{3,0,2,1:T(8,128)(2,1)} async-done(((bf16[128,3,3,512]{3,0,2,1:T(8,128)(2,1)}), bf16[512,3,3,512]{3,0,2,1:T(8,128)(2,1)}) %all-gather.7.cloned.1.call-update) | async-done | bytes 4718608 | tf_op jit(solution)/shard_map/all_gather | solution.py:131
  128.2 1.9 fusion.20
  130.1 1.9 fusion.24
  138.5 14.3 %psum.30 = f32[32]{0:T(128)S(1)} all-reduce(f32[32]{0:T(128)S(1)} %reduce_sum.72), channel_id=1, replica_groups=mesh['clip'=4,'py'=4,'px'=2] {'py','px'}, use_global_device_ids=true, to_apply=%region_8.9 | all-reduce | flops 32 | bytes 256 | tf_op jit(solution)/shard_map/psum | solution.py:56
  153.5 16.2 %psum.31 = f32[32]{0:T(128)S(1)} all-reduce(f32[32]{0:T(128)S(1)} %reduce_sum.75), channel_id=1, replica_groups=mesh['clip'=4,'py'=4,'px'=2] {'py','px'}, use_global_device_ids=true, to_apply=%region_11.12 | all-reduce | flops 32 | bytes 256 | tf_op jit(solution)/shard_map/psum | solution.py:58
  173.2 2.3 collective-permute-done.8
  175.5 4.7 %collective-permute-done.9 = bf16[2,1,32,512]{3,2,1,0:T(8,128)(2,1)S(1)} collective-permute-done((bf16[2,1,32,512]{3,2,1,0:T(8,128)(2,1)S(1)}, bf16[2,1,32,512]{3,2,1,0:T(8,128)(2,1)S(1)}, u32[]{:S(2)}, u32[]{:S(2)}) %collective-permute-start.9) | collective-permute-done | bytes 65568 | tf_op jit(solution)/shard_map/ppermute | solution.py:24
  186.6 93.1 %all-gather.11.cloned.1.call-done = bf16[512,4,4,512]{3,0,2,1:T(8,128)(2,1)} async-done(((bf16[128,4,4,512]{3,0,2,1:T(8,128)(2,1)}), bf16[512,4,4,512]{3,0,2,1:T(8,128)(2,1)}) %all-gather.11.cloned.1.call-update) | async-done | bytes 8388624 | tf_op jit(solution)/shard_map/all_gather | solution.py:136
  281.5 1.9 fusion.71
  283.4 2.5 fusion.35
  297.2 6.3 %copy.55 = bf16[2,16,2,32,2,512]{5,4,3,2,1,0:T(2,128)(2,1)} copy(bf16[2,16,2,32,2,512]{5,3,1,0,4,2:T(8,128)(2,1)S(1)} %bitcast.202) | data formatting | bytes 8388608 | tf_op jit(solution)/shard_map/transpose | solution.py:140
  303.5 7.2 %reshape.55 = bf16[2,32,64,512]{3,2,1,0:T(8,128)(2,1)} reshape(bf16[2,16,2,32,2,512]{5,4,3,2,1,0:T(2,128)(2,1)} %copy.55) | data formatting | bytes 8388608 | tf_op jit(solution)/shard_map/reshape | solution.py:140
  (117 shorter events, 43.7 us)
Async XLA Ops:
  6.5 14.3 %all-gather.5.cloned.1.call-start = ((), (), s32[]{:S(2)}) async-start(), calls=%async_computation | async-start | bytes 1769472 | tf_op jit(solution)/shard_map/all_gather | solution.py:125
  7.3 26.9 %all-gather.9.cloned.1.call-start = ((), (), s32[]{:S(2)}) async-start(), calls=%async_computation.2 | async-start | bytes 3145728 | tf_op jit(solution)/shard_map/all_gather | solution.py:126
  10.1 24.1 %copy-start.5 = (s32[6,2,16,32]{3,2,1,0:T(8,128)S(1)}, s32[6,2,16,32]{3,2,1,0:T(8,128)}, u32[]{:S(2)}) copy-start(s32[6,2,16,32]{3,2,1,0:T(8,128)} %param.7) | copy-start | bytes 73732
  10.1 24.1 %copy-start.7 = (f32[6]{0:T(128)S(1)}, f32[6]{0:T(128)}, u32[]{:S(2)}) copy-start(f32[6]{0:T(128)} %constant.48) | copy-start | bytes 76
  10.1 24.1 %copy-start.8 = (s32[6]{0:T(128)S(1)}, s32[6]{0:T(128)}, u32[]{:S(2)}) copy-start(s32[6]{0:T(128)} %constant.49) | copy-start | bytes 76
  10.1 36.2 %copy-start.6 = (bf16[3,3,6,512]{3,2,1,0:T(8,128)(2,1)S(1)}, bf16[3,3,6,512]{3,2,1,0:T(8,128)(2,1)}, u32[]{:S(2)}) copy-start(bf16[3,3,6,512]{3,2,1,0:T(8,128)(2,1)} %param.8) | copy-start | bytes 165892
  10.1 118.1 %all-gather.7.cloned.1.call-start = ((), (), s32[]{:S(2)}) async-start(), calls=%async_computation.1 | async-start | bytes 5898240 | tf_op jit(solution)/shard_map/all_gather | solution.py:131
  20.9 258.9 %all-gather.11.cloned.1.call-start = ((), (), s32[]{:S(2)}) async-start(), calls=%async_computation.3 | async-start | bytes 10485760 | tf_op jit(solution)/shard_map/all_gather | solution.py:136
  34.3 5.0 %collective-permute-start = (bf16[2,1,32,6]{2,1,0,3:T(2,128)(2,1)S(1)}, bf16[2,1,32,6]{2,1,0,3:T(2,128)(2,1)S(1)}, u32[]{:S(2)}, u32[]{:S(2)}) collective-permute-start(bf16[2,1,32,6]{2,1,0,3:T(2,128)(2,1)S(1)} %get-tuple-element.29), channel_id=1, source_target_pairs={{0,2},{2,4},{4,6},{1,3},{3,5},{5,7},{8,10},{10,12},{12,14},{9,11},... | collective-permute-start | bytes 2312 | tf_op jit(solution)/shard_map/ppermute | solution.py:22
  38.0 5.5 %collective-permute-start.1 = (bf16[2,1,32,6]{2,1,0,3:T(2,128)(2,1)S(1)}, bf16[2,1,32,6]{2,1,0,3:T(2,128)(2,1)S(1)}, u32[]{:S(2)}, u32[]{:S(2)}) collective-permute-start(bf16[2,1,32,6]{2,1,0,3:T(2,128)(2,1)S(1)} %get-tuple-element.28), channel_id=1, source_target_pairs={{2,0},{4,2},{6,4},{3,1},{5,3},{7,5},{10,8},{12,10},{14,12},{11,9},... | collective-permute-start | bytes 2312 | tf_op jit(solution)/shard_map/ppermute | solution.py:24
  43.7 2.7 collective-permute-start.2
  45.0 3.1 collective-permute-start.3
  46.3 34.0 %copy-start.9 = (f32[512]{0:T(512)S(1)}, f32[512]{0:T(512)}, u32[]{:S(2)}) copy-start(f32[512]{0:T(512)} %param.11) | copy-start | bytes 6148
  80.9 5.0 %collective-permute-start.4 = (bf16[2,1,32,512]{3,2,1,0:T(8,128)(2,1)S(1)}, bf16[2,1,32,512]{3,2,1,0:T(8,128)(2,1)S(1)}, u32[]{:S(2)}, u32[]{:S(2)}) collective-permute-start(bf16[2,1,32,512]{3,2,1,0:T(8,128)(2,1)S(1)} %get-tuple-element.15), channel_id=1, source_target_pairs={{0,2},{2,4},{4,6},{1,3},{3,5},{5,7},{8,10},{10,12},{12,14},{9,11},... | collective-permute-start | bytes 196616 | tf_op jit(solution)/shard_map/ppermute | solution.py:22
  82.5 14.2 %collective-permute-start.5 = (bf16[2,1,32,512]{3,2,1,0:T(8,128)(2,1)S(1)}, bf16[2,1,32,512]{3,2,1,0:T(8,128)(2,1)S(1)}, u32[]{:S(2)}, u32[]{:S(2)}) collective-permute-start(bf16[2,1,32,512]{3,2,1,0:T(8,128)(2,1)S(1)} %get-tuple-element.16), channel_id=1, source_target_pairs={{2,0},{4,2},{6,4},{3,1},{5,3},{7,5},{10,8},{12,10},{14,12},{11,9},... | collective-permute-start | bytes 196616 | tf_op jit(solution)/shard_map/ppermute | solution.py:24
  96.8 2.6 collective-permute-start.6
  98.1 3.2 collective-permute-start.7
  128.2 3.8 %copy-start.4 = (bf16[512,3,3,512]{3,0,2,1:T(8,128)(2,1)S(1)}, bf16[512,3,3,512]{3,0,2,1:T(8,128)(2,1)}, u32[]{:S(2)}) copy-start(bf16[512,3,3,512]{3,0,2,1:T(8,128)(2,1)} %all-gather.7.cloned.1.call-done) | copy-start | bytes 14155780
  136.9 33.0 %copy-start.10 = (f32[512]{0:T(512)S(1)}, f32[512]{0:T(512)}, u32[]{:S(2)}) copy-start(f32[512]{0:T(512)} %param.12) | copy-start | bytes 6148
  170.5 5.0 %collective-permute-start.8 = (bf16[2,1,32,512]{3,2,1,0:T(8,128)(2,1)S(1)}, bf16[2,1,32,512]{3,2,1,0:T(8,128)(2,1)S(1)}, u32[]{:S(2)}, u32[]{:S(2)}) collective-permute-start(bf16[2,1,32,512]{3,2,1,0:T(8,128)(2,1)S(1)} %get-tuple-element.13), channel_id=1, source_target_pairs={{0,2},{2,4},{4,6},{1,3},{3,5},{5,7},{8,10},{10,12},{12,14},{9,11},... | collective-permute-start | bytes 196616 | tf_op jit(solution)/shard_map/ppermute | solution.py:22
  171.9 8.4 %collective-permute-start.9 = (bf16[2,1,32,512]{3,2,1,0:T(8,128)(2,1)S(1)}, bf16[2,1,32,512]{3,2,1,0:T(8,128)(2,1)S(1)}, u32[]{:S(2)}, u32[]{:S(2)}) collective-permute-start(bf16[2,1,32,512]{3,2,1,0:T(8,128)(2,1)S(1)} %get-tuple-element.14), channel_id=1, source_target_pairs={{2,0},{4,2},{6,4},{3,1},{5,3},{7,5},{10,8},{12,10},{14,12},{11,9},... | collective-permute-start | bytes 196616 | tf_op jit(solution)/shard_map/ppermute | solution.py:24
  180.4 2.8 collective-permute-start.10
  181.7 3.2 collective-permute-start.11
  281.5 6.2 %copy-start.3 = (bf16[512,4,4,512]{3,0,2,1:T(8,128)(2,1)S(1)}, bf16[512,4,4,512]{3,0,2,1:T(8,128)(2,1)}, u32[]{:S(2)}) copy-start(bf16[512,4,4,512]{3,0,2,1:T(8,128)(2,1)} %all-gather.11.cloned.1.call-done) | copy-start | bytes 25165828
  (3 other events, 5.2 us)
Sparse Core Ops, SparseCore 0:
  8.9 11.9 all-gather.4
  22.4 11.7 all-gather.8
  35.8 92.4 all-gather.6
  129.6 150.0 all-gather.10
where the time goes:
time: 318 us; the launch traced here: 317 us
  waiting for transfers between devices  172 us (54%)
  blocking collectives  60.2 us (19%)
  matrix products  26.5 us (8%)
  starting transfers between devices  18.5 us (6%)
  local copies, waits for them, and re-layouts  18.3 us (6%)
  between operations  13.6 us (4%)
  other arithmetic  7.94 us (2%)
    all_gather x1, waiting for transfers between devices, local(): lax.all_gather(up_slab, 'py', axis=0, tiled=True)  93.1 us
    psum x2, blocking collectives, group_norm(): lax.psum(jnp.sum(centred * centred, axis=(0, 2)), ('py', 'px')) / cell_count  30.4 us
    psum x2, blocking collectives, group_norm(): average = lax.psum(jnp.sum(grouped, axis=(0, 2)), ('py', 'px')) / cell_count  29.8 us
    all_gather x1, waiting for transfers between devices, local(): lax.all_gather(res_slab, 'py', axis=0, tiled=True)  25 us
    ppermute x6, waiting for transfers between devices, with_halo(): lax.ppermute(head, axis, [((i + 1) % count, i) for i in range(ends)])  24.9 us
    dot_general x16, matrix products, upsample_rows(): jnp.einsum('fhwc,cd->fhwd', window, block_rows[:, row_kernel, col_kernel,...  16.6 us
    all_gather x1, waiting for transfers between devices, local(): lax.all_gather(up_weight, 'px', axis=0, tiled=True)  13.2 us
    all_gather x1, waiting for transfers between devices, local(): lax.all_gather(res_weight, 'px', axis=0, tiled=True)  10.7 us
  transfers between devices with their start and end apart: 16, of which 12 were waited for; matrix products, arithmetic and copies ran while one was open for 7% of the time, Pallas kernels for 0%

commit v1 on v0

v1 whole, which is shorter than its diff:
```python
import jax
import jax.numpy as jnp
import numpy as np
from jax import lax
from jax.experimental import pallas as pl
from jax.experimental.pallas import tpu as pltpu
from jax.sharding import PartitionSpec as P

GROUPS = 32

fsq_levels = (8, 8, 8, 5, 5, 5)
epsilon = 1e-06
VMEM_LIMIT = 56 << 20
up_taps = (((1, 1), (3, 0)), ((0, 2), (2, 1)))

COL = 40


def axis_gather(cells, axis, dim):
    count = lax.axis_size(axis)
    me = lax.axis_index(axis)
    step = 1
    while step < count:
        other = lax.ppermute(cells, axis, [(i, i ^ step) for i in range(count)])
        upper = (me & step) != 0
        low = jnp.where(upper, other, cells)
        high = jnp.where(upper, cells, other)
        cells = jnp.concatenate([low, high], axis=dim)
        step *= 2
    return cells


def code_values(fsq_codes):
    levels = jnp.array(fsq_levels, jnp.int32).reshape(-1, 1, 1, 1)
    half_range = levels // 2
    values = (fsq_codes - half_range).astype(jnp.float32) / half_range.astype(jnp.float32)
    return values.astype(jnp.bfloat16)


def lanes_up(count):
    return (count + 127) // 128 * 128


def flat_inputs(values, rows, cols):
    dims, frames, height, width = values.shape
    py = lax.axis_index("py")
    px = lax.axis_index("px")
    clip = jnp.pad(values, ((0, 0), (0, 0), (1, 1), (1, 1)))
    inside = np.zeros((1, frames, height + 2, width + 2), np.float32)
    inside[:, :, :height, :width] = 1.0
    clip = jnp.concatenate([clip, jnp.asarray(inside, jnp.bfloat16), jnp.zeros_like(clip[:1])], axis=0)
    clip = clip.reshape(8, -1)
    clip = jnp.pad(clip, ((0, 0), (0, lanes_up(clip.shape[1]) - clip.shape[1])))

    wide = jnp.pad(values, ((0, 0), (0, 0), (3, 3), (3, 3)))
    patch = lax.dynamic_slice(
        wide, (0, 0, py * rows, px * cols), (dims, frames, rows + 6, cols + 6)
    )
    y = py * rows - 2 + jnp.arange(rows + 6)[:, None]
    x = px * cols - 2 + jnp.arange(cols + 6)[None, :]
    valid = (y >= 0) & (y < height) & (x >= 0) & (x < width)
    valid = jnp.broadcast_to(valid, (1, frames, rows + 6, cols + 6)).astype(jnp.bfloat16)
    patch = jnp.concatenate([patch, valid, jnp.zeros_like(valid)], axis=0)
    patch = jnp.pad(patch, ((0, 0), (0, 0), (0, 0), (0, COL - cols - 6)))
    patch = jnp.transpose(patch, (0, 2, 1, 3)).reshape(8, -1)
    return clip.astype(jnp.float32), patch.astype(jnp.float32)


def group_mean(row):
    lane = lax.broadcasted_iota(jnp.int32, row.shape, 1)
    width = row.shape[1]
    for step in (1, 2, 4, 8):
        row = row + jnp.where(
            (lane & step) != 0, pltpu.roll(row, step, 1), pltpu.roll(row, width - step, 1)
        )
    return row * (1.0 / 16.0)


def silu(t):
    return t * (0.5 * jnp.tanh(0.5 * t) + 0.5)


def tap_rows(flat, stride, keep=None):
    width = flat.shape[1]
    parts = []
    for tap in range(9):
        shift = (tap // 3) * stride + tap % 3
        part = flat if shift == 0 else pltpu.roll(flat, width - shift, 1)
        parts.append(part if keep is None else part * keep)
    parts.append(jnp.zeros_like(flat))
    return [
        jnp.concatenate(parts[2 * i : 2 * i + 2], axis=0).astype(jnp.bfloat16) for i in range(5)
    ]


def prep_kernel(clip_stride, rows, clip_ref, patch_ref, w_ref, gain_ref, act_ref, feat_ref, mark_ref, taps, wide):
    channels = feat_ref.shape[1]
    row_len = 2 * COL
    for i, part in enumerate(tap_rows(clip_ref[...], clip_stride, clip_ref[6:7, :])):
        taps[16 * i : 16 * i + 16, :] = part
    moments = lax.dot_general(
        taps[...], taps[...], (((1,), (1,)), ((), ())), preferred_element_type=jnp.float32
    )
    total = moments[6:7, 6:7]
    mean_row = moments[6:7, :] / total
    mean_col = moments[:, 6:7] / total
    centred = moments / total - mean_col * mean_row
    weight = w_ref[:, :channels]
    weight32 = weight.astype(jnp.float32)
    spread_c = jnp.sum(
        weight32
        * jnp.dot(
            centred, weight32, precision=lax.Precision.HIGHEST, preferred_element_type=jnp.float32
        ),
        axis=0,
        keepdims=True,
    )
    mean_c = jnp.sum(weight32 * mean_col, axis=0, keepdims=True)
    mean_c = jnp.broadcast_to(mean_c, (8, channels))
    spread_c = jnp.broadcast_to(spread_c, (8, channels))
    average = group_mean(mean_c)
    apart = mean_c - average
    spread = jnp.maximum(group_mean(spread_c + apart * apart), 0.0)
    scale = (lax.rsqrt(spread + epsilon) * gain_ref[...])[0:1, :]
    average = average[0:1, :]

    patch = patch_ref[...]
    span = patch.shape[1]
    window = jnp.concatenate(tap_rows(patch, row_len), axis=0)
    block = 256
    for start in range(0, span, block):
        size = min(block, span - start)
        product = lax.dot_general(
            window[:, start : start + size],
            w_ref[...],
            (((0,), (0,)), ((), ())),
            preferred_element_type=jnp.float32,
        )
        keep = product[:, channels : channels + 128]
        feat = product[:, :channels].astype(jnp.bfloat16).astype(jnp.float32)
        active = silu((feat - average) * scale)
        for lane in range(0, channels, 128):
            wide[start : start + size, lane : lane + 128] = active[:, lane : lane + 128] * keep
    mark_ref[...] = jnp.broadcast_to(scale[:, 0:128], mark_ref.shape)
    count = act_ref.shape[0]
    for shift in range(3):
        act_ref[:, shift * channels : (shift + 1) * channels] = wide[
            shift : shift + count, :
        ].astype(jnp.bfloat16)
    moved = pltpu.roll(patch, span - (row_len + 1), 1)
    window = jnp.concatenate(tap_rows(moved, row_len), axis=0)
    inner = feat_ref.shape[0]
    for start in range(0, inner, block):
        size = min(block, inner - start)
        product = lax.dot_general(
            window[:, start : start + block],
            weight,
            (((0,), (0,)), ((), ())),
            preferred_element_type=jnp.float32,
        )
        feat_ref[start : start + size, :] = product[:size].astype(jnp.bfloat16)


def prep(values, in_weight, gain, rows, cols, waits=()):
    channels = in_weight.shape[3]
    dims, frames, height, width = values.shape
    clip, patch = flat_inputs(values, rows, cols)
    span = patch.shape[1]
    pad = lanes_up(span + 2) - span
    patch = jnp.pad(patch, ((0, 0), (0, pad)))
    clip, patch = after((clip, patch), *waits)
    weight = jnp.pad(in_weight.reshape(9, dims, channels), ((0, 1), (0, 8 - dims), (0, 128)))
    marks = np.zeros((10, 8, channels + 128), np.float32)
    marks[0, 6, channels:] = 1.0
    weight = (weight + jnp.asarray(marks, jnp.bfloat16)).reshape(80, channels + 128)
    row_len = frames * COL
    return pl.pallas_call(
        lambda *refs: prep_kernel(width + 2, rows, *refs),
        out_shape=(
            jax.ShapeDtypeStruct(((rows + 4) * row_len, 3 * channels), jnp.bfloat16),
            jax.ShapeDtypeStruct(((rows + 2) * row_len, channels), jnp.bfloat16),
            jax.ShapeDtypeStruct((8, 128), jnp.float32),
        ),
        scratch_shapes=[
            pltpu.VMEM((80, clip.shape[1]), jnp.bfloat16),
            pltpu.VMEM((patch.shape[1], channels), jnp.float32),
        ],
        compiler_params=pltpu.CompilerParams(vmem_limit_bytes=(24 << 20) + 512 * clip.shape[1]),
        name="prep",
    )(clip, patch, weight, gain.reshape(1, channels))


def conv1_kernel(copy_plan, rows, cols, *refs):
    act_hbm, feat_hbm, *sources, hid_ref, stat_ref, weight, act, feat, total, sems, in_sem = refs
    row_len = 2 * COL
    inputs = [
        pltpu.make_async_copy(act_hbm, act, in_sem.at[0]),
        pltpu.make_async_copy(feat_hbm, feat, in_sem.at[1]),
    ]
    copies = [copy_plan(sources, weight, sems, 3 * i, 3) for i in range(3)]
    for copy in inputs + copies[0]:
        copy.start()
    for copy in inputs:
        copy.wait()
    channels = feat.shape[1]
    count = hid_ref.shape[0]
    group = count
    for row_tap in range(3):
        for copy in copies[row_tap]:
            copy.wait()
        if row_tap < 2:
            for copy in copies[row_tap + 1]:
                copy.start()
        taps = weight[3 * row_tap : 3 * row_tap + 3].reshape(3 * channels, channels)
        for start in range(0, count, group):
            size = min(group, count - start)
            first = start + row_tap * row_len
            product = jnp.dot(
                act[first : first + size, :], taps, preferred_element_type=jnp.float32
            )
            if row_tap == 0:
                total[start : start + size, :] = product + feat[start : start + size, :]
            elif row_tap == 1:
                total[start : start + size, :] += product
            else:
                hid_ref[start : start + size, :] = (total[start : start + size, :] + product).astype(
                    jnp.bfloat16
                )

    place = lax.broadcasted_iota(jnp.int32, (row_len, 128), 0)
    place = jnp.where(place >= COL, place - COL, place)
    keep = ((place >= 1) & (place <= cols)).astype(jnp.float32)
    keep = jnp.concatenate([keep] * (channels // 128), axis=1)
    lines = range(row_len, (rows + 1) * row_len, row_len)
    cells = 2.0 * rows * cols
    mean = jnp.zeros((row_len, channels), jnp.float32)
    for line in lines:
        mean = mean + hid_ref[line : line + row_len, :].astype(jnp.float32)
    mean = jnp.sum(mean * keep, axis=0, keepdims=True) / cells
    square = jnp.zeros((row_len, channels), jnp.float32)
    for line in lines:
        apart = hid_ref[line : line + row_len, :].astype(jnp.float32) - mean
        square = square + apart * apart
    stat_ref[0:1, :] = mean
    stat_ref[1:2, :] = jnp.sum(square * keep, axis=0, keepdims=True)
    stat_ref[2:8, :] = jnp.zeros((6, channels), jnp.float32)


def conv2_kernel(copy_plan, rows, cols, edge_ref, hid_ref, stat_ref, gain_ref, *refs):
    *sources, out_ref, weight, wide, shifted, woven, result, sems, out_sem = refs
    row_len = 2 * COL
    channels = hid_ref.shape[1]
    copies = copy_plan(sources, weight, sems, 0, 16)
    for copy in copies:
        copy.start()

    parts = stat_ref.shape[0]
    cells = 2.0 * rows * cols
    means = stat_ref[:, 0, :]
    average_c = jnp.sum(means, axis=0, keepdims=True) / parts
    apart = means - average_c
    square_c = jnp.sum(stat_ref[:, 1, :] + cells * apart * apart, axis=0, keepdims=True)
    average_c = jnp.broadcast_to(average_c, (8, channels))
    spread_c = jnp.broadcast_to(square_c, (8, channels)) / (cells * parts)
    average = group_mean(average_c)
    apart = average_c - average
    spread = group_mean(spread_c + apart * apart)
    scale = (lax.rsqrt(spread + epsilon) * gain_ref[...])[0:1, :]
    average = average[0:1, :]

    place = lax.broadcasted_iota(jnp.int32, (row_len, channels), 0)
    place = jnp.where(place >= COL, place - COL, place)
    top, bottom, left, right = (edge_ref[i].astype(jnp.float32) for i in range(4))
    keep = jnp.where(place == 0, left, jnp.where(place == cols + 1, right, 1.0))

    def normalise(line, _):
        first = pl.multiple_of(line * row_len, row_len)
        t = (hid_ref[pl.ds(first, row_len), :].astype(jnp.float32) - average) * scale
        row_keep = jnp.where(line == 0, top, jnp.where(line == rows + 1, bottom, 1.0))
        wide[...] = silu(t) * (keep * row_keep)
        for shift in range(3):
            for frame in range(2):
                to = pl.multiple_of(line * (2 * cols) + frame * cols, cols)
                shifted[pl.ds(to, cols), shift * channels : (shift + 1) * channels] = wide[
                    frame * COL + shift : frame * COL + shift + cols, :
                ].astype(jnp.bfloat16)
        return 0

    lax.fori_loop(0, rows + 2, normalise, 0)
    for copy in copies:
        copy.wait()

    step = 8
    size = step * 2 * cols

    for part in range(rows // step):
        line = part * step
        for row_phase in range(2):
            for col_phase in range(2):
                acc = None
                for row_kernel, row_offset in up_taps[row_phase]:
                    first = (line + row_offset) * (2 * cols)
                    tap = 4 * row_kernel + 2 * col_phase
                    product = jnp.dot(
                        shifted[
                            pl.ds(first, size), col_phase * channels : (col_phase + 2) * channels
                        ],
                        weight[tap : tap + 2].reshape(2 * channels, channels),
                        preferred_element_type=jnp.float32,
                    )
                    acc = product if acc is None else acc + product
                for lane in range(channels // 128):
                    woven[row_phase, lane, pl.ds(col_phase, size, stride=2), :] = acc[
                        :, 128 * lane : 128 * lane + 128
                    ]
            for y in range(step):
                for frame in range(2):
                    at = (2 * y + frame) * 2 * cols
                    for lane in range(channels // 128):
                        result[
                            frame,
                            2 * (line + y) + row_phase,
                            :,
                            128 * lane : 128 * lane + 128,
                        ] = woven[row_phase, lane, at : at + 2 * cols, :].astype(jnp.bfloat16)
        for frame in range(2):
            lines = pl.ds(2 * line, 2 * step)
            pltpu.make_async_copy(
                result.at[frame, lines], out_ref.at[frame, lines], out_sem.at[part, frame]
            ).start()
    for part in range(rows // step):
        for frame in range(2):
            lines = pl.ds(2 * step * part, 2 * step)
            pltpu.make_async_copy(
                result.at[frame, lines], out_ref.at[frame, lines], out_sem.at[part, frame]
            ).wait()


def xor_pairs(axis, bits):
    return [(i, i ^ bits) for i in range(lax.axis_size(axis))]


def tap_major(weight):
    return jnp.transpose(weight, (1, 2, 0, 3)).reshape(-1, weight.shape[0], weight.shape[3])


def paired_taps(weight):
    rows, _, _, width = weight.shape
    halves = weight.reshape(rows, 4, 2, 2, width)[:, :, ::-1, ::-1, :]
    return jnp.transpose(halves, (1, 3, 2, 0, 4)).reshape(16, rows, width)


def column_part(weight):
    width = weight.shape[2] // lax.axis_size("clip")
    return lax.dynamic_slice_in_dim(weight, lax.axis_index("clip") * width, width, axis=2)


def swap(piece):
    return lax.ppermute(piece, "px", xor_pairs("px", 1))


def whole_gather(weight):
    def plan(sources, weight, sems, first, taps):
        taps = pl.ds(first, taps)
        return [pltpu.make_async_copy(sources[0].at[taps], weight.at[taps], sems.at[first, 0])]

    return [lax.all_gather(weight, ("py", "px"), axis=1, tiled=True)], plan


def after(held, *waits):
    return lax.optimization_barrier((held, waits))[0]


def to_z(part, bits):
    return lax.ppermute(part, "py", xor_pairs("py", bits))


def to_clips(piece):
    return [piece] + [lax.ppermute(piece, "clip", xor_pairs("clip", d)) for d in (1, 2, 3)]


def both_cores(pieces):
    return [one for piece in pieces for one in (piece, swap(piece))]


def placed_plan(placed):
    sources = []
    for entry in placed:
        if not any(entry[0] is source for source in sources):
            sources.append(entry[0])
    slots = [next(i for i, source in enumerate(sources) if source is entry[0]) for entry in placed]

    def plan(refs, weight, sems, first, taps):
        core, z, clip = lax.axis_index("px"), lax.axis_index("py"), lax.axis_index("clip")
        taps = pl.ds(first, taps)
        copies = []
        for i, (slot, (_, lead, z_bits, clip_bits, core_bit)) in enumerate(zip(slots, placed)):
            ref = refs[slot]
            rows, width = ref.shape[-2:]
            row = pl.ds(pl.multiple_of((2 * (z ^ z_bits) + (core ^ core_bit)) * rows, rows), rows)
            if clip_bits is None:
                to = weight.at[taps, row, :]
            elif clip_bits >= 0:
                to = weight.at[
                    taps, row, pl.ds(pl.multiple_of((clip ^ clip_bits) * width, width), width)
                ]
            else:
                to = weight.at[taps, row, pl.ds(-(clip_bits + 1) * width, width)]
            copies.append(
                pltpu.make_async_copy(ref.at[(*lead, taps)], to, sems.at[first, i])
            )
        return copies

    return sources, plan


def code_gather(values):
    if lax.axis_size("py") != 4 or lax.axis_size("px") != 2:
        return axis_gather(axis_gather(values, "px", 3), "py", 2), values
    z, core = lax.axis_index("py"), lax.axis_index("px")
    dense = values.reshape(values.shape[0] * values.shape[1], -1)
    moved = [to_z(dense, j) for j in (1, 2, 3)]
    own, *others = [values] + [piece.reshape(values.shape) for piece in moved]
    low, high = (z & 1) != 0, (z & 2) != 0
    pairs = [
        jnp.concatenate([jnp.where(low, b, a), jnp.where(low, a, b)], axis=2)
        for a, b in ((own, others[0]), (others[1], others[2]))
    ]
    column = jnp.concatenate(
        [jnp.where(high, pairs[1], pairs[0]), jnp.where(high, pairs[0], pairs[1])], axis=2
    )
    other = swap(column.reshape(dense.shape[0], -1)).reshape(column.shape)
    whole = jnp.concatenate(
        [jnp.where(core != 0, other, column), jnp.where(core != 0, column, other)], axis=3
    )
    return whole, moved


def stat_gather(stat):
    if lax.axis_size("py") != 4 or lax.axis_size("px") != 2:
        return axis_gather(axis_gather(stat[None], "px", 0), "py", 0)
    pair = jnp.stack([stat, swap(stat)])
    return jnp.concatenate(
        [pair] + [lax.ppermute(pair, "py", xor_pairs("py", j)) for j in (1, 2, 3)], axis=0
    )


ANY = pl.BlockSpec(memory_space=pl.ANY)
WHOLE = pl.BlockSpec(memory_space=pltpu.VMEM)


def local(fsq_codes, in_weight, res_weight, up_weight, first_gain, second_gain):
    dims, frames, rows, cols = fsq_codes.shape
    channels = in_weight.shape[3]
    row_len = frames * COL
    res_taps, up_taps_own = tap_major(res_weight), paired_taps(up_weight)
    paired = tuple(lax.axis_size(axis) for axis in ("clip", "py", "px")) == (4, 4, 2)
    if paired:
        codes = code_gather(code_values(fsq_codes))
        res_part, up_part = column_part(res_taps), column_part(up_taps_own)
        res = [to_z(res_part, j) for j in (1, 2, 3)]
        res_other, up_other = (swap(after(own, codes[1])) for own in (res_taps, up_taps_own))
        waits = (res_other, up_other)
        act, feat, mark = prep(codes[0], in_weight, first_gain, rows, cols, waits)
        res_spread = to_clips(after(jnp.stack(res), mark))
        up = [to_z(after(up_part, mark, *res), j) for j in (2, 3)]
        up_near = to_z(after(up_taps_own, *res_spread), 1)
        up_spread = to_clips(after(jnp.stack(up), *res_spread))
        placed = [(res_taps, (), 0, None, 0), (res_other, (), 0, None, 1)]
        for d in range(4):
            for core, held in enumerate((res_spread[d], swap(res_spread[d]))):
                placed += [(held, (j - 1,), j, d, core) for j in (1, 2, 3)]
        res_sources, res_plan = placed_plan(placed)
    else:
        act, feat, _ = prep(code_gather(code_values(fsq_codes))[0], in_weight, first_gain, rows, cols)
        res_sources, res_plan = whole_gather(res_taps)
    hidden, stat = pl.pallas_call(
        lambda *refs: conv1_kernel(res_plan, rows, cols, *refs),
        out_shape=(
            jax.ShapeDtypeStruct(feat.shape, jnp.bfloat16),
            jax.ShapeDtypeStruct((8, channels), jnp.float32),
        ),
        in_specs=[ANY, ANY] + [ANY] * len(res_sources),
        scratch_shapes=[
            pltpu.VMEM((9, channels, channels), jnp.bfloat16),
            pltpu.VMEM(act.shape, jnp.bfloat16),
            pltpu.VMEM(feat.shape, jnp.bfloat16),
            pltpu.VMEM(feat.shape, jnp.float32),
            pltpu.SemaphoreType.DMA((9, 32)),
            pltpu.SemaphoreType.DMA((2,)),
        ],
        compiler_params=pltpu.CompilerParams(vmem_limit_bytes=VMEM_LIMIT),
        cost_estimate=pl.CostEstimate(
            flops=2 * 9 * feat.shape[0] * channels * channels, bytes_accessed=12 << 20, transcendentals=0
        ),
        name="conv1",
    )(act, feat, *res_sources)
    if paired:
        stat = after(stat, up_near, *up_spread)
        stats = stat_gather(stat)
        up_near, *up_spread = after((up_near, *up_spread), stat)
        placed = [(up_taps_own, (), 0, None, 0), (up_other, (), 0, None, 1)]
        placed += [(up_near, (), 1, None, 0), (swap(up_near), (), 1, None, 1)]
        for d in range(4):
            for core, held in enumerate((up_spread[d], swap(up_spread[d]))):
                placed += [(held, (j - 2,), j, d, core) for j in (2, 3)]
        up_sources, up_plan = placed_plan(placed)
    else:
        up_sources, up_plan = whole_gather(up_taps_own)
        stats = stat_gather(stat)
    py, px = lax.axis_index("py"), lax.axis_index("px")
    edges = jnp.stack(
        [py > 0, py < lax.axis_size("py") - 1, px > 0, px < lax.axis_size("px") - 1]
    ).astype(jnp.int32)
    step = 8
    return pl.pallas_call(
        lambda *refs: conv2_kernel(up_plan, rows, cols, *refs),
        out_shape=jax.ShapeDtypeStruct((frames, 2 * rows, 2 * cols, channels), jnp.bfloat16),
        in_specs=[pl.BlockSpec(memory_space=pltpu.SMEM), WHOLE, WHOLE, WHOLE]
        + [ANY] * len(up_sources),
        out_specs=ANY,
        scratch_shapes=[
            pltpu.VMEM((16, channels, channels), jnp.bfloat16),
            pltpu.VMEM((row_len, channels), jnp.float32),
            pltpu.VMEM(((rows + 2) * frames * cols, 3 * channels), jnp.bfloat16),
            pltpu.VMEM((2, channels // 128, 2 * step * frames * cols, 128), jnp.float32),
            pltpu.VMEM((frames, 2 * rows, 2 * cols, channels), jnp.bfloat16),
            pltpu.SemaphoreType.DMA((1, 32)),
            pltpu.SemaphoreType.DMA((rows // step, frames)),
        ],
        compiler_params=pltpu.CompilerParams(vmem_limit_bytes=VMEM_LIMIT),
        cost_estimate=pl.CostEstimate(
            flops=2 * 16 * frames * rows * cols * channels * channels,
            bytes_accessed=16 << 20,
            transcendentals=0,
        ),
        name="conv2",
    )(edges, hidden, stats, second_gain.reshape(1, channels), *up_sources)


def solution(mesh):
    placed = (
        P(None, "clip", "py", "px"),
        P(),
        P(("py", "px"), None, None, None),
        P(("py", "px"), None, None, None),
        P(),
        P(),
    )
    return jax.shard_map(
        local, mesh=mesh, in_specs=placed, out_specs=P("clip", "py", "px", None), check_vma=False
    )
```

time: 318 us -> 117 us (0.37)
  waiting for transfers between devices: 172 us -> 34.8 us
  blocking collectives: 60.2 us -> 0 us
  Pallas kernels: 0 us -> 36.6 us
  matrix products: 26.5 us -> 0 us
  between operations: 13.6 us -> 0.71 us
  starting transfers between devices: 18.5 us -> 26.7 us
  local copies, waits for them, and re-layouts: 18.3 us -> 12.6 us
    all_gather x4 -> x0, waiting for transfers between devices: 142 us -> none  [the longest x1 93.1 us: local(): lax.all_gather(up_slab, 'py', axis=0, tiled=True)]
    psum x4 -> x0, blocking collectives: 60.2 us -> none  [the longest x2 30.4 us: group_norm(): lax.psum(jnp.sum(centred * centred, axis=(0, 2)), ('py', 'px')) / cell_count]
    pallas_call x0 -> x3, Pallas kernels: none -> 36.6 us  [the longest x1 15.9 us: local(): pl.pallas_call(lambda *refs: conv2_kernel(up_plan, rows, cols, *refs), ou...]
    dot_general x26 -> x0, matrix products: 26.5 us -> none  [the longest x16 16.6 us: upsample_rows(): jnp.einsum('fhwc,cd->fhwd', window, block_rows[:, row_kernel, col_kernel,...]
    ppermute x12 -> x31, starting transfers between devices: 18.4 us -> 26.7 us  [the longest x9 12.6 us: to_z(): return lax.ppermute(part, 'py', xor_pairs('py', bits))]
    transpose x1 -> x0, local copies, waits for them, and re-layouts: 6.32 us -> none  [local(): jnp.transpose(stacked, (2, 3, 0, 4, 1, 5))]
    ppermute x12 -> x31, waiting for transfers between devices: 29.4 us -> 34.8 us  [the longest x9 16.4 us: to_z(): return lax.ppermute(part, 'py', xor_pairs('py', bits))]
    concatenate x4, other arithmetic: 4.37 us -> 0.41 us  [the longest x1 0.15 us: flat_inputs(): jnp.concatenate([clip, jnp.asarray(inside, jnp.bfloat16), jnp.zeros_like(...]
  transfers between devices with their start and end apart: 16 -> 31, of which waited for: 12 -> 10; matrix products, arithmetic and copies ran while one was open for 7% -> 9% of each run, Pallas kernels for 0% -> 13%
where the time goes in v1:
time: 117 us
  Pallas kernels  36.6 us (31%)
  waiting for transfers between devices  34.8 us (30%)
  starting transfers between devices  26.7 us (23%)
  local copies, waits for them, and re-layouts  12.6 us (11%)
  other arithmetic  5.12 us (4%)
    ppermute x9, waiting for transfers between devices, to_z(): return lax.ppermute(part, 'py', xor_pairs('py', bits))  16.4 us
    pallas_call x1, Pallas kernels, local(): pl.pallas_call(lambda *refs: conv2_kernel(up_plan, rows, cols, *refs), ou...  15.9 us
    pallas_call x1, Pallas kernels, local(): pl.pallas_call(lambda *refs: conv1_kernel(res_plan, rows, cols, *refs), o...  15.6 us
    ppermute x9, starting transfers between devices, to_z(): return lax.ppermute(part, 'py', xor_pairs('py', bits))  12.6 us
    ppermute x6, waiting for transfers between devices, to_clips(): lax.ppermute(piece, 'clip', xor_pairs('clip', d))  11.8 us
    ppermute x6, starting transfers between devices, to_clips(): lax.ppermute(piece, 'clip', xor_pairs('clip', d))  7.04 us
    unnamed x53, local copies, waits for them, and re-layouts  6.9 us
    pallas_call x1, Pallas kernels, prep(): pl.pallas_call(lambda *refs: prep_kernel(width + 2, rows, *refs), out_sha...  5.11 us
  transfers between devices with their start and end apart: 31, of which 10 were waited for; matrix products, arithmetic and copies ran while one was open for 9% of the time, Pallas kernels for 13%

profile of v1, /device:TPU:0, one launch (start us, length us, event | category | flops | bytes accessed | tf_op | source)
XLA Modules:
  0.0 116.6 jit_solution(16553783693490328570)
XLA Ops:
  1.1 4.1 %collective-permute-start.1 = (bf16[12,512]{1,0:T(8,128)(2,1)S(1)}, bf16[12,512]{1,0:T(8,128)(2,1)S(1)}, u32[]{:S(2)}, u32[]{:S(2)}) collective-permute-start(bf16[12,512]{1,0:T(8,128)(2,1)S(1)} %reshape.88), channel_id=1, source_target_pairs={{0,4},{2,6},{4,0},{6,2},{1,5},{3,7},{5,1},{7,3},{8,12},{10,14},{12... | collective-permute-start | bytes 36872 | tf_op jit(solution)/shard_map/ppermute | solution.py:375
  5.2 1.3 %collective-permute-start = (bf16[12,512]{1,0:T(8,128)(2,1)S(1)}, bf16[12,512]{1,0:T(8,128)(2,1)S(1)}, u32[]{:S(2)}, u32[]{:S(2)}) collective-permute-start(bf16[12,512]{1,0:T(8,128)(2,1)S(1)} %reshape.88), channel_id=1, source_target_pairs={{0,6},{2,4},{4,2},{6,0},{1,7},{3,5},{5,3},{7,1},{8,14},{10,12},{12... | collective-permute-start | bytes 36872 | tf_op jit(solution)/shard_map/ppermute | solution.py:375
  7.7 3.0 %collective-permute-start.8 = (bf16[9,64,128]{2,1,0:T(8,128)(2,1)S(1)}, bf16[9,64,128]{2,1,0:T(8,128)(2,1)S(1)}, u32[]{:S(2)}, u32[]{:S(2)}) collective-permute-start(bf16[9,64,128]{2,1,0:T(8,128)(2,1)S(1)} %constant_dynamic-slice_fusion), channel_id=1, source_target_pairs={{0,6},{2,4},{4,2},{6,0},{1,7},{3,5},{5,3},{7,1},{8,14},{10,12},{12... | collective-permute-start | bytes 442376 | tf_op jit(solution)/shard_map/ppermute | solution.py:375
  15.1 2.5 %reshape.94 = bf16[64,4,2,2,512]{4,3,2,1,0:T(2,128)(2,1)S(1)} reshape(bf16[64,4,4,512]{3,2,1,0:T(4,128)(2,1)} %param.12) | data formatting | bytes 2097152 | tf_op jit(solution)/shard_map/reshape | solution.py:349
  20.4 2.9 %collective-permute-done.7 = bf16[9,64,128]{2,1,0:T(8,128)(2,1)S(1)} collective-permute-done((bf16[9,64,128]{2,1,0:T(8,128)(2,1)S(1)}, bf16[9,64,128]{2,1,0:T(8,128)(2,1)S(1)}, u32[]{:S(2)}, u32[]{:S(2)}) %collective-permute-start.7) | collective-permute-done | bytes 147488 | tf_op jit(solution)/shard_map/ppermute | solution.py:375
  23.5 5.1 %prep.1 = (bf16[1600,1536]{1,0:T(8,128)(2,1)S(1)}, bf16[1440,512]{1,0:T(8,128)(2,1)S(1)}, f32[8,128]{1,0:T(8,128)}) custom-call(f32[8,8832]{1,0:T(8,128)S(1)} %pad_convert_fusion.refs_0_, f32[8,1792]{1,0:T(8,128)S(1)} %pad_convert_fusion.1.refs_1_, bf16[80,640]{1,0:T(8,128)(2,1)S(1)} %add_bitcast_fusion.refs_2_, f32[1,512]{1,0:T(1,128)S(1)} %bitcast.32), custom_call_target="tpu_custom_call" | custom-call | tf_op jit(solution)/shard_map/prep/pallas_call | solution.py:177
  28.6 2.2 %copy-done.1 = bf16[1600,1536]{1,0:T(8,128)(2,1)} copy-done((bf16[1600,1536]{1,0:T(8,128)(2,1)}, bf16[1600,1536]{1,0:T(8,128)(2,1)S(1)}, u32[]{:S(2)}) %copy-start.1) | copy-done | bytes 4915224
  31.9 1.5 %collective-permute-start.10 = (bf16[3,9,64,128]{3,2,1,0:T(8,128)(2,1)S(1)}, bf16[3,9,64,128]{3,2,1,0:T(8,128)(2,1)S(1)}, u32[]{:S(2)}, u32[]{:S(2)}) collective-permute-start(bf16[3,9,64,128]{3,2,1,0:T(8,128)(2,1)S(1)} %pad_maximum_fusion.1.refs_4_), channel_id=1, source_target_pairs={{0,8},{8,0},{16,24},{24,16},{1,9},{9,1},{17,25},{25,17},{2,10},{10... | collective-permute-start | bytes 1327112 | tf_op jit(solution)/shard_map/ppermute | solution.py:379
  33.4 1.5 %collective-permute-start.12 = (bf16[3,9,64,128]{3,2,1,0:T(8,128)(2,1)S(1)}, bf16[3,9,64,128]{3,2,1,0:T(8,128)(2,1)S(1)}, u32[]{:S(2)}, u32[]{:S(2)}) collective-permute-start(bf16[3,9,64,128]{3,2,1,0:T(8,128)(2,1)S(1)} %pad_maximum_fusion.1.refs_4_), channel_id=1, source_target_pairs={{0,16},{8,24},{16,0},{24,8},{1,17},{9,25},{17,1},{25,9},{2,18},{10... | collective-permute-start | bytes 1327112 | tf_op jit(solution)/shard_map/ppermute | solution.py:379
  35.5 2.4 %collective-permute-start.18 = (bf16[16,64,128]{2,1,0:T(8,128)(2,1)S(1)}, bf16[16,64,128]{2,1,0:T(8,128)(2,1)S(1)}, u32[]{:S(2)}, u32[]{:S(2)}) collective-permute-start(bf16[16,64,128]{2,1,0:T(8,128)(2,1)S(1)} %constant_dynamic-slice_fusion.1), channel_id=1, source_target_pairs={{0,6},{2,4},{4,2},{6,0},{1,7},{3,5},{5,3},{7,1},{8,14},{10,12},{12... | collective-permute-start | bytes 786440 | tf_op jit(solution)/shard_map/ppermute | solution.py:375
  37.9 8.8 %collective-permute-done.18 = bf16[16,64,128]{2,1,0:T(8,128)(2,1)S(1)} collective-permute-done((bf16[16,64,128]{2,1,0:T(8,128)(2,1)S(1)}, bf16[16,64,128]{2,1,0:T(8,128)(2,1)S(1)}, u32[]{:S(2)}, u32[]{:S(2)}) %collective-permute-start.18) | collective-permute-done | bytes 262176 | tf_op jit(solution)/shard_map/ppermute | solution.py:375
  47.1 6.8 %collective-permute-done.12.refs_8_ = bf16[3,9,64,128]{3,2,1,0:T(8,128)(2,1)S(1)} collective-permute-done((bf16[3,9,64,128]{3,2,1,0:T(8,128)(2,1)S(1)}, bf16[3,9,64,128]{3,2,1,0:T(8,128)(2,1)S(1)}, u32[]{:S(2)}, u32[]{:S(2)}) %collective-permute-start.12) | collective-permute-done | bytes 442400 | tf_op jit(solution)/shard_map/ppermute | solution.py:379
  54.5 4.7 %collective-permute-done.17 = bf16[16,64,128]{2,1,0:T(8,128)(2,1)S(1)} collective-permute-done((bf16[16,64,128]{2,1,0:T(8,128)(2,1)S(1)}, bf16[16,64,128]{2,1,0:T(8,128)(2,1)S(1)}, u32[]{:S(2)}, u32[]{:S(2)}) %collective-permute-start.17) | collective-permute-done | bytes 262176 | tf_op jit(solution)/shard_map/ppermute | solution.py:375
  59.3 1.6 %collective-permute-start.19 = (bf16[2,16,64,128]{3,2,1,0:T(8,128)(2,1)S(1)}, bf16[2,16,64,128]{3,2,1,0:T(8,128)(2,1)S(1)}, u32[]{:S(2)}, u32[]{:S(2)}) collective-permute-start(bf16[2,16,64,128]{3,2,1,0:T(8,128)(2,1)S(1)} %pad_maximum_fusion.refs_8_), channel_id=1, source_target_pairs={{0,8},{8,0},{16,24},{24,16},{1,9},{9,1},{17,25},{25,17},{2,10},{10... | collective-permute-start | bytes 1572872 | tf_op jit(solution)/shard_map/ppermute | solution.py:379
  60.8 1.5 %collective-permute-start.20 = (bf16[2,16,64,128]{3,2,1,0:T(8,128)(2,1)S(1)}, bf16[2,16,64,128]{3,2,1,0:T(8,128)(2,1)S(1)}, u32[]{:S(2)}, u32[]{:S(2)}) collective-permute-start(bf16[2,16,64,128]{3,2,1,0:T(8,128)(2,1)S(1)} %pad_maximum_fusion.refs_8_), channel_id=1, source_target_pairs={{0,16},{8,24},{16,0},{24,8},{1,17},{9,25},{17,1},{25,9},{2,18},{10... | collective-permute-start | bytes 1572872 | tf_op jit(solution)/shard_map/ppermute | solution.py:379
  63.6 15.6 %conv1.1 = (bf16[1440,512]{1,0:T(8,128)(2,1)}, f32[8,512]{1,0:T(8,128)}) custom-call(bf16[1600,1536]{1,0:T(8,128)(2,1)} %copy-done.1, bf16[1440,512]{1,0:T(8,128)(2,1)} %copy-done.2, bf16[9,64,512]{2,1,0:T(8,128)(2,1)} %bitcast.47, bf16[9,64,512]{2,1,0:T(8,128)(2,1)} %collective-permute-done.4.refs_3_, bf16[3,9,64,128]{3,2,1,0:T(8,128)(2,1)} %copy-done.5, ...), custom_call_target="tpu_custom_call" | custom-call | flops 6794772480 | bytes 12582912 | tf_op jit(solution)/shard_map/conv1/pallas_call | solution.py:477
  79.2 5.0 %collective-permute-done.20.refs_12_ = bf16[2,16,64,128]{3,2,1,0:T(8,128)(2,1)S(1)} collective-permute-done((bf16[2,16,64,128]{3,2,1,0:T(8,128)(2,1)S(1)}, bf16[2,16,64,128]{3,2,1,0:T(8,128)(2,1)S(1)}, u32[]{:S(2)}, u32[]{:S(2)}) %collective-permute-start.20) | collective-permute-done | bytes 524320 | tf_op jit(solution)/shard_map/ppermute | solution.py:379
  86.4 1.3 %collective-permute-done.22 = f32[8,512]{1,0:T(8,128)S(1)} collective-permute-done((f32[8,512]{1,0:T(8,128)}, f32[8,512]{1,0:T(8,128)S(1)}, u32[]{:S(2)}, u32[]{:S(2)}) %collective-permute-start.22) | collective-permute-done | bytes 16416 | tf_op jit(solution)/shard_map/ppermute | solution.py:359
  88.4 1.8 %collective-permute-start.23 = (f32[2,8,512]{2,1,0:T(8,128)S(1)}, f32[2,8,512]{2,1,0:T(8,128)S(1)}, u32[]{:S(2)}, u32[]{:S(2)}) collective-permute-start(f32[2,8,512]{2,1,0:T(8,128)S(1)} %pad_maximum_fusion.5), channel_id=1, source_target_pairs={{0,2},{2,0},{4,6},{6,4},{1,3},{3,1},{5,7},{7,5},{8,10},{10,8},{12,... | collective-permute-start | bytes 98312 | tf_op jit(solution)/shard_map/ppermute | solution.py:444
  91.5 1.3 %collective-permute-start.25 = (f32[2,8,512]{2,1,0:T(8,128)S(1)}, f32[2,8,512]{2,1,0:T(8,128)S(1)}, u32[]{:S(2)}, u32[]{:S(2)}) collective-permute-start(f32[2,8,512]{2,1,0:T(8,128)S(1)} %pad_maximum_fusion.5), channel_id=1, source_target_pairs={{0,6},{2,4},{4,2},{6,0},{1,7},{3,5},{5,3},{7,1},{8,14},{10,12},{12... | collective-permute-start | bytes 98312 | tf_op jit(solution)/shard_map/ppermute | solution.py:444
  94.1 1.6 %collective-permute-done.24 = f32[2,8,512]{2,1,0:T(8,128)S(1)} collective-permute-done((f32[2,8,512]{2,1,0:T(8,128)S(1)}, f32[2,8,512]{2,1,0:T(8,128)S(1)}, u32[]{:S(2)}, u32[]{:S(2)}) %collective-permute-start.24) | collective-permute-done | bytes 32800 | tf_op jit(solution)/shard_map/ppermute | solution.py:444
  95.6 1.6 %collective-permute-done.25 = f32[2,8,512]{2,1,0:T(8,128)S(1)} collective-permute-done((f32[2,8,512]{2,1,0:T(8,128)S(1)}, f32[2,8,512]{2,1,0:T(8,128)S(1)}, u32[]{:S(2)}, u32[]{:S(2)}) %collective-permute-start.25) | collective-permute-done | bytes 32800 | tf_op jit(solution)/shard_map/ppermute | solution.py:444
  97.8 1.6 %collective-permute-done.30.refs_15_ = bf16[2,16,64,128]{3,2,1,0:T(8,128)(2,1)S(1)} collective-permute-done((bf16[2,16,64,128]{3,2,1,0:T(8,128)(2,1)}, bf16[2,16,64,128]{3,2,1,0:T(8,128)(2,1)S(1)}, u32[]{:S(2)}, u32[]{:S(2)}) %collective-permute-start.30) | collective-permute-done | bytes 524320 | tf_op jit(solution)/shard_map/ppermute | solution.py:359
  100.5 15.9 %conv2.1 = bf16[2,32,64,512]{3,2,1,0:T(8,128)(2,1)} custom-call(s32[4]{0:T(128)} %add_convert_fusion.1.refs_0_, bf16[1440,512]{1,0:T(8,128)(2,1)} %get-tuple-element.32.refs_1_, f32[8,8,512]{2,1,0:T(8,128)} %copy-done.7, f32[1,512]{1,0:T(1,128)} %bitcast.48, bf16[16,64,512]{2,1,0:T(8,128)(2,1)} %bitcast.36, ...), custom_call_target="tpu_custom_call" | custom-call | flops 8589934592 | bytes 16777216 | tf_op jit(solution)/shard_map/conv2/pallas_call | solution.py:516
  (133 shorter events, 20.2 us)
Async XLA Ops:
  1.1 10.9 %collective-permute-start.1 = (bf16[12,512]{1,0:T(8,128)(2,1)S(1)}, bf16[12,512]{1,0:T(8,128)(2,1)S(1)}, u32[]{:S(2)}, u32[]{:S(2)}) collective-permute-start(bf16[12,512]{1,0:T(8,128)(2,1)S(1)} %reshape.88), channel_id=1, source_target_pairs={{0,4},{2,6},{4,0},{6,2},{1,5},{3,7},{5,1},{7,3},{8,12},{10,14},{12... | collective-permute-start | bytes 36872 | tf_op jit(solution)/shard_map/ppermute | solution.py:375
  5.2 8.0 %collective-permute-start = (bf16[12,512]{1,0:T(8,128)(2,1)S(1)}, bf16[12,512]{1,0:T(8,128)(2,1)S(1)}, u32[]{:S(2)}, u32[]{:S(2)}) collective-permute-start(bf16[12,512]{1,0:T(8,128)(2,1)S(1)} %reshape.88), channel_id=1, source_target_pairs={{0,6},{2,4},{4,2},{6,0},{1,7},{3,5},{5,3},{7,1},{8,14},{10,12},{12... | collective-permute-start | bytes 36872 | tf_op jit(solution)/shard_map/ppermute | solution.py:375
  6.6 6.9 %collective-permute-start.2 = (bf16[12,512]{1,0:T(8,128)(2,1)S(1)}, bf16[12,512]{1,0:T(8,128)(2,1)S(1)}, u32[]{:S(2)}, u32[]{:S(2)}) collective-permute-start(bf16[12,512]{1,0:T(8,128)(2,1)S(1)} %reshape.88), channel_id=1, source_target_pairs={{0,2},{2,0},{4,6},{6,4},{1,3},{3,1},{5,7},{7,5},{8,10},{10,8},{12,... | collective-permute-start | bytes 36872 | tf_op jit(solution)/shard_map/ppermute | solution.py:375
  7.7 12.7 %collective-permute-start.8 = (bf16[9,64,128]{2,1,0:T(8,128)(2,1)S(1)}, bf16[9,64,128]{2,1,0:T(8,128)(2,1)S(1)}, u32[]{:S(2)}, u32[]{:S(2)}) collective-permute-start(bf16[9,64,128]{2,1,0:T(8,128)(2,1)S(1)} %constant_dynamic-slice_fusion), channel_id=1, source_target_pairs={{0,6},{2,4},{4,2},{6,0},{1,7},{3,5},{5,3},{7,1},{8,14},{10,12},{12... | collective-permute-start | bytes 442376 | tf_op jit(solution)/shard_map/ppermute | solution.py:375
  10.7 12.7 %collective-permute-start.7 = (bf16[9,64,128]{2,1,0:T(8,128)(2,1)S(1)}, bf16[9,64,128]{2,1,0:T(8,128)(2,1)S(1)}, u32[]{:S(2)}, u32[]{:S(2)}) collective-permute-start(bf16[9,64,128]{2,1,0:T(8,128)(2,1)S(1)} %constant_dynamic-slice_fusion), channel_id=1, source_target_pairs={{0,4},{2,6},{4,0},{6,2},{1,5},{3,7},{5,1},{7,3},{8,12},{10,14},{12... | collective-permute-start | bytes 442376 | tf_op jit(solution)/shard_map/ppermute | solution.py:375
  12.0 11.4 %collective-permute-start.6 = (bf16[9,64,128]{2,1,0:T(8,128)(2,1)S(1)}, bf16[9,64,128]{2,1,0:T(8,128)(2,1)S(1)}, u32[]{:S(2)}, u32[]{:S(2)}) collective-permute-start(bf16[9,64,128]{2,1,0:T(8,128)(2,1)S(1)} %constant_dynamic-slice_fusion), channel_id=1, source_target_pairs={{0,2},{2,0},{4,6},{6,4},{1,3},{3,1},{5,7},{7,5},{8,10},{10,8},{12,... | collective-permute-start | bytes 442376 | tf_op jit(solution)/shard_map/ppermute | solution.py:375
  18.4 5.0 %collective-permute-start.4 = (bf16[9,64,512]{2,1,0:T(8,128)(2,1)}, bf16[9,64,512]{2,1,0:T(8,128)(2,1)}, u32[]{:S(2)}, u32[]{:S(2)}) collective-permute-start(bf16[9,64,512]{2,1,0:T(8,128)(2,1)} %bitcast.46), channel_id=1, source_target_pairs={{0,1},{1,0},{2,3},{3,2},{4,5},{5,4},{6,7},{7,6},{8,9},{9,8},{10,11... | collective-permute-start | bytes 1769480 | tf_op jit(solution)/shard_map/ppermute | solution.py:359
  31.9 14.7 %collective-permute-start.10 = (bf16[3,9,64,128]{3,2,1,0:T(8,128)(2,1)S(1)}, bf16[3,9,64,128]{3,2,1,0:T(8,128)(2,1)S(1)}, u32[]{:S(2)}, u32[]{:S(2)}) collective-permute-start(bf16[3,9,64,128]{3,2,1,0:T(8,128)(2,1)S(1)} %pad_maximum_fusion.1.refs_4_), channel_id=1, source_target_pairs={{0,8},{8,0},{16,24},{24,16},{1,9},{9,1},{17,25},{25,17},{2,10},{10... | collective-permute-start | bytes 1327112 | tf_op jit(solution)/shard_map/ppermute | solution.py:379
  33.4 20.5 %collective-permute-start.12 = (bf16[3,9,64,128]{3,2,1,0:T(8,128)(2,1)S(1)}, bf16[3,9,64,128]{3,2,1,0:T(8,128)(2,1)S(1)}, u32[]{:S(2)}, u32[]{:S(2)}) collective-permute-start(bf16[3,9,64,128]{3,2,1,0:T(8,128)(2,1)S(1)} %pad_maximum_fusion.1.refs_4_), channel_id=1, source_target_pairs={{0,16},{8,24},{16,0},{24,8},{1,17},{9,25},{17,1},{25,9},{2,18},{10... | collective-permute-start | bytes 1327112 | tf_op jit(solution)/shard_map/ppermute | solution.py:379
  34.9 19.0 %collective-permute-start.14 = (bf16[3,9,64,128]{3,2,1,0:T(8,128)(2,1)S(1)}, bf16[3,9,64,128]{3,2,1,0:T(8,128)(2,1)S(1)}, u32[]{:S(2)}, u32[]{:S(2)}) collective-permute-start(bf16[3,9,64,128]{3,2,1,0:T(8,128)(2,1)S(1)} %pad_maximum_fusion.1.refs_4_), channel_id=1, source_target_pairs={{0,24},{8,16},{16,8},{24,0},{1,25},{9,17},{17,9},{25,1},{2,26},{10... | collective-permute-start | bytes 1327112 | tf_op jit(solution)/shard_map/ppermute | solution.py:379
  35.5 11.2 %collective-permute-start.18 = (bf16[16,64,128]{2,1,0:T(8,128)(2,1)S(1)}, bf16[16,64,128]{2,1,0:T(8,128)(2,1)S(1)}, u32[]{:S(2)}, u32[]{:S(2)}) collective-permute-start(bf16[16,64,128]{2,1,0:T(8,128)(2,1)S(1)} %constant_dynamic-slice_fusion.1), channel_id=1, source_target_pairs={{0,6},{2,4},{4,2},{6,0},{1,7},{3,5},{5,3},{7,1},{8,14},{10,12},{12... | collective-permute-start | bytes 786440 | tf_op jit(solution)/shard_map/ppermute | solution.py:375
  37.9 21.3 %collective-permute-start.17 = (bf16[16,64,128]{2,1,0:T(8,128)(2,1)S(1)}, bf16[16,64,128]{2,1,0:T(8,128)(2,1)S(1)}, u32[]{:S(2)}, u32[]{:S(2)}) collective-permute-start(bf16[16,64,128]{2,1,0:T(8,128)(2,1)S(1)} %constant_dynamic-slice_fusion.1), channel_id=1, source_target_pairs={{0,4},{2,6},{4,0},{6,2},{1,5},{3,7},{5,1},{7,3},{8,12},{10,14},{12... | collective-permute-start | bytes 786440 | tf_op jit(solution)/shard_map/ppermute | solution.py:375
  46.6 12.6 %collective-permute-start.9 = (bf16[3,9,64,128]{3,2,1,0:T(8,128)(2,1)S(1)}, bf16[3,9,64,128]{3,2,1,0:T(8,128)(2,1)S(1)}, u32[]{:S(2)}, u32[]{:S(2)}) collective-permute-start(bf16[3,9,64,128]{3,2,1,0:T(8,128)(2,1)S(1)} %pad_maximum_fusion.1.refs_4_), channel_id=1, source_target_pairs={{0,1},{1,0},{2,3},{3,2},{4,5},{5,4},{6,7},{7,6},{8,9},{9,8},{10,11... | collective-permute-start | bytes 1327112 | tf_op jit(solution)/shard_map/ppermute | solution.py:359
  46.6 14.2 %collective-permute-start.11 = (bf16[3,9,64,128]{3,2,1,0:T(8,128)(2,1)S(1)}, bf16[3,9,64,128]{3,2,1,0:T(8,128)(2,1)S(1)}, u32[]{:S(2)}, u32[]{:S(2)}) collective-permute-start(bf16[3,9,64,128]{3,2,1,0:T(8,128)(2,1)S(1)} %collective-permute-done.10.refs_6_), channel_id=1, source_target_pairs={{0,1},{1,0},{2,3},{3,2},{4,5},{5,4},{6,7},{7,6},{8,9},{9,8},{10,11... | collective-permute-start | bytes 1327112 | tf_op jit(solution)/shard_map/ppermute | solution.py:359
  53.9 8.4 %collective-permute-start.13 = (bf16[3,9,64,128]{3,2,1,0:T(8,128)(2,1)S(1)}, bf16[3,9,64,128]{3,2,1,0:T(8,128)(2,1)S(1)}, u32[]{:S(2)}, u32[]{:S(2)}) collective-permute-start(bf16[3,9,64,128]{3,2,1,0:T(8,128)(2,1)S(1)} %collective-permute-done.12.refs_8_), channel_id=1, source_target_pairs={{0,1},{1,0},{2,3},{3,2},{4,5},{5,4},{6,7},{7,6},{8,9},{9,8},{10,11... | collective-permute-start | bytes 1327112 | tf_op jit(solution)/shard_map/ppermute | solution.py:359
  54.0 8.9 %collective-permute-start.15 = (bf16[3,9,64,128]{3,2,1,0:T(8,128)(2,1)S(1)}, bf16[3,9,64,128]{3,2,1,0:T(8,128)(2,1)S(1)}, u32[]{:S(2)}, u32[]{:S(2)}) collective-permute-start(bf16[3,9,64,128]{3,2,1,0:T(8,128)(2,1)S(1)} %collective-permute-done.14.refs_10_), channel_id=1, source_target_pairs={{0,1},{1,0},{2,3},{3,2},{4,5},{5,4},{6,7},{7,6},{8,9},{9,8},{10,11... | collective-permute-start | bytes 1327112 | tf_op jit(solution)/shard_map/ppermute | solution.py:359
  59.2 25.0 %collective-permute-start.16 = (bf16[16,64,512]{2,1,0:T(8,128)(2,1)S(1)}, bf16[16,64,512]{2,1,0:T(8,128)(2,1)S(1)}, u32[]{:S(2)}, u32[]{:S(2)}) collective-permute-start(bf16[16,64,512]{2,1,0:T(8,128)(2,1)S(1)} %bitcast.35), channel_id=1, source_target_pairs={{0,2},{2,0},{4,6},{6,4},{1,3},{3,1},{5,7},{7,5},{8,10},{10,8},{12,... | collective-permute-start | bytes 3145736 | tf_op jit(solution)/shard_map/ppermute | solution.py:375
  59.3 19.9 %collective-permute-start.19 = (bf16[2,16,64,128]{3,2,1,0:T(8,128)(2,1)S(1)}, bf16[2,16,64,128]{3,2,1,0:T(8,128)(2,1)S(1)}, u32[]{:S(2)}, u32[]{:S(2)}) collective-permute-start(bf16[2,16,64,128]{3,2,1,0:T(8,128)(2,1)S(1)} %pad_maximum_fusion.refs_8_), channel_id=1, source_target_pairs={{0,8},{8,0},{16,24},{24,16},{1,9},{9,1},{17,25},{25,17},{2,10},{10... | collective-permute-start | bytes 1572872 | tf_op jit(solution)/shard_map/ppermute | solution.py:379
  60.8 23.4 %collective-permute-start.20 = (bf16[2,16,64,128]{3,2,1,0:T(8,128)(2,1)S(1)}, bf16[2,16,64,128]{3,2,1,0:T(8,128)(2,1)S(1)}, u32[]{:S(2)}, u32[]{:S(2)}) collective-permute-start(bf16[2,16,64,128]{3,2,1,0:T(8,128)(2,1)S(1)} %pad_maximum_fusion.refs_8_), channel_id=1, source_target_pairs={{0,16},{8,24},{16,0},{24,8},{1,17},{9,25},{17,1},{25,9},{2,18},{10... | collective-permute-start | bytes 1572872 | tf_op jit(solution)/shard_map/ppermute | solution.py:379
  62.3 21.9 %collective-permute-start.21 = (bf16[2,16,64,128]{3,2,1,0:T(8,128)(2,1)S(1)}, bf16[2,16,64,128]{3,2,1,0:T(8,128)(2,1)S(1)}, u32[]{:S(2)}, u32[]{:S(2)}) collective-permute-start(bf16[2,16,64,128]{3,2,1,0:T(8,128)(2,1)S(1)} %pad_maximum_fusion.refs_8_), channel_id=1, source_target_pairs={{0,24},{8,16},{16,8},{24,0},{1,25},{9,17},{17,9},{25,1},{2,26},{10... | collective-permute-start | bytes 1572872 | tf_op jit(solution)/shard_map/ppermute | solution.py:379
  85.2 14.1 %collective-permute-start.26 = (bf16[16,64,512]{2,1,0:T(8,128)(2,1)S(1)}, bf16[16,64,512]{2,1,0:T(8,128)(2,1)S(1)}, u32[]{:S(2)}, u32[]{:S(2)}) collective-permute-start(bf16[16,64,512]{2,1,0:T(8,128)(2,1)S(1)} %collective-permute-done.16.refs_6_), channel_id=1, source_target_pairs={{0,1},{1,0},{2,3},{3,2},{4,5},{5,4},{6,7},{7,6},{8,9},{9,8},{10,11... | collective-permute-start | bytes 3145736 | tf_op jit(solution)/shard_map/ppermute | solution.py:359
  88.4 5.1 %collective-permute-start.23 = (f32[2,8,512]{2,1,0:T(8,128)S(1)}, f32[2,8,512]{2,1,0:T(8,128)S(1)}, u32[]{:S(2)}, u32[]{:S(2)}) collective-permute-start(f32[2,8,512]{2,1,0:T(8,128)S(1)} %pad_maximum_fusion.5), channel_id=1, source_target_pairs={{0,2},{2,0},{4,6},{6,4},{1,3},{3,1},{5,7},{7,5},{8,10},{10,8},{12,... | collective-permute-start | bytes 98312 | tf_op jit(solution)/shard_map/ppermute | solution.py:444
  90.2 5.4 %collective-permute-start.24 = (f32[2,8,512]{2,1,0:T(8,128)S(1)}, f32[2,8,512]{2,1,0:T(8,128)S(1)}, u32[]{:S(2)}, u32[]{:S(2)}) collective-permute-start(f32[2,8,512]{2,1,0:T(8,128)S(1)} %pad_maximum_fusion.5), channel_id=1, source_target_pairs={{0,4},{2,6},{4,0},{6,2},{1,5},{3,7},{5,1},{7,3},{8,12},{10,14},{12... | collective-permute-start | bytes 98312 | tf_op jit(solution)/shard_map/ppermute | solution.py:444
  91.5 5.7 %collective-permute-start.25 = (f32[2,8,512]{2,1,0:T(8,128)S(1)}, f32[2,8,512]{2,1,0:T(8,128)S(1)}, u32[]{:S(2)}, u32[]{:S(2)}) collective-permute-start(f32[2,8,512]{2,1,0:T(8,128)S(1)} %pad_maximum_fusion.5), channel_id=1, source_target_pairs={{0,6},{2,4},{4,2},{6,0},{1,7},{3,5},{5,3},{7,1},{8,14},{10,12},{12... | collective-permute-start | bytes 98312 | tf_op jit(solution)/shard_map/ppermute | solution.py:444
  (31 other events, 258.5 us)

commit v2 on v1

--- a/solution.py
+++ b/solution.py
@@ -93,9 +93,8 @@
     ]
 
 
-def prep_kernel(clip_stride, rows, clip_ref, patch_ref, w_ref, gain_ref, act_ref, feat_ref, mark_ref, taps, wide):
-    channels = feat_ref.shape[1]
-    row_len = 2 * COL
+def prep_kernel(clip_stride, clip_ref, w_ref, gain_ref, norm_ref, taps):
+    channels = gain_ref.shape[1]
     for i, part in enumerate(tap_rows(clip_ref[...], clip_stride, clip_ref[6:7, :])):
         taps[16 * i : 16 * i + 16, :] = part
     moments = lax.dot_general(
@@ -105,8 +104,7 @@
     mean_row = moments[6:7, :] / total
     mean_col = moments[:, 6:7] / total
     centred = moments / total - mean_col * mean_row
-    weight = w_ref[:, :channels]
-    weight32 = weight.astype(jnp.float32)
+    weight32 = w_ref[:, :channels].astype(jnp.float32)
     spread_c = jnp.sum(
         weight32
         * jnp.dot(
@@ -121,10 +119,16 @@
     average = group_mean(mean_c)
     apart = mean_c - average
     spread = jnp.maximum(group_mean(spread_c + apart * apart), 0.0)
-    scale = (lax.rsqrt(spread + epsilon) * gain_ref[...])[0:1, :]
-    average = average[0:1, :]
-
-    patch = patch_ref[...]
+    norm_ref[0:8, :] = average
+    norm_ref[8:16, :] = lax.rsqrt(spread + epsilon) * gain_ref[...]
+
+
+def features(patch, w_ref, norm_ref, wide, act, feat):
+    channels = feat.shape[1]
+    row_len = 2 * COL
+    weight = w_ref[:, :channels]
+    average = norm_ref[0:1, :]
+    scale = norm_ref[8:9, :]
     span = patch.shape[1]
     window = jnp.concatenate(tap_rows(patch, row_len), axis=0)
     block = 256
@@ -137,19 +141,18 @@
             preferred_element_type=jnp.float32,
         )
         keep = product[:, channels : channels + 128]
-        feat = product[:, :channels].astype(jnp.bfloat16).astype(jnp.float32)
-        active = silu((feat - average) * scale)
+        rounded = product[:, :channels].astype(jnp.bfloat16).astype(jnp.float32)
+        active = silu((rounded - average) * scale)
         for lane in range(0, channels, 128):
             wide[start : start + size, lane : lane + 128] = active[:, lane : lane + 128] * keep
-    mark_ref[...] = jnp.broadcast_to(scale[:, 0:128], mark_ref.shape)
-    count = act_ref.shape[0]
+    count = act.shape[0]
     for shift in range(3):
-        act_ref[:, shift * channels : (shift + 1) * channels] = wide[
-            shift : shift + count, :
-        ].astype(jnp.bfloat16)
+        act[:, shift * channels : (shift + 1) * channels] = wide[shift : shift + count, :].astype(
+            jnp.bfloat16
+        )
     moved = pltpu.roll(patch, span - (row_len + 1), 1)
     window = jnp.concatenate(tap_rows(moved, row_len), axis=0)
-    inner = feat_ref.shape[0]
+    inner = feat.shape[0]
     for start in range(0, inner, block):
         size = min(block, inner - start)
         product = lax.dot_general(
@@ -158,7 +161,7 @@
             (((0,), (0,)), ((), ())),
             preferred_element_type=jnp.float32,
         )
-        feat_ref[start : start + size, :] = product[:size].astype(jnp.bfloat16)
+        feat[start : start + size, :] = product[:size].astype(jnp.bfloat16)
 
 
 def prep(values, in_weight, gain, rows, cols, waits=()):
@@ -173,44 +176,29 @@
     marks = np.zeros((10, 8, channels + 128), np.float32)
     marks[0, 6, channels:] = 1.0
     weight = (weight + jnp.asarray(marks, jnp.bfloat16)).reshape(80, channels + 128)
-    row_len = frames * COL
-    return pl.pallas_call(
-        lambda *refs: prep_kernel(width + 2, rows, *refs),
-        out_shape=(
-            jax.ShapeDtypeStruct(((rows + 4) * row_len, 3 * channels), jnp.bfloat16),
-            jax.ShapeDtypeStruct(((rows + 2) * row_len, channels), jnp.bfloat16),
-            jax.ShapeDtypeStruct((8, 128), jnp.float32),
-        ),
-        scratch_shapes=[
-            pltpu.VMEM((80, clip.shape[1]), jnp.bfloat16),
-            pltpu.VMEM((patch.shape[1], channels), jnp.float32),
-        ],
-        compiler_params=pltpu.CompilerParams(vmem_limit_bytes=(24 << 20) + 512 * clip.shape[1]),
+    norm = pl.pallas_call(
+        lambda *refs: prep_kernel(width + 2, *refs),
+        out_shape=jax.ShapeDtypeStruct((16, channels), jnp.float32),
+        scratch_shapes=[pltpu.VMEM((80, clip.shape[1]), jnp.bfloat16)],
+        compiler_params=pltpu.CompilerParams(vmem_limit_bytes=(16 << 20) + 512 * clip.shape[1]),
         name="prep",
-    )(clip, patch, weight, gain.reshape(1, channels))
+    )(clip, weight, gain.reshape(1, channels))
+    return patch, weight, norm
 
 
 def conv1_kernel(copy_plan, rows, cols, *refs):
-    act_hbm, feat_hbm, *sources, hid_ref, stat_ref, weight, act, feat, total, sems, in_sem = refs
+    patch_ref, w_ref, norm_ref, *sources, hid_ref, stat_ref, weight, wide, act, feat, total, sems = refs
     row_len = 2 * COL
-    inputs = [
-        pltpu.make_async_copy(act_hbm, act, in_sem.at[0]),
-        pltpu.make_async_copy(feat_hbm, feat, in_sem.at[1]),
-    ]
     copies = [copy_plan(sources, weight, sems, 3 * i, 3) for i in range(3)]
-    for copy in inputs + copies[0]:
+    for copy in copies[0] + copies[1] + copies[2]:
         copy.start()
-    for copy in inputs:
-        copy.wait()
+    features(patch_ref[...], w_ref, norm_ref, wide, act, feat)
     channels = feat.shape[1]
     count = hid_ref.shape[0]
     group = count
     for row_tap in range(3):
         for copy in copies[row_tap]:
             copy.wait()
-        if row_tap < 2:
-            for copy in copies[row_tap + 1]:
-                copy.start()
         taps = weight[3 * row_tap : 3 * row_tap + 3].reshape(3 * channels, channels)
         for start in range(0, count, group):
             size = min(group, count - start)
@@ -436,10 +424,10 @@
     return whole, moved
 
 
-def stat_gather(stat):
+def stat_gather(stat, other=None):
     if lax.axis_size("py") != 4 or lax.axis_size("px") != 2:
         return axis_gather(axis_gather(stat[None], "px", 0), "py", 0)
-    pair = jnp.stack([stat, swap(stat)])
+    pair = jnp.stack([stat, other])
     return jnp.concatenate(
         [pair] + [lax.ppermute(pair, "py", xor_pairs("py", j)) for j in (1, 2, 3)], axis=0
     )
@@ -461,9 +449,10 @@
         res = [to_z(res_part, j) for j in (1, 2, 3)]
         res_other, up_other = (swap(after(own, codes[1])) for own in (res_taps, up_taps_own))
         waits = (res_other, up_other)
-        act, feat, mark = prep(codes[0], in_weight, first_gain, rows, cols, waits)
-        res_spread = to_clips(after(jnp.stack(res), mark))
-        up = [to_z(after(up_part, mark, *res), j) for j in (2, 3)]
+        patch, in_taps, norm = prep(codes[0], in_weight, first_gain, rows, cols, waits)
+        res_spread = to_clips(after(jnp.stack(res), norm))
+        up = [to_z(after(up_part, norm, *res), 2)]
+        up.append(to_z(up[0], 1))
         up_near = to_z(after(up_taps_own, *res_spread), 1)
         up_spread = to_clips(after(jnp.stack(up), *res_spread))
         placed = [(res_taps, (), 0, None, 0), (res_other, (), 0, None, 1)]
@@ -472,33 +461,34 @@
                 placed += [(held, (j - 1,), j, d, core) for j in (1, 2, 3)]
         res_sources, res_plan = placed_plan(placed)
     else:
-        act, feat, _ = prep(code_gather(code_values(fsq_codes))[0], in_weight, first_gain, rows, cols)
+        patch, in_taps, norm = prep(code_gather(code_values(fsq_codes))[0], in_weight, first_gain, rows, cols)
         res_sources, res_plan = whole_gather(res_taps)
+    cells = (rows + 2) * row_len
     hidden, stat = pl.pallas_call(
         lambda *refs: conv1_kernel(res_plan, rows, cols, *refs),
         out_shape=(
-            jax.ShapeDtypeStruct(feat.shape, jnp.bfloat16),
+            jax.ShapeDtypeStruct((cells, channels), jnp.bfloat16),
             jax.ShapeDtypeStruct((8, channels), jnp.float32),
         ),
-        in_specs=[ANY, ANY] + [ANY] * len(res_sources),
+        in_specs=[WHOLE, WHOLE, WHOLE] + [ANY] * len(res_sources),
         scratch_shapes=[
             pltpu.VMEM((9, channels, channels), jnp.bfloat16),
-            pltpu.VMEM(act.shape, jnp.bfloat16),
-            pltpu.VMEM(feat.shape, jnp.bfloat16),
-            pltpu.VMEM(feat.shape, jnp.float32),
+            pltpu.VMEM((patch.shape[1], channels), jnp.float32),
+            pltpu.VMEM((cells + 2 * row_len, 3 * channels), jnp.bfloat16),
+            pltpu.VMEM((cells, channels), jnp.bfloat16),
+            pltpu.VMEM((cells, channels), jnp.float32),
             pltpu.SemaphoreType.DMA((9, 32)),
-            pltpu.SemaphoreType.DMA((2,)),
         ],
         compiler_params=pltpu.CompilerParams(vmem_limit_bytes=VMEM_LIMIT),
         cost_estimate=pl.CostEstimate(
-            flops=2 * 9 * feat.shape[0] * channels * channels, bytes_accessed=12 << 20, transcendentals=0
+            flops=2 * 9 * cells * channels * channels, bytes_accessed=12 << 20, transcendentals=0
         ),
         name="conv1",
-    )(act, feat, *res_sources)
+    )(patch, in_taps, norm, *res_sources)
     if paired:
-        stat = after(stat, up_near, *up_spread)
-        stats = stat_gather(stat)
-        up_near, *up_spread = after((up_near, *up_spread), stat)
+        other = swap(stat)
+        up_near, *up_spread = after((up_near, *up_spread), other)
+        stats = stat_gather(stat, after(other, up_near, *up_spread))
         placed = [(up_taps_own, (), 0, None, 0), (up_other, (), 0, None, 1)]
         placed += [(up_near, (), 1, None, 0), (swap(up_near), (), 1, None, 1)]
         for d in range(4):

time: 117 us -> 107 us (0.915)
  waiting for transfers between devices: 34.8 us -> 28.6 us
  Pallas kernels: 36.6 us -> 33.6 us
  local copies, waits for them, and re-layouts: 12.6 us -> 10 us
  starting transfers between devices: 26.7 us -> 28.3 us
    ppermute x9, waiting for transfers between devices: 16.4 us -> 9.17 us  [to_z(): return lax.ppermute(part, 'py', xor_pairs('py', bits))]
    pallas_call x1, Pallas kernels: 5.11 us -> 1.66 us  [prep(): pl.pallas_call(lambda *refs: prep_kernel(width + 2, *refs), out_shape=jax...]
    unnamed x53 -> x55, local copies, waits for them, and re-layouts: 6.9 us -> 3.54 us
    ppermute x9, starting transfers between devices: 12.6 us -> 15 us  [to_z(): return lax.ppermute(part, 'py', xor_pairs('py', bits))]
    ppermute x3, waiting for transfers between devices: 3.13 us -> 1.05 us  [stat_gather(): lax.ppermute(pair, 'py', xor_pairs('py', j))]
    ppermute x6, waiting for transfers between devices: 11.8 us -> 13.5 us  [to_clips(): lax.ppermute(piece, 'clip', xor_pairs('clip', d))]
    ppermute x13, waiting for transfers between devices: 3.4 us -> 4.91 us  [swap(): return lax.ppermute(piece, 'px', xor_pairs('px', 1))]
  transfers between devices with their start and end apart: 31 -> 31, of which waited for: 10 -> 14; matrix products, arithmetic and copies ran while one was open for 9% -> 11% of each run, Pallas kernels for 13% -> 17%
where the time goes in v2:
time: 107 us
  Pallas kernels  33.6 us (31%)
  waiting for transfers between devices  28.6 us (27%)
  starting transfers between devices  28.3 us (26%)
  local copies, waits for them, and re-layouts  10 us (9%)
  other arithmetic  5.49 us (5%)
    pallas_call x1, Pallas kernels, local(): pl.pallas_call(lambda *refs: conv1_kernel(res_plan, rows, cols, *refs), o...  16.1 us
    pallas_call x1, Pallas kernels, local(): pl.pallas_call(lambda *refs: conv2_kernel(up_plan, rows, cols, *refs), ou...  15.9 us
    ppermute x9, starting transfers between devices, to_z(): return lax.ppermute(part, 'py', xor_pairs('py', bits))  15 us
    ppermute x6, waiting for transfers between devices, to_clips(): lax.ppermute(piece, 'clip', xor_pairs('clip', d))  13.5 us
    ppermute x9, waiting for transfers between devices, to_z(): return lax.ppermute(part, 'py', xor_pairs('py', bits))  9.17 us
    ppermute x6, starting transfers between devices, to_clips(): lax.ppermute(piece, 'clip', xor_pairs('clip', d))  7.11 us
    ppermute x13, waiting for transfers between devices, swap(): return lax.ppermute(piece, 'px', xor_pairs('px', 1))  4.91 us
    ppermute x3, starting transfers between devices, stat_gather(): lax.ppermute(pair, 'py', xor_pairs('py', j))  4.42 us
  transfers between devices with their start and end apart: 31, of which 14 were waited for; matrix products, arithmetic and copies ran while one was open for 11% of the time, Pallas kernels for 17%

profile of v2, /device:TPU:0, one launch (start us, length us, event | category | flops | bytes accessed | tf_op | source)
XLA Modules:
  0.0 106.8 jit_solution(10805382216653603890)
XLA Ops:
  0.0 1.0 multiply_convert_fusion
  1.2 3.1 %collective-permute-start.2 = (bf16[12,512]{1,0:T(8,128)(2,1)S(1)}, bf16[12,512]{1,0:T(8,128)(2,1)S(1)}, u32[]{:S(2)}, u32[]{:S(2)}) collective-permute-start(bf16[12,512]{1,0:T(8,128)(2,1)S(1)} %reshape.88), channel_id=1, source_target_pairs={{0,2},{2,0},{4,6},{6,4},{1,3},{3,1},{5,7},{7,5},{8,10},{10,8},{12,... | collective-permute-start | bytes 36872 | tf_op jit(solution)/shard_map/ppermute | solution.py:363
  4.3 2.6 %collective-permute-start.1 = (bf16[12,512]{1,0:T(8,128)(2,1)S(1)}, bf16[12,512]{1,0:T(8,128)(2,1)S(1)}, u32[]{:S(2)}, u32[]{:S(2)}) collective-permute-start(bf16[12,512]{1,0:T(8,128)(2,1)S(1)} %reshape.88), channel_id=1, source_target_pairs={{0,4},{2,6},{4,0},{6,2},{1,5},{3,7},{5,1},{7,3},{8,12},{10,14},{12... | collective-permute-start | bytes 36872 | tf_op jit(solution)/shard_map/ppermute | solution.py:363
  6.8 0.9 constant_dynamic-slice_fusion
  7.8 3.9 %collective-permute-start.8 = (bf16[9,64,128]{2,1,0:T(8,128)(2,1)S(1)}, bf16[9,64,128]{2,1,0:T(8,128)(2,1)S(1)}, u32[]{:S(2)}, u32[]{:S(2)}) collective-permute-start(bf16[9,64,128]{2,1,0:T(8,128)(2,1)S(1)} %constant_dynamic-slice_fusion), channel_id=1, source_target_pairs={{0,6},{2,4},{4,2},{6,0},{1,7},{3,5},{5,3},{7,1},{8,14},{10,12},{12... | collective-permute-start | bytes 442376 | tf_op jit(solution)/shard_map/ppermute | solution.py:363
  11.7 1.0 add_bitcast_fusion.refs_1_
  13.3 2.6 %reshape.94 = bf16[64,4,2,2,512]{4,3,2,1,0:T(2,128)(2,1)S(1)} reshape(bf16[64,4,4,512]{3,2,1,0:T(4,128)(2,1)} %param.12) | data formatting | bytes 2097152 | tf_op jit(solution)/shard_map/reshape | solution.py:337
  22.4 1.7 %prep.1.refs_2_ = f32[16,512]{1,0:T(8,128)S(1)} custom-call(f32[8,8832]{1,0:T(8,128)S(1)} %pad_convert_fusion.refs_0_, bf16[80,640]{1,0:T(8,128)(2,1)S(1)} %add_bitcast_fusion.refs_1_, f32[1,512]{1,0:T(1,128)S(1)} %bitcast.32), custom_call_target="tpu_custom_call" | custom-call | tf_op jit(solution)/shard_map/prep/pallas_call | solution.py:179
  24.7 2.4 %collective-permute-start.18 = (bf16[16,64,128]{2,1,0:T(8,128)(2,1)S(1)}, bf16[16,64,128]{2,1,0:T(8,128)(2,1)S(1)}, u32[]{:S(2)}, u32[]{:S(2)}) collective-permute-start(bf16[16,64,128]{2,1,0:T(8,128)(2,1)S(1)} %constant_dynamic-slice_fusion.1), channel_id=1, source_target_pairs={{0,4},{2,6},{4,0},{6,2},{1,5},{3,7},{5,1},{7,3},{8,12},{10,14},{12... | collective-permute-start | bytes 786440 | tf_op jit(solution)/shard_map/ppermute | solution.py:363
  27.1 2.5 %collective-permute-start.14 = (bf16[3,9,64,128]{3,2,1,0:T(8,128)(2,1)S(1)}, bf16[3,9,64,128]{3,2,1,0:T(8,128)(2,1)S(1)}, u32[]{:S(2)}, u32[]{:S(2)}) collective-permute-start(bf16[3,9,64,128]{3,2,1,0:T(8,128)(2,1)S(1)} %pad_maximum_fusion.1.refs_5_), channel_id=1, source_target_pairs={{0,24},{8,16},{16,8},{24,0},{1,25},{9,17},{17,9},{25,1},{2,26},{10... | collective-permute-start | bytes 1327112 | tf_op jit(solution)/shard_map/ppermute | solution.py:367
  30.7 9.2 %collective-permute-done.18 = bf16[16,64,128]{2,1,0:T(8,128)(2,1)S(1)} collective-permute-done((bf16[16,64,128]{2,1,0:T(8,128)(2,1)S(1)}, bf16[16,64,128]{2,1,0:T(8,128)(2,1)S(1)}, u32[]{:S(2)}, u32[]{:S(2)}) %collective-permute-start.18) | collective-permute-done | bytes 262176 | tf_op jit(solution)/shard_map/ppermute | solution.py:363
  40.3 0.9 collective-permute-done.14.refs_11_
  41.2 8.6 %collective-permute-done.12.refs_9_ = bf16[3,9,64,128]{3,2,1,0:T(8,128)(2,1)S(1)} collective-permute-done((bf16[3,9,64,128]{3,2,1,0:T(8,128)(2,1)S(1)}, bf16[3,9,64,128]{3,2,1,0:T(8,128)(2,1)S(1)}, u32[]{:S(2)}, u32[]{:S(2)}) %collective-permute-start.12) | collective-permute-done | bytes 442400 | tf_op jit(solution)/shard_map/ppermute | solution.py:367
  50.3 2.0 %collective-permute-start.17 = (bf16[16,64,512]{2,1,0:T(8,128)(2,1)S(1)}, bf16[16,64,512]{2,1,0:T(8,128)(2,1)S(1)}, u32[]{:S(2)}, u32[]{:S(2)}) collective-permute-start(bf16[16,64,512]{2,1,0:T(8,128)(2,1)S(1)} %bitcast.35), channel_id=1, source_target_pairs={{0,2},{2,0},{4,6},{6,4},{1,3},{3,1},{5,7},{7,5},{8,10},{10,8},{12,... | collective-permute-start | bytes 3145736 | tf_op jit(solution)/shard_map/ppermute | solution.py:363
  52.3 1.8 %collective-permute-start.22 = (bf16[2,16,64,128]{3,2,1,0:T(8,128)(2,1)S(1)}, bf16[2,16,64,128]{3,2,1,0:T(8,128)(2,1)}, u32[]{:S(2)}, u32[]{:S(2)}) collective-permute-start(bf16[2,16,64,128]{3,2,1,0:T(8,128)(2,1)S(1)} %pad_maximum_fusion.refs_8_), channel_id=1, source_target_pairs={{0,24},{8,16},{16,8},{24,0},{1,25},{9,17},{17,9},{25,1},{2,26},{10... | collective-permute-start | bytes 1572872 | tf_op jit(solution)/shard_map/ppermute | solution.py:367
  54.2 1.2 %collective-permute-start.21 = (bf16[2,16,64,128]{3,2,1,0:T(8,128)(2,1)S(1)}, bf16[2,16,64,128]{3,2,1,0:T(8,128)(2,1)}, u32[]{:S(2)}, u32[]{:S(2)}) collective-permute-start(bf16[2,16,64,128]{3,2,1,0:T(8,128)(2,1)S(1)} %pad_maximum_fusion.refs_8_), channel_id=1, source_target_pairs={{0,16},{8,24},{16,0},{24,8},{1,17},{9,25},{17,1},{25,9},{2,18},{10... | collective-permute-start | bytes 1572872 | tf_op jit(solution)/shard_map/ppermute | solution.py:367
  56.9 16.1 %conv1.1 = (bf16[1440,512]{1,0:T(8,128)(2,1)}, f32[8,512]{1,0:T(8,128)}) custom-call(f32[8,1792]{1,0:T(8,128)} %pad_convert_fusion.1.refs_0_, bf16[80,640]{1,0:T(8,128)(2,1)} %copy-done, f32[16,512]{1,0:T(8,128)} %copy-done.1, bf16[9,64,512]{2,1,0:T(8,128)(2,1)} %bitcast.46, bf16[9,64,512]{2,1,0:T(8,128)(2,1)} %collective-permute-done.4.refs_4_, ...), custom_call_target="tpu_custom_call" | custom-call | flops 6794772480 | bytes 12582912 | tf_op jit(solution)/shard_map/conv1/pallas_call | solution.py:467
  73.0 1.4 %collective-permute-done.16 = f32[8,512]{1,0:T(8,128)S(1)} collective-permute-done((f32[8,512]{1,0:T(8,128)}, f32[8,512]{1,0:T(8,128)S(1)}, u32[]{:S(2)}, u32[]{:S(2)}) %collective-permute-start.16) | collective-permute-done | bytes 16416 | tf_op jit(solution)/shard_map/ppermute | solution.py:347
  74.4 3.9 %collective-permute-done.21.refs_12_ = bf16[2,16,64,128]{3,2,1,0:T(8,128)(2,1)} collective-permute-done((bf16[2,16,64,128]{3,2,1,0:T(8,128)(2,1)S(1)}, bf16[2,16,64,128]{3,2,1,0:T(8,128)(2,1)}, u32[]{:S(2)}, u32[]{:S(2)}) %collective-permute-start.21) | collective-permute-done | bytes 524320 | tf_op jit(solution)/shard_map/ppermute | solution.py:367
  80.0 1.5 %collective-permute-start.24 = (f32[2,8,512]{2,1,0:T(8,128)S(1)}, f32[2,8,512]{2,1,0:T(8,128)S(1)}, u32[]{:S(2)}, u32[]{:S(2)}) collective-permute-start(f32[2,8,512]{2,1,0:T(8,128)S(1)} %pad_maximum_fusion.5), channel_id=1, source_target_pairs={{0,4},{2,6},{4,0},{6,2},{1,5},{3,7},{5,1},{7,3},{8,12},{10,14},{12... | collective-permute-start | bytes 98312 | tf_op jit(solution)/shard_map/ppermute | solution.py:432
  81.5 2.7 %collective-permute-start.23 = (f32[2,8,512]{2,1,0:T(8,128)S(1)}, f32[2,8,512]{2,1,0:T(8,128)S(1)}, u32[]{:S(2)}, u32[]{:S(2)}) collective-permute-start(f32[2,8,512]{2,1,0:T(8,128)S(1)} %pad_maximum_fusion.5), channel_id=1, source_target_pairs={{0,2},{2,0},{4,6},{6,4},{1,3},{3,1},{5,7},{7,5},{8,10},{10,8},{12,... | collective-permute-start | bytes 98312 | tf_op jit(solution)/shard_map/ppermute | solution.py:432
  84.9 0.9 collective-permute-done.25
  86.8 1.1 %collective-permute-done.28.refs_11_ = bf16[2,16,64,128]{3,2,1,0:T(8,128)(2,1)S(1)} collective-permute-done((bf16[2,16,64,128]{3,2,1,0:T(8,128)(2,1)}, bf16[2,16,64,128]{3,2,1,0:T(8,128)(2,1)S(1)}, u32[]{:S(2)}, u32[]{:S(2)}) %collective-permute-start.28) | collective-permute-done | bytes 524320 | tf_op jit(solution)/shard_map/ppermute | solution.py:347
  90.7 15.9 %conv2.1 = bf16[2,32,64,512]{3,2,1,0:T(8,128)(2,1)} custom-call(s32[4]{0:T(128)} %add_convert_fusion.1.refs_0_, bf16[1440,512]{1,0:T(8,128)(2,1)} %get-tuple-element.26.refs_1_, f32[8,8,512]{2,1,0:T(8,128)} %copy-done.11, f32[1,512]{1,0:T(1,128)} %bitcast.48, bf16[16,64,512]{2,1,0:T(8,128)(2,1)} %bitcast.36, ...), custom_call_target="tpu_custom_call" | custom-call | flops 8589934592 | bytes 16777216 | tf_op jit(solution)/shard_map/conv2/pallas_call | solution.py:506
  (135 shorter events, 17.4 us)
Async XLA Ops:
  1.2 16.4 %collective-permute-start.2 = (bf16[12,512]{1,0:T(8,128)(2,1)S(1)}, bf16[12,512]{1,0:T(8,128)(2,1)S(1)}, u32[]{:S(2)}, u32[]{:S(2)}) collective-permute-start(bf16[12,512]{1,0:T(8,128)(2,1)S(1)} %reshape.88), channel_id=1, source_target_pairs={{0,2},{2,0},{4,6},{6,4},{1,3},{3,1},{5,7},{7,5},{8,10},{10,8},{12,... | collective-permute-start | bytes 36872 | tf_op jit(solution)/shard_map/ppermute | solution.py:363
  4.3 12.4 %collective-permute-start.1 = (bf16[12,512]{1,0:T(8,128)(2,1)S(1)}, bf16[12,512]{1,0:T(8,128)(2,1)S(1)}, u32[]{:S(2)}, u32[]{:S(2)}) collective-permute-start(bf16[12,512]{1,0:T(8,128)(2,1)S(1)} %reshape.88), channel_id=1, source_target_pairs={{0,4},{2,6},{4,0},{6,2},{1,5},{3,7},{5,1},{7,3},{8,12},{10,14},{12... | collective-permute-start | bytes 36872 | tf_op jit(solution)/shard_map/ppermute | solution.py:363
  6.8 10.5 %collective-permute-start = (bf16[12,512]{1,0:T(8,128)(2,1)S(1)}, bf16[12,512]{1,0:T(8,128)(2,1)S(1)}, u32[]{:S(2)}, u32[]{:S(2)}) collective-permute-start(bf16[12,512]{1,0:T(8,128)(2,1)S(1)} %reshape.88), channel_id=1, source_target_pairs={{0,6},{2,4},{4,2},{6,0},{1,7},{3,5},{5,3},{7,1},{8,14},{10,12},{12... | collective-permute-start | bytes 36872 | tf_op jit(solution)/shard_map/ppermute | solution.py:363
  7.8 16.9 %collective-permute-start.8 = (bf16[9,64,128]{2,1,0:T(8,128)(2,1)S(1)}, bf16[9,64,128]{2,1,0:T(8,128)(2,1)S(1)}, u32[]{:S(2)}, u32[]{:S(2)}) collective-permute-start(bf16[9,64,128]{2,1,0:T(8,128)(2,1)S(1)} %constant_dynamic-slice_fusion), channel_id=1, source_target_pairs={{0,6},{2,4},{4,2},{6,0},{1,7},{3,5},{5,3},{7,1},{8,14},{10,12},{12... | collective-permute-start | bytes 442376 | tf_op jit(solution)/shard_map/ppermute | solution.py:363
  11.7 13.0 %collective-permute-start.7 = (bf16[9,64,128]{2,1,0:T(8,128)(2,1)S(1)}, bf16[9,64,128]{2,1,0:T(8,128)(2,1)S(1)}, u32[]{:S(2)}, u32[]{:S(2)}) collective-permute-start(bf16[9,64,128]{2,1,0:T(8,128)(2,1)S(1)} %constant_dynamic-slice_fusion), channel_id=1, source_target_pairs={{0,4},{2,6},{4,0},{6,2},{1,5},{3,7},{5,1},{7,3},{8,12},{10,14},{12... | collective-permute-start | bytes 442376 | tf_op jit(solution)/shard_map/ppermute | solution.py:363
  16.7 8.0 %collective-permute-start.6 = (bf16[9,64,128]{2,1,0:T(8,128)(2,1)S(1)}, bf16[9,64,128]{2,1,0:T(8,128)(2,1)S(1)}, u32[]{:S(2)}, u32[]{:S(2)}) collective-permute-start(bf16[9,64,128]{2,1,0:T(8,128)(2,1)S(1)} %constant_dynamic-slice_fusion), channel_id=1, source_target_pairs={{0,2},{2,0},{4,6},{6,4},{1,3},{3,1},{5,7},{7,5},{8,10},{10,8},{12,... | collective-permute-start | bytes 442376 | tf_op jit(solution)/shard_map/ppermute | solution.py:363
  18.4 4.0 %collective-permute-start.4 = (bf16[9,64,512]{2,1,0:T(8,128)(2,1)S(1)}, bf16[9,64,512]{2,1,0:T(8,128)(2,1)}, u32[]{:S(2)}, u32[]{:S(2)}) collective-permute-start(bf16[9,64,512]{2,1,0:T(8,128)(2,1)S(1)} %bitcast.47), channel_id=1, source_target_pairs={{0,1},{1,0},{2,3},{3,2},{4,5},{5,4},{6,7},{7,6},{8,9},{9,8},{10,11... | collective-permute-start | bytes 1769480 | tf_op jit(solution)/shard_map/ppermute | solution.py:347
  24.7 15.1 %collective-permute-start.18 = (bf16[16,64,128]{2,1,0:T(8,128)(2,1)S(1)}, bf16[16,64,128]{2,1,0:T(8,128)(2,1)S(1)}, u32[]{:S(2)}, u32[]{:S(2)}) collective-permute-start(bf16[16,64,128]{2,1,0:T(8,128)(2,1)S(1)} %constant_dynamic-slice_fusion.1), channel_id=1, source_target_pairs={{0,4},{2,6},{4,0},{6,2},{1,5},{3,7},{5,1},{7,3},{8,12},{10,14},{12... | collective-permute-start | bytes 786440 | tf_op jit(solution)/shard_map/ppermute | solution.py:363
  27.1 14.0 %collective-permute-start.14 = (bf16[3,9,64,128]{3,2,1,0:T(8,128)(2,1)S(1)}, bf16[3,9,64,128]{3,2,1,0:T(8,128)(2,1)S(1)}, u32[]{:S(2)}, u32[]{:S(2)}) collective-permute-start(bf16[3,9,64,128]{3,2,1,0:T(8,128)(2,1)S(1)} %pad_maximum_fusion.1.refs_5_), channel_id=1, source_target_pairs={{0,24},{8,16},{16,8},{24,0},{1,25},{9,17},{17,9},{25,1},{2,26},{10... | collective-permute-start | bytes 1327112 | tf_op jit(solution)/shard_map/ppermute | solution.py:367
  29.7 20.1 %collective-permute-start.12 = (bf16[3,9,64,128]{3,2,1,0:T(8,128)(2,1)S(1)}, bf16[3,9,64,128]{3,2,1,0:T(8,128)(2,1)S(1)}, u32[]{:S(2)}, u32[]{:S(2)}) collective-permute-start(bf16[3,9,64,128]{3,2,1,0:T(8,128)(2,1)S(1)} %pad_maximum_fusion.1.refs_5_), channel_id=1, source_target_pairs={{0,16},{8,24},{16,0},{24,8},{1,17},{9,25},{17,1},{25,9},{2,18},{10... | collective-permute-start | bytes 1327112 | tf_op jit(solution)/shard_map/ppermute | solution.py:367
  30.2 19.7 %collective-permute-start.10 = (bf16[3,9,64,128]{3,2,1,0:T(8,128)(2,1)S(1)}, bf16[3,9,64,128]{3,2,1,0:T(8,128)(2,1)S(1)}, u32[]{:S(2)}, u32[]{:S(2)}) collective-permute-start(bf16[3,9,64,128]{3,2,1,0:T(8,128)(2,1)S(1)} %pad_maximum_fusion.1.refs_5_), channel_id=1, source_target_pairs={{0,8},{8,0},{16,24},{24,16},{1,9},{9,1},{17,25},{25,17},{2,10},{10... | collective-permute-start | bytes 1327112 | tf_op jit(solution)/shard_map/ppermute | solution.py:367
  39.8 10.4 %collective-permute-start.19 = (bf16[16,64,128]{2,1,0:T(8,128)(2,1)S(1)}, bf16[16,64,128]{2,1,0:T(8,128)(2,1)S(1)}, u32[]{:S(2)}, u32[]{:S(2)}) collective-permute-start(bf16[16,64,128]{2,1,0:T(8,128)(2,1)S(1)} %collective-permute-done.18), channel_id=1, source_target_pairs={{0,2},{2,0},{4,6},{6,4},{1,3},{3,1},{5,7},{7,5},{8,10},{10,8},{12,... | collective-permute-start | bytes 786440 | tf_op jit(solution)/shard_map/ppermute | solution.py:363
  40.3 12.1 %collective-permute-start.9 = (bf16[3,9,64,128]{3,2,1,0:T(8,128)(2,1)S(1)}, bf16[3,9,64,128]{3,2,1,0:T(8,128)(2,1)S(1)}, u32[]{:S(2)}, u32[]{:S(2)}) collective-permute-start(bf16[3,9,64,128]{3,2,1,0:T(8,128)(2,1)S(1)} %pad_maximum_fusion.1.refs_5_), channel_id=1, source_target_pairs={{0,1},{1,0},{2,3},{3,2},{4,5},{5,4},{6,7},{7,6},{8,9},{9,8},{10,11... | collective-permute-start | bytes 1327112 | tf_op jit(solution)/shard_map/ppermute | solution.py:347
  41.2 13.0 %collective-permute-start.15 = (bf16[3,9,64,128]{3,2,1,0:T(8,128)(2,1)S(1)}, bf16[3,9,64,128]{3,2,1,0:T(8,128)(2,1)S(1)}, u32[]{:S(2)}, u32[]{:S(2)}) collective-permute-start(bf16[3,9,64,128]{3,2,1,0:T(8,128)(2,1)S(1)} %collective-permute-done.14.refs_11_), channel_id=1, source_target_pairs={{0,1},{1,0},{2,3},{3,2},{4,5},{5,4},{6,7},{7,6},{8,9},{9,8},{10,11... | collective-permute-start | bytes 1327112 | tf_op jit(solution)/shard_map/ppermute | solution.py:347
  49.7 5.6 %collective-permute-start.13 = (bf16[3,9,64,128]{3,2,1,0:T(8,128)(2,1)S(1)}, bf16[3,9,64,128]{3,2,1,0:T(8,128)(2,1)S(1)}, u32[]{:S(2)}, u32[]{:S(2)}) collective-permute-start(bf16[3,9,64,128]{3,2,1,0:T(8,128)(2,1)S(1)} %collective-permute-done.12.refs_9_), channel_id=1, source_target_pairs={{0,1},{1,0},{2,3},{3,2},{4,5},{5,4},{6,7},{7,6},{8,9},{9,8},{10,11... | collective-permute-start | bytes 1327112 | tf_op jit(solution)/shard_map/ppermute | solution.py:347
  49.8 6.1 %collective-permute-start.11 = (bf16[3,9,64,128]{3,2,1,0:T(8,128)(2,1)S(1)}, bf16[3,9,64,128]{3,2,1,0:T(8,128)(2,1)S(1)}, u32[]{:S(2)}, u32[]{:S(2)}) collective-permute-start(bf16[3,9,64,128]{3,2,1,0:T(8,128)(2,1)S(1)} %collective-permute-done.10.refs_7_), channel_id=1, source_target_pairs={{0,1},{1,0},{2,3},{3,2},{4,5},{5,4},{6,7},{7,6},{8,9},{9,8},{10,11... | collective-permute-start | bytes 1327112 | tf_op jit(solution)/shard_map/ppermute | solution.py:347
  50.3 28.1 %collective-permute-start.17 = (bf16[16,64,512]{2,1,0:T(8,128)(2,1)S(1)}, bf16[16,64,512]{2,1,0:T(8,128)(2,1)S(1)}, u32[]{:S(2)}, u32[]{:S(2)}) collective-permute-start(bf16[16,64,512]{2,1,0:T(8,128)(2,1)S(1)} %bitcast.35), channel_id=1, source_target_pairs={{0,2},{2,0},{4,6},{6,4},{1,3},{3,1},{5,7},{7,5},{8,10},{10,8},{12,... | collective-permute-start | bytes 3145736 | tf_op jit(solution)/shard_map/ppermute | solution.py:363
  52.3 22.1 %collective-permute-start.22 = (bf16[2,16,64,128]{3,2,1,0:T(8,128)(2,1)S(1)}, bf16[2,16,64,128]{3,2,1,0:T(8,128)(2,1)}, u32[]{:S(2)}, u32[]{:S(2)}) collective-permute-start(bf16[2,16,64,128]{3,2,1,0:T(8,128)(2,1)S(1)} %pad_maximum_fusion.refs_8_), channel_id=1, source_target_pairs={{0,24},{8,16},{16,8},{24,0},{1,25},{9,17},{17,9},{25,1},{2,26},{10... | collective-permute-start | bytes 1572872 | tf_op jit(solution)/shard_map/ppermute | solution.py:367
  54.2 24.1 %collective-permute-start.21 = (bf16[2,16,64,128]{3,2,1,0:T(8,128)(2,1)S(1)}, bf16[2,16,64,128]{3,2,1,0:T(8,128)(2,1)}, u32[]{:S(2)}, u32[]{:S(2)}) collective-permute-start(bf16[2,16,64,128]{3,2,1,0:T(8,128)(2,1)S(1)} %pad_maximum_fusion.refs_8_), channel_id=1, source_target_pairs={{0,16},{8,24},{16,0},{24,8},{1,17},{9,25},{17,1},{25,9},{2,18},{10... | collective-permute-start | bytes 1572872 | tf_op jit(solution)/shard_map/ppermute | solution.py:367
  55.4 23.0 %collective-permute-start.20 = (bf16[2,16,64,128]{3,2,1,0:T(8,128)(2,1)S(1)}, bf16[2,16,64,128]{3,2,1,0:T(8,128)(2,1)}, u32[]{:S(2)}, u32[]{:S(2)}) collective-permute-start(bf16[2,16,64,128]{3,2,1,0:T(8,128)(2,1)S(1)} %pad_maximum_fusion.refs_8_), channel_id=1, source_target_pairs={{0,8},{8,0},{16,24},{24,16},{1,9},{9,1},{17,25},{25,17},{2,10},{10... | collective-permute-start | bytes 1572872 | tf_op jit(solution)/shard_map/ppermute | solution.py:367
  78.4 11.1 %collective-permute-start.26 = (bf16[16,64,512]{2,1,0:T(8,128)(2,1)S(1)}, bf16[16,64,512]{2,1,0:T(8,128)(2,1)S(1)}, u32[]{:S(2)}, u32[]{:S(2)}) collective-permute-start(bf16[16,64,512]{2,1,0:T(8,128)(2,1)S(1)} %collective-permute-done.17.refs_6_), channel_id=1, source_target_pairs={{0,1},{1,0},{2,3},{3,2},{4,5},{5,4},{6,7},{7,6},{8,9},{9,8},{10,11... | collective-permute-start | bytes 3145736 | tf_op jit(solution)/shard_map/ppermute | solution.py:347
  79.8 6.0 %collective-permute-start.25 = (f32[2,8,512]{2,1,0:T(8,128)S(1)}, f32[2,8,512]{2,1,0:T(8,128)S(1)}, u32[]{:S(2)}, u32[]{:S(2)}) collective-permute-start(f32[2,8,512]{2,1,0:T(8,128)S(1)} %pad_maximum_fusion.5), channel_id=1, source_target_pairs={{0,6},{2,4},{4,2},{6,0},{1,7},{3,5},{5,3},{7,1},{8,14},{10,12},{12... | collective-permute-start | bytes 98312 | tf_op jit(solution)/shard_map/ppermute | solution.py:432
  80.0 5.9 %collective-permute-start.24 = (f32[2,8,512]{2,1,0:T(8,128)S(1)}, f32[2,8,512]{2,1,0:T(8,128)S(1)}, u32[]{:S(2)}, u32[]{:S(2)}) collective-permute-start(f32[2,8,512]{2,1,0:T(8,128)S(1)} %pad_maximum_fusion.5), channel_id=1, source_target_pairs={{0,4},{2,6},{4,0},{6,2},{1,5},{3,7},{5,1},{7,3},{8,12},{10,14},{12... | collective-permute-start | bytes 98312 | tf_op jit(solution)/shard_map/ppermute | solution.py:432
  81.5 4.8 %collective-permute-start.23 = (f32[2,8,512]{2,1,0:T(8,128)S(1)}, f32[2,8,512]{2,1,0:T(8,128)S(1)}, u32[]{:S(2)}, u32[]{:S(2)}) collective-permute-start(f32[2,8,512]{2,1,0:T(8,128)S(1)} %pad_maximum_fusion.5), channel_id=1, source_target_pairs={{0,2},{2,0},{4,6},{6,4},{1,3},{3,1},{5,7},{7,5},{8,10},{10,8},{12,... | collective-permute-start | bytes 98312 | tf_op jit(solution)/shard_map/ppermute | solution.py:432
  (32 other events, 246.2 us)

commit v3 on v2

--- a/solution.py
+++ b/solution.py
@@ -238,8 +238,8 @@
     *sources, out_ref, weight, wide, shifted, woven, result, sems, out_sem = refs
     row_len = 2 * COL
     channels = hid_ref.shape[1]
-    copies = copy_plan(sources, weight, sems, 0, 16)
-    for copy in copies:
+    copies = [copy_plan(sources, weight, sems, 4 * i, 4) for i in range(4)]
+    for copy in copies[0] + copies[1]:
         copy.start()
 
     parts = stat_ref.shape[0]
@@ -275,53 +275,57 @@
         return 0
 
     lax.fori_loop(0, rows + 2, normalise, 0)
-    for copy in copies:
-        copy.wait()
 
     step = 8
+    parts = rows // step
     size = step * 2 * cols
 
-    for part in range(rows // step):
-        line = part * step
-        for row_phase in range(2):
-            for col_phase in range(2):
+    def out_copy(part, row_phase):
+        lines = pl.ds(part * step, step)
+        return pltpu.make_async_copy(
+            result.at[:, lines, row_phase],
+            out_ref.at[:, lines, row_phase],
+            out_sem.at[part, row_phase],
+        )
+
+    for row_phase in range(2):
+        for col_phase in range(2):
+            phase = 2 * row_phase + col_phase
+            for copy in copies[phase]:
+                copy.wait()
+            if phase < 2:
+                for copy in copies[phase + 2]:
+                    copy.start()
+            for part in range(parts):
                 acc = None
-                for row_kernel, row_offset in up_taps[row_phase]:
-                    first = (line + row_offset) * (2 * cols)
-                    tap = 4 * row_kernel + 2 * col_phase
+                for i, (_, row_offset) in enumerate(up_taps[row_phase]):
+                    first = (part * step + row_offset) * (2 * cols)
+                    tap = 4 * phase + 2 * i
                     product = jnp.dot(
                         shifted[
-                            pl.ds(first, size), col_phase * channels : (col_phase + 2) * channels
+                            first : first + size, col_phase * channels : (col_phase + 2) * channels
                         ],
                         weight[tap : tap + 2].reshape(2 * channels, channels),
                         preferred_element_type=jnp.float32,
                     )
                     acc = product if acc is None else acc + product
                 for lane in range(channels // 128):
-                    woven[row_phase, lane, pl.ds(col_phase, size, stride=2), :] = acc[
+                    woven[part, lane, pl.ds(col_phase, size, stride=2), :] = acc[
                         :, 128 * lane : 128 * lane + 128
                     ]
-            for y in range(step):
-                for frame in range(2):
-                    at = (2 * y + frame) * 2 * cols
-                    for lane in range(channels // 128):
-                        result[
-                            frame,
-                            2 * (line + y) + row_phase,
-                            :,
-                            128 * lane : 128 * lane + 128,
-                        ] = woven[row_phase, lane, at : at + 2 * cols, :].astype(jnp.bfloat16)
-        for frame in range(2):
-            lines = pl.ds(2 * line, 2 * step)
-            pltpu.make_async_copy(
-                result.at[frame, lines], out_ref.at[frame, lines], out_sem.at[part, frame]
-            ).start()
-    for part in range(rows // step):
-        for frame in range(2):
-            lines = pl.ds(2 * step * part, 2 * step)
-            pltpu.make_async_copy(
-                result.at[frame, lines], out_ref.at[frame, lines], out_sem.at[part, frame]
-            ).wait()
+                if col_phase == 0:
+                    continue
+                for y in range(step):
+                    for frame in range(2):
+                        at = (2 * y + frame) * 2 * cols
+                        for lane in range(channels // 128):
+                            result[
+                                frame, part * step + y, row_phase, :, 128 * lane : 128 * lane + 128
+                            ] = woven[part, lane, at : at + 2 * cols, :].astype(jnp.bfloat16)
+                out_copy(part, row_phase).start()
+    for row_phase in range(2):
+        for part in range(parts):
+            out_copy(part, row_phase).wait()
 
 
 def xor_pairs(axis, bits):
@@ -334,8 +338,8 @@
 
 def paired_taps(weight):
     rows, _, _, width = weight.shape
-    halves = weight.reshape(rows, 4, 2, 2, width)[:, :, ::-1, ::-1, :]
-    return jnp.transpose(halves, (1, 3, 2, 0, 4)).reshape(16, rows, width)
+    halves = weight.reshape(rows, 2, 2, 2, 2, width)[:, :, ::-1, ::-1, ::-1, :]
+    return jnp.transpose(halves, (2, 4, 1, 3, 0, 5)).reshape(16, rows, width)
 
 
 def column_part(weight):
@@ -505,7 +509,7 @@
     step = 8
     return pl.pallas_call(
         lambda *refs: conv2_kernel(up_plan, rows, cols, *refs),
-        out_shape=jax.ShapeDtypeStruct((frames, 2 * rows, 2 * cols, channels), jnp.bfloat16),
+        out_shape=jax.ShapeDtypeStruct((frames, rows, 2, 2 * cols, channels), jnp.bfloat16),
         in_specs=[pl.BlockSpec(memory_space=pltpu.SMEM), WHOLE, WHOLE, WHOLE]
         + [ANY] * len(up_sources),
         out_specs=ANY,
@@ -513,10 +517,10 @@
             pltpu.VMEM((16, channels, channels), jnp.bfloat16),
             pltpu.VMEM((row_len, channels), jnp.float32),
             pltpu.VMEM(((rows + 2) * frames * cols, 3 * channels), jnp.bfloat16),
-            pltpu.VMEM((2, channels // 128, 2 * step * frames * cols, 128), jnp.float32),
-            pltpu.VMEM((frames, 2 * rows, 2 * cols, channels), jnp.bfloat16),
-            pltpu.SemaphoreType.DMA((1, 32)),
-            pltpu.SemaphoreType.DMA((rows // step, frames)),
+            pltpu.VMEM((rows // step, channels // 128, 2 * step * frames * cols, 128), jnp.float32),
+            pltpu.VMEM((frames, rows, 2, 2 * cols, channels), jnp.bfloat16),
+            pltpu.SemaphoreType.DMA((16, 32)),
+            pltpu.SemaphoreType.DMA((rows // step, 2)),
         ],
         compiler_params=pltpu.CompilerParams(vmem_limit_bytes=VMEM_LIMIT),
         cost_estimate=pl.CostEstimate(
@@ -525,7 +529,7 @@
             transcendentals=0,
         ),
         name="conv2",
-    )(edges, hidden, stats, second_gain.reshape(1, channels), *up_sources)
+    )(edges, hidden, stats, second_gain.reshape(1, channels), *up_sources).reshape(frames, 2 * rows, 2 * cols, channels)
 
 
 def solution(mesh):

time: 107 us -> 111 us (1.037)
  Pallas kernels: 33.6 us -> 37.8 us
    pallas_call x1, Pallas kernels: 15.9 us -> 20.1 us  [local(): pl.pallas_call(lambda *refs: conv2_kernel(up_plan, rows, cols, *refs), ou...]
  transfers between devices with their start and end apart: 31 -> 31, of which waited for: 14 -> 14; matrix products, arithmetic and copies ran while one was open for 11% -> 10% of each run, Pallas kernels for 17% -> 16%
where the time goes in v3:
time: 111 us
  Pallas kernels  37.8 us (34%)
  waiting for transfers between devices  28.6 us (26%)
  starting transfers between devices  28.3 us (25%)
  local copies, waits for them, and re-layouts  10 us (9%)
  other arithmetic  5.49 us (5%)
    pallas_call x1, Pallas kernels, local(): pl.pallas_call(lambda *refs: conv2_kernel(up_plan, rows, cols, *refs), ou...  20.1 us
    pallas_call x1, Pallas kernels, local(): pl.pallas_call(lambda *refs: conv1_kernel(res_plan, rows, cols, *refs), o...  16.1 us
    ppermute x9, starting transfers between devices, to_z(): return lax.ppermute(part, 'py', xor_pairs('py', bits))  15 us
    ppermute x6, waiting for transfers between devices, to_clips(): lax.ppermute(piece, 'clip', xor_pairs('clip', d))  13.5 us
    ppermute x9, waiting for transfers between devices, to_z(): return lax.ppermute(part, 'py', xor_pairs('py', bits))  9.17 us
    ppermute x6, starting transfers between devices, to_clips(): lax.ppermute(piece, 'clip', xor_pairs('clip', d))  7.11 us
    ppermute x13, waiting for transfers between devices, swap(): return lax.ppermute(piece, 'px', xor_pairs('px', 1))  4.91 us
    ppermute x3, starting transfers between devices, stat_gather(): lax.ppermute(pair, 'py', xor_pairs('py', j))  4.42 us
  transfers between devices with their start and end apart: 31, of which 14 were waited for; matrix products, arithmetic and copies ran while one was open for 10% of the time, Pallas kernels for 16%

profile of v3, /device:TPU:0, one launch (start us, length us, event | category | flops | bytes accessed | tf_op | source)
XLA Modules:
  0.0 110.9 jit_solution(127303741755661542)
XLA Ops:
  0.0 1.0 multiply_convert_fusion
  1.2 3.1 %collective-permute-start.2 = (bf16[12,512]{1,0:T(8,128)(2,1)S(1)}, bf16[12,512]{1,0:T(8,128)(2,1)S(1)}, u32[]{:S(2)}, u32[]{:S(2)}) collective-permute-start(bf16[12,512]{1,0:T(8,128)(2,1)S(1)} %reshape.91), channel_id=1, source_target_pairs={{0,2},{2,0},{4,6},{6,4},{1,3},{3,1},{5,7},{7,5},{8,10},{10,8},{12,... | collective-permute-start | bytes 36872 | tf_op jit(solution)/shard_map/ppermute | solution.py:367
  4.3 2.6 %collective-permute-start.1 = (bf16[12,512]{1,0:T(8,128)(2,1)S(1)}, bf16[12,512]{1,0:T(8,128)(2,1)S(1)}, u32[]{:S(2)}, u32[]{:S(2)}) collective-permute-start(bf16[12,512]{1,0:T(8,128)(2,1)S(1)} %reshape.91), channel_id=1, source_target_pairs={{0,4},{2,6},{4,0},{6,2},{1,5},{3,7},{5,1},{7,3},{8,12},{10,14},{12... | collective-permute-start | bytes 36872 | tf_op jit(solution)/shard_map/ppermute | solution.py:367
  6.8 0.9 constant_dynamic-slice_fusion
  7.8 3.9 %collective-permute-start.8 = (bf16[9,64,128]{2,1,0:T(8,128)(2,1)S(1)}, bf16[9,64,128]{2,1,0:T(8,128)(2,1)S(1)}, u32[]{:S(2)}, u32[]{:S(2)}) collective-permute-start(bf16[9,64,128]{2,1,0:T(8,128)(2,1)S(1)} %constant_dynamic-slice_fusion), channel_id=1, source_target_pairs={{0,6},{2,4},{4,2},{6,0},{1,7},{3,5},{5,3},{7,1},{8,14},{10,12},{12... | collective-permute-start | bytes 442376 | tf_op jit(solution)/shard_map/ppermute | solution.py:367
  11.7 1.0 add_bitcast_fusion.refs_1_
  13.3 2.6 %reshape.97 = bf16[64,2,2,2,2,512]{5,4,3,2,1,0:T(2,128)(2,1)S(1)} reshape(bf16[64,4,4,512]{3,2,1,0:T(4,128)(2,1)} %param.12) | data formatting | bytes 2097152 | tf_op jit(solution)/shard_map/reshape | solution.py:341
  22.4 1.7 %prep.1.refs_2_ = f32[16,512]{1,0:T(8,128)S(1)} custom-call(f32[8,8832]{1,0:T(8,128)S(1)} %pad_convert_fusion.refs_0_, bf16[80,640]{1,0:T(8,128)(2,1)S(1)} %add_bitcast_fusion.refs_1_, f32[1,512]{1,0:T(1,128)S(1)} %bitcast.33), custom_call_target="tpu_custom_call" | custom-call | tf_op jit(solution)/shard_map/prep/pallas_call | solution.py:179
  24.7 2.4 %collective-permute-start.18 = (bf16[16,64,128]{2,1,0:T(8,128)(2,1)S(1)}, bf16[16,64,128]{2,1,0:T(8,128)(2,1)S(1)}, u32[]{:S(2)}, u32[]{:S(2)}) collective-permute-start(bf16[16,64,128]{2,1,0:T(8,128)(2,1)S(1)} %constant_dynamic-slice_fusion.1), channel_id=1, source_target_pairs={{0,4},{2,6},{4,0},{6,2},{1,5},{3,7},{5,1},{7,3},{8,12},{10,14},{12... | collective-permute-start | bytes 786440 | tf_op jit(solution)/shard_map/ppermute | solution.py:367
  27.1 2.5 %collective-permute-start.14 = (bf16[3,9,64,128]{3,2,1,0:T(8,128)(2,1)S(1)}, bf16[3,9,64,128]{3,2,1,0:T(8,128)(2,1)S(1)}, u32[]{:S(2)}, u32[]{:S(2)}) collective-permute-start(bf16[3,9,64,128]{3,2,1,0:T(8,128)(2,1)S(1)} %pad_maximum_fusion.1.refs_5_), channel_id=1, source_target_pairs={{0,24},{8,16},{16,8},{24,0},{1,25},{9,17},{17,9},{25,1},{2,26},{10... | collective-permute-start | bytes 1327112 | tf_op jit(solution)/shard_map/ppermute | solution.py:371
  30.7 9.2 %collective-permute-done.18 = bf16[16,64,128]{2,1,0:T(8,128)(2,1)S(1)} collective-permute-done((bf16[16,64,128]{2,1,0:T(8,128)(2,1)S(1)}, bf16[16,64,128]{2,1,0:T(8,128)(2,1)S(1)}, u32[]{:S(2)}, u32[]{:S(2)}) %collective-permute-start.18) | collective-permute-done | bytes 262176 | tf_op jit(solution)/shard_map/ppermute | solution.py:367
  40.3 0.9 collective-permute-done.14.refs_11_
  41.2 8.6 %collective-permute-done.12.refs_9_ = bf16[3,9,64,128]{3,2,1,0:T(8,128)(2,1)S(1)} collective-permute-done((bf16[3,9,64,128]{3,2,1,0:T(8,128)(2,1)S(1)}, bf16[3,9,64,128]{3,2,1,0:T(8,128)(2,1)S(1)}, u32[]{:S(2)}, u32[]{:S(2)}) %collective-permute-start.12) | collective-permute-done | bytes 442400 | tf_op jit(solution)/shard_map/ppermute | solution.py:371
  50.3 2.0 %collective-permute-start.17 = (bf16[16,64,512]{2,1,0:T(8,128)(2,1)S(1)}, bf16[16,64,512]{2,1,0:T(8,128)(2,1)S(1)}, u32[]{:S(2)}, u32[]{:S(2)}) collective-permute-start(bf16[16,64,512]{2,1,0:T(8,128)(2,1)S(1)} %bitcast.36), channel_id=1, source_target_pairs={{0,2},{2,0},{4,6},{6,4},{1,3},{3,1},{5,7},{7,5},{8,10},{10,8},{12,... | collective-permute-start | bytes 3145736 | tf_op jit(solution)/shard_map/ppermute | solution.py:367
  52.3 1.8 %collective-permute-start.22 = (bf16[2,16,64,128]{3,2,1,0:T(8,128)(2,1)S(1)}, bf16[2,16,64,128]{3,2,1,0:T(8,128)(2,1)}, u32[]{:S(2)}, u32[]{:S(2)}) collective-permute-start(bf16[2,16,64,128]{3,2,1,0:T(8,128)(2,1)S(1)} %pad_maximum_fusion.refs_8_), channel_id=1, source_target_pairs={{0,24},{8,16},{16,8},{24,0},{1,25},{9,17},{17,9},{25,1},{2,26},{10... | collective-permute-start | bytes 1572872 | tf_op jit(solution)/shard_map/ppermute | solution.py:371
  54.2 1.2 %collective-permute-start.21 = (bf16[2,16,64,128]{3,2,1,0:T(8,128)(2,1)S(1)}, bf16[2,16,64,128]{3,2,1,0:T(8,128)(2,1)}, u32[]{:S(2)}, u32[]{:S(2)}) collective-permute-start(bf16[2,16,64,128]{3,2,1,0:T(8,128)(2,1)S(1)} %pad_maximum_fusion.refs_8_), channel_id=1, source_target_pairs={{0,16},{8,24},{16,0},{24,8},{1,17},{9,25},{17,1},{25,9},{2,18},{10... | collective-permute-start | bytes 1572872 | tf_op jit(solution)/shard_map/ppermute | solution.py:371
  56.9 16.1 %conv1.1 = (bf16[1440,512]{1,0:T(8,128)(2,1)}, f32[8,512]{1,0:T(8,128)}) custom-call(f32[8,1792]{1,0:T(8,128)} %pad_convert_fusion.1.refs_0_, bf16[80,640]{1,0:T(8,128)(2,1)} %copy-done, f32[16,512]{1,0:T(8,128)} %copy-done.1, bf16[9,64,512]{2,1,0:T(8,128)(2,1)} %bitcast.47, bf16[9,64,512]{2,1,0:T(8,128)(2,1)} %collective-permute-done.4.refs_4_, ...), custom_call_target="tpu_custom_call" | custom-call | flops 6794772480 | bytes 12582912 | tf_op jit(solution)/shard_map/conv1/pallas_call | solution.py:471
  73.0 1.4 %collective-permute-done.16 = f32[8,512]{1,0:T(8,128)S(1)} collective-permute-done((f32[8,512]{1,0:T(8,128)}, f32[8,512]{1,0:T(8,128)S(1)}, u32[]{:S(2)}, u32[]{:S(2)}) %collective-permute-start.16) | collective-permute-done | bytes 16416 | tf_op jit(solution)/shard_map/ppermute | solution.py:351
  74.4 3.9 %collective-permute-done.21.refs_12_ = bf16[2,16,64,128]{3,2,1,0:T(8,128)(2,1)} collective-permute-done((bf16[2,16,64,128]{3,2,1,0:T(8,128)(2,1)S(1)}, bf16[2,16,64,128]{3,2,1,0:T(8,128)(2,1)}, u32[]{:S(2)}, u32[]{:S(2)}) %collective-permute-start.21) | collective-permute-done | bytes 524320 | tf_op jit(solution)/shard_map/ppermute | solution.py:371
  80.0 1.5 %collective-permute-start.24 = (f32[2,8,512]{2,1,0:T(8,128)S(1)}, f32[2,8,512]{2,1,0:T(8,128)S(1)}, u32[]{:S(2)}, u32[]{:S(2)}) collective-permute-start(f32[2,8,512]{2,1,0:T(8,128)S(1)} %pad_maximum_fusion.5), channel_id=1, source_target_pairs={{0,4},{2,6},{4,0},{6,2},{1,5},{3,7},{5,1},{7,3},{8,12},{10,14},{12... | collective-permute-start | bytes 98312 | tf_op jit(solution)/shard_map/ppermute | solution.py:436
  81.5 2.7 %collective-permute-start.23 = (f32[2,8,512]{2,1,0:T(8,128)S(1)}, f32[2,8,512]{2,1,0:T(8,128)S(1)}, u32[]{:S(2)}, u32[]{:S(2)}) collective-permute-start(f32[2,8,512]{2,1,0:T(8,128)S(1)} %pad_maximum_fusion.5), channel_id=1, source_target_pairs={{0,2},{2,0},{4,6},{6,4},{1,3},{3,1},{5,7},{7,5},{8,10},{10,8},{12,... | collective-permute-start | bytes 98312 | tf_op jit(solution)/shard_map/ppermute | solution.py:436
  84.9 0.9 collective-permute-done.25
  86.8 1.1 %collective-permute-done.28.refs_11_ = bf16[2,16,64,128]{3,2,1,0:T(8,128)(2,1)S(1)} collective-permute-done((bf16[2,16,64,128]{3,2,1,0:T(8,128)(2,1)}, bf16[2,16,64,128]{3,2,1,0:T(8,128)(2,1)S(1)}, u32[]{:S(2)}, u32[]{:S(2)}) %collective-permute-start.28) | collective-permute-done | bytes 524320 | tf_op jit(solution)/shard_map/ppermute | solution.py:351
  90.7 20.1 %conv2.1 = bf16[2,16,2,64,512]{4,3,2,1,0:T(8,128)(2,1)} custom-call(s32[4]{0:T(128)} %add_convert_fusion.1.refs_0_, bf16[1440,512]{1,0:T(8,128)(2,1)} %get-tuple-element.26.refs_1_, f32[8,8,512]{2,1,0:T(8,128)} %copy-done.11, f32[1,512]{1,0:T(1,128)} %bitcast.49, bf16[16,64,512]{2,1,0:T(8,128)(2,1)} %bitcast.37, ...), custom_call_target="tpu_custom_call" | custom-call | flops 8589934592 | bytes 16777216 | tf_op jit(solution)/shard_map/conv2/pallas_call | solution.py:510
  (135 shorter events, 17.4 us)
Async XLA Ops:
  1.2 16.4 %collective-permute-start.2 = (bf16[12,512]{1,0:T(8,128)(2,1)S(1)}, bf16[12,512]{1,0:T(8,128)(2,1)S(1)}, u32[]{:S(2)}, u32[]{:S(2)}) collective-permute-start(bf16[12,512]{1,0:T(8,128)(2,1)S(1)} %reshape.91), channel_id=1, source_target_pairs={{0,2},{2,0},{4,6},{6,4},{1,3},{3,1},{5,7},{7,5},{8,10},{10,8},{12,... | collective-permute-start | bytes 36872 | tf_op jit(solution)/shard_map/ppermute | solution.py:367
  4.3 12.4 %collective-permute-start.1 = (bf16[12,512]{1,0:T(8,128)(2,1)S(1)}, bf16[12,512]{1,0:T(8,128)(2,1)S(1)}, u32[]{:S(2)}, u32[]{:S(2)}) collective-permute-start(bf16[12,512]{1,0:T(8,128)(2,1)S(1)} %reshape.91), channel_id=1, source_target_pairs={{0,4},{2,6},{4,0},{6,2},{1,5},{3,7},{5,1},{7,3},{8,12},{10,14},{12... | collective-permute-start | bytes 36872 | tf_op jit(solution)/shard_map/ppermute | solution.py:367
  6.8 10.5 %collective-permute-start = (bf16[12,512]{1,0:T(8,128)(2,1)S(1)}, bf16[12,512]{1,0:T(8,128)(2,1)S(1)}, u32[]{:S(2)}, u32[]{:S(2)}) collective-permute-start(bf16[12,512]{1,0:T(8,128)(2,1)S(1)} %reshape.91), channel_id=1, source_target_pairs={{0,6},{2,4},{4,2},{6,0},{1,7},{3,5},{5,3},{7,1},{8,14},{10,12},{12... | collective-permute-start | bytes 36872 | tf_op jit(solution)/shard_map/ppermute | solution.py:367
  7.8 16.9 %collective-permute-start.8 = (bf16[9,64,128]{2,1,0:T(8,128)(2,1)S(1)}, bf16[9,64,128]{2,1,0:T(8,128)(2,1)S(1)}, u32[]{:S(2)}, u32[]{:S(2)}) collective-permute-start(bf16[9,64,128]{2,1,0:T(8,128)(2,1)S(1)} %constant_dynamic-slice_fusion), channel_id=1, source_target_pairs={{0,6},{2,4},{4,2},{6,0},{1,7},{3,5},{5,3},{7,1},{8,14},{10,12},{12... | collective-permute-start | bytes 442376 | tf_op jit(solution)/shard_map/ppermute | solution.py:367
  11.7 13.0 %collective-permute-start.7 = (bf16[9,64,128]{2,1,0:T(8,128)(2,1)S(1)}, bf16[9,64,128]{2,1,0:T(8,128)(2,1)S(1)}, u32[]{:S(2)}, u32[]{:S(2)}) collective-permute-start(bf16[9,64,128]{2,1,0:T(8,128)(2,1)S(1)} %constant_dynamic-slice_fusion), channel_id=1, source_target_pairs={{0,4},{2,6},{4,0},{6,2},{1,5},{3,7},{5,1},{7,3},{8,12},{10,14},{12... | collective-permute-start | bytes 442376 | tf_op jit(solution)/shard_map/ppermute | solution.py:367
  16.7 8.0 %collective-permute-start.6 = (bf16[9,64,128]{2,1,0:T(8,128)(2,1)S(1)}, bf16[9,64,128]{2,1,0:T(8,128)(2,1)S(1)}, u32[]{:S(2)}, u32[]{:S(2)}) collective-permute-start(bf16[9,64,128]{2,1,0:T(8,128)(2,1)S(1)} %constant_dynamic-slice_fusion), channel_id=1, source_target_pairs={{0,2},{2,0},{4,6},{6,4},{1,3},{3,1},{5,7},{7,5},{8,10},{10,8},{12,... | collective-permute-start | bytes 442376 | tf_op jit(solution)/shard_map/ppermute | solution.py:367
  18.4 4.0 %collective-permute-start.4 = (bf16[9,64,512]{2,1,0:T(8,128)(2,1)S(1)}, bf16[9,64,512]{2,1,0:T(8,128)(2,1)}, u32[]{:S(2)}, u32[]{:S(2)}) collective-permute-start(bf16[9,64,512]{2,1,0:T(8,128)(2,1)S(1)} %bitcast.48), channel_id=1, source_target_pairs={{0,1},{1,0},{2,3},{3,2},{4,5},{5,4},{6,7},{7,6},{8,9},{9,8},{10,11... | collective-permute-start | bytes 1769480 | tf_op jit(solution)/shard_map/ppermute | solution.py:351
  24.7 15.1 %collective-permute-start.18 = (bf16[16,64,128]{2,1,0:T(8,128)(2,1)S(1)}, bf16[16,64,128]{2,1,0:T(8,128)(2,1)S(1)}, u32[]{:S(2)}, u32[]{:S(2)}) collective-permute-start(bf16[16,64,128]{2,1,0:T(8,128)(2,1)S(1)} %constant_dynamic-slice_fusion.1), channel_id=1, source_target_pairs={{0,4},{2,6},{4,0},{6,2},{1,5},{3,7},{5,1},{7,3},{8,12},{10,14},{12... | collective-permute-start | bytes 786440 | tf_op jit(solution)/shard_map/ppermute | solution.py:367
  27.1 14.0 %collective-permute-start.14 = (bf16[3,9,64,128]{3,2,1,0:T(8,128)(2,1)S(1)}, bf16[3,9,64,128]{3,2,1,0:T(8,128)(2,1)S(1)}, u32[]{:S(2)}, u32[]{:S(2)}) collective-permute-start(bf16[3,9,64,128]{3,2,1,0:T(8,128)(2,1)S(1)} %pad_maximum_fusion.1.refs_5_), channel_id=1, source_target_pairs={{0,24},{8,16},{16,8},{24,0},{1,25},{9,17},{17,9},{25,1},{2,26},{10... | collective-permute-start | bytes 1327112 | tf_op jit(solution)/shard_map/ppermute | solution.py:371
  29.7 20.1 %collective-permute-start.12 = (bf16[3,9,64,128]{3,2,1,0:T(8,128)(2,1)S(1)}, bf16[3,9,64,128]{3,2,1,0:T(8,128)(2,1)S(1)}, u32[]{:S(2)}, u32[]{:S(2)}) collective-permute-start(bf16[3,9,64,128]{3,2,1,0:T(8,128)(2,1)S(1)} %pad_maximum_fusion.1.refs_5_), channel_id=1, source_target_pairs={{0,16},{8,24},{16,0},{24,8},{1,17},{9,25},{17,1},{25,9},{2,18},{10... | collective-permute-start | bytes 1327112 | tf_op jit(solution)/shard_map/ppermute | solution.py:371
  30.2 19.7 %collective-permute-start.10 = (bf16[3,9,64,128]{3,2,1,0:T(8,128)(2,1)S(1)}, bf16[3,9,64,128]{3,2,1,0:T(8,128)(2,1)S(1)}, u32[]{:S(2)}, u32[]{:S(2)}) collective-permute-start(bf16[3,9,64,128]{3,2,1,0:T(8,128)(2,1)S(1)} %pad_maximum_fusion.1.refs_5_), channel_id=1, source_target_pairs={{0,8},{8,0},{16,24},{24,16},{1,9},{9,1},{17,25},{25,17},{2,10},{10... | collective-permute-start | bytes 1327112 | tf_op jit(solution)/shard_map/ppermute | solution.py:371
  39.8 10.4 %collective-permute-start.19 = (bf16[16,64,128]{2,1,0:T(8,128)(2,1)S(1)}, bf16[16,64,128]{2,1,0:T(8,128)(2,1)S(1)}, u32[]{:S(2)}, u32[]{:S(2)}) collective-permute-start(bf16[16,64,128]{2,1,0:T(8,128)(2,1)S(1)} %collective-permute-done.18), channel_id=1, source_target_pairs={{0,2},{2,0},{4,6},{6,4},{1,3},{3,1},{5,7},{7,5},{8,10},{10,8},{12,... | collective-permute-start | bytes 786440 | tf_op jit(solution)/shard_map/ppermute | solution.py:367
  40.3 12.1 %collective-permute-start.9 = (bf16[3,9,64,128]{3,2,1,0:T(8,128)(2,1)S(1)}, bf16[3,9,64,128]{3,2,1,0:T(8,128)(2,1)S(1)}, u32[]{:S(2)}, u32[]{:S(2)}) collective-permute-start(bf16[3,9,64,128]{3,2,1,0:T(8,128)(2,1)S(1)} %pad_maximum_fusion.1.refs_5_), channel_id=1, source_target_pairs={{0,1},{1,0},{2,3},{3,2},{4,5},{5,4},{6,7},{7,6},{8,9},{9,8},{10,11... | collective-permute-start | bytes 1327112 | tf_op jit(solution)/shard_map/ppermute | solution.py:351
  41.2 13.0 %collective-permute-start.15 = (bf16[3,9,64,128]{3,2,1,0:T(8,128)(2,1)S(1)}, bf16[3,9,64,128]{3,2,1,0:T(8,128)(2,1)S(1)}, u32[]{:S(2)}, u32[]{:S(2)}) collective-permute-start(bf16[3,9,64,128]{3,2,1,0:T(8,128)(2,1)S(1)} %collective-permute-done.14.refs_11_), channel_id=1, source_target_pairs={{0,1},{1,0},{2,3},{3,2},{4,5},{5,4},{6,7},{7,6},{8,9},{9,8},{10,11... | collective-permute-start | bytes 1327112 | tf_op jit(solution)/shard_map/ppermute | solution.py:351
  49.7 5.6 %collective-permute-start.13 = (bf16[3,9,64,128]{3,2,1,0:T(8,128)(2,1)S(1)}, bf16[3,9,64,128]{3,2,1,0:T(8,128)(2,1)S(1)}, u32[]{:S(2)}, u32[]{:S(2)}) collective-permute-start(bf16[3,9,64,128]{3,2,1,0:T(8,128)(2,1)S(1)} %collective-permute-done.12.refs_9_), channel_id=1, source_target_pairs={{0,1},{1,0},{2,3},{3,2},{4,5},{5,4},{6,7},{7,6},{8,9},{9,8},{10,11... | collective-permute-start | bytes 1327112 | tf_op jit(solution)/shard_map/ppermute | solution.py:351
  49.8 6.1 %collective-permute-start.11 = (bf16[3,9,64,128]{3,2,1,0:T(8,128)(2,1)S(1)}, bf16[3,9,64,128]{3,2,1,0:T(8,128)(2,1)S(1)}, u32[]{:S(2)}, u32[]{:S(2)}) collective-permute-start(bf16[3,9,64,128]{3,2,1,0:T(8,128)(2,1)S(1)} %collective-permute-done.10.refs_7_), channel_id=1, source_target_pairs={{0,1},{1,0},{2,3},{3,2},{4,5},{5,4},{6,7},{7,6},{8,9},{9,8},{10,11... | collective-permute-start | bytes 1327112 | tf_op jit(solution)/shard_map/ppermute | solution.py:351
  50.3 28.1 %collective-permute-start.17 = (bf16[16,64,512]{2,1,0:T(8,128)(2,1)S(1)}, bf16[16,64,512]{2,1,0:T(8,128)(2,1)S(1)}, u32[]{:S(2)}, u32[]{:S(2)}) collective-permute-start(bf16[16,64,512]{2,1,0:T(8,128)(2,1)S(1)} %bitcast.36), channel_id=1, source_target_pairs={{0,2},{2,0},{4,6},{6,4},{1,3},{3,1},{5,7},{7,5},{8,10},{10,8},{12,... | collective-permute-start | bytes 3145736 | tf_op jit(solution)/shard_map/ppermute | solution.py:367
  52.3 22.1 %collective-permute-start.22 = (bf16[2,16,64,128]{3,2,1,0:T(8,128)(2,1)S(1)}, bf16[2,16,64,128]{3,2,1,0:T(8,128)(2,1)}, u32[]{:S(2)}, u32[]{:S(2)}) collective-permute-start(bf16[2,16,64,128]{3,2,1,0:T(8,128)(2,1)S(1)} %pad_maximum_fusion.refs_8_), channel_id=1, source_target_pairs={{0,24},{8,16},{16,8},{24,0},{1,25},{9,17},{17,9},{25,1},{2,26},{10... | collective-permute-start | bytes 1572872 | tf_op jit(solution)/shard_map/ppermute | solution.py:371
  54.2 24.1 %collective-permute-start.21 = (bf16[2,16,64,128]{3,2,1,0:T(8,128)(2,1)S(1)}, bf16[2,16,64,128]{3,2,1,0:T(8,128)(2,1)}, u32[]{:S(2)}, u32[]{:S(2)}) collective-permute-start(bf16[2,16,64,128]{3,2,1,0:T(8,128)(2,1)S(1)} %pad_maximum_fusion.refs_8_), channel_id=1, source_target_pairs={{0,16},{8,24},{16,0},{24,8},{1,17},{9,25},{17,1},{25,9},{2,18},{10... | collective-permute-start | bytes 1572872 | tf_op jit(solution)/shard_map/ppermute | solution.py:371
  55.4 23.0 %collective-permute-start.20 = (bf16[2,16,64,128]{3,2,1,0:T(8,128)(2,1)S(1)}, bf16[2,16,64,128]{3,2,1,0:T(8,128)(2,1)}, u32[]{:S(2)}, u32[]{:S(2)}) collective-permute-start(bf16[2,16,64,128]{3,2,1,0:T(8,128)(2,1)S(1)} %pad_maximum_fusion.refs_8_), channel_id=1, source_target_pairs={{0,8},{8,0},{16,24},{24,16},{1,9},{9,1},{17,25},{25,17},{2,10},{10... | collective-permute-start | bytes 1572872 | tf_op jit(solution)/shard_map/ppermute | solution.py:371
  78.4 11.1 %collective-permute-start.26 = (bf16[16,64,512]{2,1,0:T(8,128)(2,1)S(1)}, bf16[16,64,512]{2,1,0:T(8,128)(2,1)S(1)}, u32[]{:S(2)}, u32[]{:S(2)}) collective-permute-start(bf16[16,64,512]{2,1,0:T(8,128)(2,1)S(1)} %collective-permute-done.17.refs_6_), channel_id=1, source_target_pairs={{0,1},{1,0},{2,3},{3,2},{4,5},{5,4},{6,7},{7,6},{8,9},{9,8},{10,11... | collective-permute-start | bytes 3145736 | tf_op jit(solution)/shard_map/ppermute | solution.py:351
  79.8 6.0 %collective-permute-start.25 = (f32[2,8,512]{2,1,0:T(8,128)S(1)}, f32[2,8,512]{2,1,0:T(8,128)S(1)}, u32[]{:S(2)}, u32[]{:S(2)}) collective-permute-start(f32[2,8,512]{2,1,0:T(8,128)S(1)} %pad_maximum_fusion.5), channel_id=1, source_target_pairs={{0,6},{2,4},{4,2},{6,0},{1,7},{3,5},{5,3},{7,1},{8,14},{10,12},{12... | collective-permute-start | bytes 98312 | tf_op jit(solution)/shard_map/ppermute | solution.py:436
  80.0 5.9 %collective-permute-start.24 = (f32[2,8,512]{2,1,0:T(8,128)S(1)}, f32[2,8,512]{2,1,0:T(8,128)S(1)}, u32[]{:S(2)}, u32[]{:S(2)}) collective-permute-start(f32[2,8,512]{2,1,0:T(8,128)S(1)} %pad_maximum_fusion.5), channel_id=1, source_target_pairs={{0,4},{2,6},{4,0},{6,2},{1,5},{3,7},{5,1},{7,3},{8,12},{10,14},{12... | collective-permute-start | bytes 98312 | tf_op jit(solution)/shard_map/ppermute | solution.py:436
  81.5 4.8 %collective-permute-start.23 = (f32[2,8,512]{2,1,0:T(8,128)S(1)}, f32[2,8,512]{2,1,0:T(8,128)S(1)}, u32[]{:S(2)}, u32[]{:S(2)}) collective-permute-start(f32[2,8,512]{2,1,0:T(8,128)S(1)} %pad_maximum_fusion.5), channel_id=1, source_target_pairs={{0,2},{2,0},{4,6},{6,4},{1,3},{3,1},{5,7},{7,5},{8,10},{10,8},{12,... | collective-permute-start | bytes 98312 | tf_op jit(solution)/shard_map/ppermute | solution.py:436
  (32 other events, 246.2 us)

commit v4 on v2

--- a/solution.py
+++ b/solution.py
@@ -189,16 +189,16 @@
 def conv1_kernel(copy_plan, rows, cols, *refs):
     patch_ref, w_ref, norm_ref, *sources, hid_ref, stat_ref, weight, wide, act, feat, total, sems = refs
     row_len = 2 * COL
-    copies = [copy_plan(sources, weight, sems, 3 * i, 3) for i in range(3)]
-    for copy in copies[0] + copies[1] + copies[2]:
+    copies = copy_plan(sources, weight, sems, 0, 9)
+    for copy in copies:
         copy.start()
     features(patch_ref[...], w_ref, norm_ref, wide, act, feat)
     channels = feat.shape[1]
     count = hid_ref.shape[0]
     group = count
+    for copy in copies:
+        copy.wait()
     for row_tap in range(3):
-        for copy in copies[row_tap]:
-            copy.wait()
         taps = weight[3 * row_tap : 3 * row_tap + 3].reshape(3 * channels, channels)
         for start in range(0, count, group):
             size = min(group, count - start)
@@ -234,7 +234,8 @@
     stat_ref[2:8, :] = jnp.zeros((6, channels), jnp.float32)
 
 
-def conv2_kernel(copy_plan, rows, cols, edge_ref, hid_ref, stat_ref, gain_ref, *refs):
+def conv2_kernel(copy_plan, stat_count, rows, cols, edge_ref, hid_ref, gain_ref, *refs):
+    stat_refs, refs = refs[:stat_count], refs[stat_count:]
     *sources, out_ref, weight, wide, shifted, woven, result, sems, out_sem = refs
     row_len = 2 * COL
     channels = hid_ref.shape[1]
@@ -242,12 +243,13 @@
     for copy in copies:
         copy.start()
 
-    parts = stat_ref.shape[0]
+    parts = sum(ref.shape[0] for ref in stat_refs)
     cells = 2.0 * rows * cols
-    means = stat_ref[:, 0, :]
+    means = jnp.concatenate([ref[:, 0, :] for ref in stat_refs], axis=0)
+    squares = jnp.concatenate([ref[:, 1, :] for ref in stat_refs], axis=0)
     average_c = jnp.sum(means, axis=0, keepdims=True) / parts
     apart = means - average_c
-    square_c = jnp.sum(stat_ref[:, 1, :] + cells * apart * apart, axis=0, keepdims=True)
+    square_c = jnp.sum(squares + cells * apart * apart, axis=0, keepdims=True)
     average_c = jnp.broadcast_to(average_c, (8, channels))
     spread_c = jnp.broadcast_to(square_c, (8, channels)) / (cells * parts)
     average = group_mean(average_c)
@@ -424,13 +426,8 @@
     return whole, moved
 
 
-def stat_gather(stat, other=None):
-    if lax.axis_size("py") != 4 or lax.axis_size("px") != 2:
-        return axis_gather(axis_gather(stat[None], "px", 0), "py", 0)
-    pair = jnp.stack([stat, other])
-    return jnp.concatenate(
-        [pair] + [lax.ppermute(pair, "py", xor_pairs("py", j)) for j in (1, 2, 3)], axis=0
-    )
+def stat_gather(pair):
+    return [pair] + [lax.ppermute(pair, "py", xor_pairs("py", j)) for j in (1, 2, 3)]
 
 
 ANY = pl.BlockSpec(memory_space=pl.ANY)
@@ -477,7 +474,7 @@
             pltpu.VMEM((cells + 2 * row_len, 3 * channels), jnp.bfloat16),
             pltpu.VMEM((cells, channels), jnp.bfloat16),
             pltpu.VMEM((cells, channels), jnp.float32),
-            pltpu.SemaphoreType.DMA((9, 32)),
+            pltpu.SemaphoreType.DMA((1, 32)),
         ],
         compiler_params=pltpu.CompilerParams(vmem_limit_bytes=VMEM_LIMIT),
         cost_estimate=pl.CostEstimate(
@@ -488,7 +485,7 @@
     if paired:
         other = swap(stat)
         up_near, *up_spread = after((up_near, *up_spread), other)
-        stats = stat_gather(stat, after(other, up_near, *up_spread))
+        stats = stat_gather(after(jnp.stack([stat, other]), up_near, *up_spread))
         placed = [(up_taps_own, (), 0, None, 0), (up_other, (), 0, None, 1)]
         placed += [(up_near, (), 1, None, 0), (swap(up_near), (), 1, None, 1)]
         for d in range(4):
@@ -497,16 +494,17 @@
         up_sources, up_plan = placed_plan(placed)
     else:
         up_sources, up_plan = whole_gather(up_taps_own)
-        stats = stat_gather(stat)
+        stats = [axis_gather(axis_gather(stat[None], "px", 0), "py", 0)]
     py, px = lax.axis_index("py"), lax.axis_index("px")
     edges = jnp.stack(
         [py > 0, py < lax.axis_size("py") - 1, px > 0, px < lax.axis_size("px") - 1]
     ).astype(jnp.int32)
     step = 8
     return pl.pallas_call(
-        lambda *refs: conv2_kernel(up_plan, rows, cols, *refs),
+        lambda *refs: conv2_kernel(up_plan, len(stats), rows, cols, *refs),
         out_shape=jax.ShapeDtypeStruct((frames, 2 * rows, 2 * cols, channels), jnp.bfloat16),
-        in_specs=[pl.BlockSpec(memory_space=pltpu.SMEM), WHOLE, WHOLE, WHOLE]
+        in_specs=[pl.BlockSpec(memory_space=pltpu.SMEM), WHOLE, WHOLE]
+        + [WHOLE] * len(stats)
         + [ANY] * len(up_sources),
         out_specs=ANY,
         scratch_shapes=[
@@ -525,7 +523,7 @@
             transcendentals=0,
         ),
         name="conv2",
-    )(edges, hidden, stats, second_gain.reshape(1, channels), *up_sources)
+    )(edges, hidden, second_gain.reshape(1, channels), *stats, *up_sources)
 
 
 def solution(mesh):

time: 107 us -> 106 us (level)
  waiting for transfers between devices: 28.6 us -> 32.1 us
  Pallas kernels: 33.6 us -> 30.5 us
    pallas_call x1, Pallas kernels: 16.1 us -> 12.9 us  [local(): pl.pallas_call(lambda *refs: conv1_kernel(res_plan, rows, cols, *refs), o...]
    ppermute x6, waiting for transfers between devices: 13.5 us -> 16.6 us  [to_clips(): lax.ppermute(piece, 'clip', xor_pairs('clip', d))]
    unnamed x55 -> x51, local copies, waits for them, and re-layouts: 3.54 us -> 2.55 us
  transfers between devices with their start and end apart: 31 -> 31, of which waited for: 14 -> 13; matrix products, arithmetic and copies ran while one was open for 11% -> 10% of each run, Pallas kernels for 17% -> 14%
where the time goes in v4:
time: 106 us
  waiting for transfers between devices  32.1 us (30%)
  Pallas kernels  30.5 us (29%)
  starting transfers between devices  28.3 us (27%)
  local copies, waits for them, and re-layouts  9.04 us (9%)
  other arithmetic  5.42 us (5%)
    ppermute x6, waiting for transfers between devices, to_clips(): lax.ppermute(piece, 'clip', xor_pairs('clip', d))  16.6 us
    pallas_call x1, Pallas kernels, local(): pl.pallas_call(lambda *refs: conv2_kernel(up_plan, len(stats), rows, cols...  15.9 us
    ppermute x9, starting transfers between devices, to_z(): return lax.ppermute(part, 'py', xor_pairs('py', bits))  15 us
    pallas_call x1, Pallas kernels, local(): pl.pallas_call(lambda *refs: conv1_kernel(res_plan, rows, cols, *refs), o...  12.9 us
    ppermute x9, waiting for transfers between devices, to_z(): return lax.ppermute(part, 'py', xor_pairs('py', bits))  9.17 us
    ppermute x6, starting transfers between devices, to_clips(): lax.ppermute(piece, 'clip', xor_pairs('clip', d))  7.11 us
    ppermute x13, waiting for transfers between devices, swap(): return lax.ppermute(piece, 'px', xor_pairs('px', 1))  4.58 us
    ppermute x3, starting transfers between devices, stat_gather(): lax.ppermute(pair, 'py', xor_pairs('py', j))  4.39 us
  transfers between devices with their start and end apart: 31, of which 13 were waited for; matrix products, arithmetic and copies ran while one was open for 10% of the time, Pallas kernels for 14%

profile of v4, /device:TPU:0, one launch (start us, length us, event | category | flops | bytes accessed | tf_op | source)
XLA Modules:
  0.0 106.0 jit_solution(3914977159323647133)
XLA Ops:
  0.0 1.0 multiply_convert_fusion
  1.2 3.1 %collective-permute-start.2 = (bf16[12,512]{1,0:T(8,128)(2,1)S(1)}, bf16[12,512]{1,0:T(8,128)(2,1)S(1)}, u32[]{:S(2)}, u32[]{:S(2)}) collective-permute-start(bf16[12,512]{1,0:T(8,128)(2,1)S(1)} %reshape.88), channel_id=1, source_target_pairs={{0,2},{2,0},{4,6},{6,4},{1,3},{3,1},{5,7},{7,5},{8,10},{10,8},{12,... | collective-permute-start | bytes 36872 | tf_op jit(solution)/shard_map/ppermute | solution.py:365
  4.3 2.6 %collective-permute-start.1 = (bf16[12,512]{1,0:T(8,128)(2,1)S(1)}, bf16[12,512]{1,0:T(8,128)(2,1)S(1)}, u32[]{:S(2)}, u32[]{:S(2)}) collective-permute-start(bf16[12,512]{1,0:T(8,128)(2,1)S(1)} %reshape.88), channel_id=1, source_target_pairs={{0,4},{2,6},{4,0},{6,2},{1,5},{3,7},{5,1},{7,3},{8,12},{10,14},{12... | collective-permute-start | bytes 36872 | tf_op jit(solution)/shard_map/ppermute | solution.py:365
  6.8 0.9 constant_dynamic-slice_fusion
  7.8 3.9 %collective-permute-start.8 = (bf16[9,64,128]{2,1,0:T(8,128)(2,1)S(1)}, bf16[9,64,128]{2,1,0:T(8,128)(2,1)S(1)}, u32[]{:S(2)}, u32[]{:S(2)}) collective-permute-start(bf16[9,64,128]{2,1,0:T(8,128)(2,1)S(1)} %constant_dynamic-slice_fusion), channel_id=1, source_target_pairs={{0,6},{2,4},{4,2},{6,0},{1,7},{3,5},{5,3},{7,1},{8,14},{10,12},{12... | collective-permute-start | bytes 442376 | tf_op jit(solution)/shard_map/ppermute | solution.py:365
  11.7 1.0 add_bitcast_fusion.refs_1_
  13.3 2.6 %reshape.94 = bf16[64,4,2,2,512]{4,3,2,1,0:T(2,128)(2,1)S(1)} reshape(bf16[64,4,4,512]{3,2,1,0:T(4,128)(2,1)} %param.12) | data formatting | bytes 2097152 | tf_op jit(solution)/shard_map/reshape | solution.py:339
  22.4 1.7 %prep.1.refs_2_ = f32[16,512]{1,0:T(8,128)S(1)} custom-call(f32[8,8832]{1,0:T(8,128)S(1)} %pad_convert_fusion.refs_0_, bf16[80,640]{1,0:T(8,128)(2,1)S(1)} %add_bitcast_fusion.refs_1_, f32[1,512]{1,0:T(1,128)S(1)} %bitcast.30), custom_call_target="tpu_custom_call" | custom-call | tf_op jit(solution)/shard_map/prep/pallas_call | solution.py:179
  24.7 2.4 %collective-permute-start.18 = (bf16[16,64,128]{2,1,0:T(8,128)(2,1)S(1)}, bf16[16,64,128]{2,1,0:T(8,128)(2,1)S(1)}, u32[]{:S(2)}, u32[]{:S(2)}) collective-permute-start(bf16[16,64,128]{2,1,0:T(8,128)(2,1)S(1)} %constant_dynamic-slice_fusion.1), channel_id=1, source_target_pairs={{0,4},{2,6},{4,0},{6,2},{1,5},{3,7},{5,1},{7,3},{8,12},{10,14},{12... | collective-permute-start | bytes 786440 | tf_op jit(solution)/shard_map/ppermute | solution.py:365
  27.1 2.5 %collective-permute-start.14 = (bf16[3,9,64,128]{3,2,1,0:T(8,128)(2,1)S(1)}, bf16[3,9,64,128]{3,2,1,0:T(8,128)(2,1)S(1)}, u32[]{:S(2)}, u32[]{:S(2)}) collective-permute-start(bf16[3,9,64,128]{3,2,1,0:T(8,128)(2,1)S(1)} %pad_maximum_fusion.1.refs_5_), channel_id=1, source_target_pairs={{0,24},{8,16},{16,8},{24,0},{1,25},{9,17},{17,9},{25,1},{2,26},{10... | collective-permute-start | bytes 1327112 | tf_op jit(solution)/shard_map/ppermute | solution.py:369
  30.7 9.2 %collective-permute-done.18 = bf16[16,64,128]{2,1,0:T(8,128)(2,1)S(1)} collective-permute-done((bf16[16,64,128]{2,1,0:T(8,128)(2,1)S(1)}, bf16[16,64,128]{2,1,0:T(8,128)(2,1)S(1)}, u32[]{:S(2)}, u32[]{:S(2)}) %collective-permute-start.18) | collective-permute-done | bytes 262176 | tf_op jit(solution)/shard_map/ppermute | solution.py:365
  41.2 8.6 %collective-permute-done.12.refs_9_ = bf16[3,9,64,128]{3,2,1,0:T(8,128)(2,1)S(1)} collective-permute-done((bf16[3,9,64,128]{3,2,1,0:T(8,128)(2,1)S(1)}, bf16[3,9,64,128]{3,2,1,0:T(8,128)(2,1)S(1)}, u32[]{:S(2)}, u32[]{:S(2)}) %collective-permute-start.12) | collective-permute-done | bytes 442400 | tf_op jit(solution)/shard_map/ppermute | solution.py:369
  50.3 2.0 %collective-permute-start.17 = (bf16[16,64,512]{2,1,0:T(8,128)(2,1)S(1)}, bf16[16,64,512]{2,1,0:T(8,128)(2,1)S(1)}, u32[]{:S(2)}, u32[]{:S(2)}) collective-permute-start(bf16[16,64,512]{2,1,0:T(8,128)(2,1)S(1)} %bitcast.33), channel_id=1, source_target_pairs={{0,2},{2,0},{4,6},{6,4},{1,3},{3,1},{5,7},{7,5},{8,10},{10,8},{12,... | collective-permute-start | bytes 3145736 | tf_op jit(solution)/shard_map/ppermute | solution.py:365
  52.3 1.8 %collective-permute-start.22 = (bf16[2,16,64,128]{3,2,1,0:T(8,128)(2,1)S(1)}, bf16[2,16,64,128]{3,2,1,0:T(8,128)(2,1)}, u32[]{:S(2)}, u32[]{:S(2)}) collective-permute-start(bf16[2,16,64,128]{3,2,1,0:T(8,128)(2,1)S(1)} %pad_maximum_fusion.refs_11_), channel_id=1, source_target_pairs={{0,24},{8,16},{16,8},{24,0},{1,25},{9,17},{17,9},{25,1},{2,26},{10... | collective-permute-start | bytes 1572872 | tf_op jit(solution)/shard_map/ppermute | solution.py:369
  54.2 1.2 %collective-permute-start.21 = (bf16[2,16,64,128]{3,2,1,0:T(8,128)(2,1)S(1)}, bf16[2,16,64,128]{3,2,1,0:T(8,128)(2,1)}, u32[]{:S(2)}, u32[]{:S(2)}) collective-permute-start(bf16[2,16,64,128]{3,2,1,0:T(8,128)(2,1)S(1)} %pad_maximum_fusion.refs_11_), channel_id=1, source_target_pairs={{0,16},{8,24},{16,0},{24,8},{1,17},{9,25},{17,1},{25,9},{2,18},{10... | collective-permute-start | bytes 1572872 | tf_op jit(solution)/shard_map/ppermute | solution.py:369
  56.9 12.9 %conv1.1 = (bf16[1440,512]{1,0:T(8,128)(2,1)}, f32[8,512]{1,0:T(8,128)}) custom-call(f32[8,1792]{1,0:T(8,128)} %pad_convert_fusion.1.refs_0_, bf16[80,640]{1,0:T(8,128)(2,1)} %copy-done, f32[16,512]{1,0:T(8,128)} %copy-done.1, bf16[9,64,512]{2,1,0:T(8,128)(2,1)} %bitcast.42, bf16[9,64,512]{2,1,0:T(8,128)(2,1)} %collective-permute-done.4.refs_4_, ...), custom_call_target="tpu_custom_call" | custom-call | flops 6794772480 | bytes 12582912 | tf_op jit(solution)/shard_map/conv1/pallas_call | solution.py:464
  69.9 1.4 %collective-permute-done.16 = f32[8,512]{1,0:T(8,128)S(1)} collective-permute-done((f32[8,512]{1,0:T(8,128)}, f32[8,512]{1,0:T(8,128)S(1)}, u32[]{:S(2)}, u32[]{:S(2)}) %collective-permute-start.16) | collective-permute-done | bytes 16416 | tf_op jit(solution)/shard_map/ppermute | solution.py:349
  71.3 7.0 %collective-permute-done.21.refs_15_ = bf16[2,16,64,128]{3,2,1,0:T(8,128)(2,1)} collective-permute-done((bf16[2,16,64,128]{3,2,1,0:T(8,128)(2,1)S(1)}, bf16[2,16,64,128]{3,2,1,0:T(8,128)(2,1)}, u32[]{:S(2)}, u32[]{:S(2)}) %collective-permute-start.21) | collective-permute-done | bytes 524320 | tf_op jit(solution)/shard_map/ppermute | solution.py:369
  79.4 1.5 %collective-permute-start.24 = (f32[2,8,512]{2,1,0:T(8,128)S(1)}, f32[2,8,512]{2,1,0:T(8,128)S(1)}, u32[]{:S(2)}, u32[]{:S(2)}) collective-permute-start(f32[2,8,512]{2,1,0:T(8,128)S(1)} %pad_maximum_fusion.5.refs_3_), channel_id=1, source_target_pairs={{0,4},{2,6},{4,0},{6,2},{1,5},{3,7},{5,1},{7,3},{8,12},{10,14},{12... | collective-permute-start | bytes 98312 | tf_op jit(solution)/shard_map/ppermute | solution.py:430
  80.9 2.6 %collective-permute-start.23 = (f32[2,8,512]{2,1,0:T(8,128)S(1)}, f32[2,8,512]{2,1,0:T(8,128)S(1)}, u32[]{:S(2)}, u32[]{:S(2)}) collective-permute-start(f32[2,8,512]{2,1,0:T(8,128)S(1)} %pad_maximum_fusion.5.refs_3_), channel_id=1, source_target_pairs={{0,2},{2,0},{4,6},{6,4},{1,3},{3,1},{5,7},{7,5},{8,10},{10,8},{12,... | collective-permute-start | bytes 98312 | tf_op jit(solution)/shard_map/ppermute | solution.py:430
  83.5 1.6 %collective-permute-done.25.refs_6_ = f32[2,8,512]{2,1,0:T(8,128)S(1)} collective-permute-done((f32[2,8,512]{2,1,0:T(8,128)S(1)}, f32[2,8,512]{2,1,0:T(8,128)S(1)}, u32[]{:S(2)}, u32[]{:S(2)}) %collective-permute-start.25) | collective-permute-done | bytes 32800 | tf_op jit(solution)/shard_map/ppermute | solution.py:430
  86.4 1.1 %collective-permute-done.28.refs_14_ = bf16[2,16,64,128]{3,2,1,0:T(8,128)(2,1)} collective-permute-done((bf16[2,16,64,128]{3,2,1,0:T(8,128)(2,1)}, bf16[2,16,64,128]{3,2,1,0:T(8,128)(2,1)}, u32[]{:S(2)}, u32[]{:S(2)}) %collective-permute-start.28) | collective-permute-done | bytes 524320 | tf_op jit(solution)/shard_map/ppermute | solution.py:349
  89.0 0.9 copy-done.13
  89.9 15.9 %conv2.1 = bf16[2,32,64,512]{3,2,1,0:T(8,128)(2,1)} custom-call(s32[4]{0:T(128)} %add_convert_fusion.1.refs_0_, bf16[1440,512]{1,0:T(8,128)(2,1)} %get-tuple-element.26.refs_1_, f32[1,512]{1,0:T(1,128)} %bitcast.46, f32[2,8,512]{2,1,0:T(8,128)} %copy-done.9, f32[2,8,512]{2,1,0:T(8,128)} %copy-done.24, f32[2,8,512]{2,1,0:T(8,128)} %copy-done.23, ...), custom_call_target="tpu_custom_call" | custom-call | flops 8589934592 | bytes 16777216 | tf_op jit(solution)/shard_map/conv2/pallas_call | solution.py:503
  (130 shorter events, 16.0 us)
Async XLA Ops:
  1.2 16.4 %collective-permute-start.2 = (bf16[12,512]{1,0:T(8,128)(2,1)S(1)}, bf16[12,512]{1,0:T(8,128)(2,1)S(1)}, u32[]{:S(2)}, u32[]{:S(2)}) collective-permute-start(bf16[12,512]{1,0:T(8,128)(2,1)S(1)} %reshape.88), channel_id=1, source_target_pairs={{0,2},{2,0},{4,6},{6,4},{1,3},{3,1},{5,7},{7,5},{8,10},{10,8},{12,... | collective-permute-start | bytes 36872 | tf_op jit(solution)/shard_map/ppermute | solution.py:365
  4.3 12.4 %collective-permute-start.1 = (bf16[12,512]{1,0:T(8,128)(2,1)S(1)}, bf16[12,512]{1,0:T(8,128)(2,1)S(1)}, u32[]{:S(2)}, u32[]{:S(2)}) collective-permute-start(bf16[12,512]{1,0:T(8,128)(2,1)S(1)} %reshape.88), channel_id=1, source_target_pairs={{0,4},{2,6},{4,0},{6,2},{1,5},{3,7},{5,1},{7,3},{8,12},{10,14},{12... | collective-permute-start | bytes 36872 | tf_op jit(solution)/shard_map/ppermute | solution.py:365
  6.8 10.5 %collective-permute-start = (bf16[12,512]{1,0:T(8,128)(2,1)S(1)}, bf16[12,512]{1,0:T(8,128)(2,1)S(1)}, u32[]{:S(2)}, u32[]{:S(2)}) collective-permute-start(bf16[12,512]{1,0:T(8,128)(2,1)S(1)} %reshape.88), channel_id=1, source_target_pairs={{0,6},{2,4},{4,2},{6,0},{1,7},{3,5},{5,3},{7,1},{8,14},{10,12},{12... | collective-permute-start | bytes 36872 | tf_op jit(solution)/shard_map/ppermute | solution.py:365
  7.8 16.9 %collective-permute-start.8 = (bf16[9,64,128]{2,1,0:T(8,128)(2,1)S(1)}, bf16[9,64,128]{2,1,0:T(8,128)(2,1)S(1)}, u32[]{:S(2)}, u32[]{:S(2)}) collective-permute-start(bf16[9,64,128]{2,1,0:T(8,128)(2,1)S(1)} %constant_dynamic-slice_fusion), channel_id=1, source_target_pairs={{0,6},{2,4},{4,2},{6,0},{1,7},{3,5},{5,3},{7,1},{8,14},{10,12},{12... | collective-permute-start | bytes 442376 | tf_op jit(solution)/shard_map/ppermute | solution.py:365
  11.7 13.0 %collective-permute-start.7 = (bf16[9,64,128]{2,1,0:T(8,128)(2,1)S(1)}, bf16[9,64,128]{2,1,0:T(8,128)(2,1)S(1)}, u32[]{:S(2)}, u32[]{:S(2)}) collective-permute-start(bf16[9,64,128]{2,1,0:T(8,128)(2,1)S(1)} %constant_dynamic-slice_fusion), channel_id=1, source_target_pairs={{0,4},{2,6},{4,0},{6,2},{1,5},{3,7},{5,1},{7,3},{8,12},{10,14},{12... | collective-permute-start | bytes 442376 | tf_op jit(solution)/shard_map/ppermute | solution.py:365
  16.7 8.0 %collective-permute-start.6 = (bf16[9,64,128]{2,1,0:T(8,128)(2,1)S(1)}, bf16[9,64,128]{2,1,0:T(8,128)(2,1)S(1)}, u32[]{:S(2)}, u32[]{:S(2)}) collective-permute-start(bf16[9,64,128]{2,1,0:T(8,128)(2,1)S(1)} %constant_dynamic-slice_fusion), channel_id=1, source_target_pairs={{0,2},{2,0},{4,6},{6,4},{1,3},{3,1},{5,7},{7,5},{8,10},{10,8},{12,... | collective-permute-start | bytes 442376 | tf_op jit(solution)/shard_map/ppermute | solution.py:365
  18.4 4.0 %collective-permute-start.4 = (bf16[9,64,512]{2,1,0:T(8,128)(2,1)S(1)}, bf16[9,64,512]{2,1,0:T(8,128)(2,1)}, u32[]{:S(2)}, u32[]{:S(2)}) collective-permute-start(bf16[9,64,512]{2,1,0:T(8,128)(2,1)S(1)} %bitcast.43), channel_id=1, source_target_pairs={{0,1},{1,0},{2,3},{3,2},{4,5},{5,4},{6,7},{7,6},{8,9},{9,8},{10,11... | collective-permute-start | bytes 1769480 | tf_op jit(solution)/shard_map/ppermute | solution.py:349
  24.7 15.1 %collective-permute-start.18 = (bf16[16,64,128]{2,1,0:T(8,128)(2,1)S(1)}, bf16[16,64,128]{2,1,0:T(8,128)(2,1)S(1)}, u32[]{:S(2)}, u32[]{:S(2)}) collective-permute-start(bf16[16,64,128]{2,1,0:T(8,128)(2,1)S(1)} %constant_dynamic-slice_fusion.1), channel_id=1, source_target_pairs={{0,4},{2,6},{4,0},{6,2},{1,5},{3,7},{5,1},{7,3},{8,12},{10,14},{12... | collective-permute-start | bytes 786440 | tf_op jit(solution)/shard_map/ppermute | solution.py:365
  27.1 14.0 %collective-permute-start.14 = (bf16[3,9,64,128]{3,2,1,0:T(8,128)(2,1)S(1)}, bf16[3,9,64,128]{3,2,1,0:T(8,128)(2,1)S(1)}, u32[]{:S(2)}, u32[]{:S(2)}) collective-permute-start(bf16[3,9,64,128]{3,2,1,0:T(8,128)(2,1)S(1)} %pad_maximum_fusion.1.refs_5_), channel_id=1, source_target_pairs={{0,24},{8,16},{16,8},{24,0},{1,25},{9,17},{17,9},{25,1},{2,26},{10... | collective-permute-start | bytes 1327112 | tf_op jit(solution)/shard_map/ppermute | solution.py:369
  29.7 20.1 %collective-permute-start.12 = (bf16[3,9,64,128]{3,2,1,0:T(8,128)(2,1)S(1)}, bf16[3,9,64,128]{3,2,1,0:T(8,128)(2,1)S(1)}, u32[]{:S(2)}, u32[]{:S(2)}) collective-permute-start(bf16[3,9,64,128]{3,2,1,0:T(8,128)(2,1)S(1)} %pad_maximum_fusion.1.refs_5_), channel_id=1, source_target_pairs={{0,16},{8,24},{16,0},{24,8},{1,17},{9,25},{17,1},{25,9},{2,18},{10... | collective-permute-start | bytes 1327112 | tf_op jit(solution)/shard_map/ppermute | solution.py:369
  30.2 19.7 %collective-permute-start.10 = (bf16[3,9,64,128]{3,2,1,0:T(8,128)(2,1)S(1)}, bf16[3,9,64,128]{3,2,1,0:T(8,128)(2,1)S(1)}, u32[]{:S(2)}, u32[]{:S(2)}) collective-permute-start(bf16[3,9,64,128]{3,2,1,0:T(8,128)(2,1)S(1)} %pad_maximum_fusion.1.refs_5_), channel_id=1, source_target_pairs={{0,8},{8,0},{16,24},{24,16},{1,9},{9,1},{17,25},{25,17},{2,10},{10... | collective-permute-start | bytes 1327112 | tf_op jit(solution)/shard_map/ppermute | solution.py:369
  39.8 10.4 %collective-permute-start.19 = (bf16[16,64,128]{2,1,0:T(8,128)(2,1)S(1)}, bf16[16,64,128]{2,1,0:T(8,128)(2,1)S(1)}, u32[]{:S(2)}, u32[]{:S(2)}) collective-permute-start(bf16[16,64,128]{2,1,0:T(8,128)(2,1)S(1)} %collective-permute-done.18), channel_id=1, source_target_pairs={{0,2},{2,0},{4,6},{6,4},{1,3},{3,1},{5,7},{7,5},{8,10},{10,8},{12,... | collective-permute-start | bytes 786440 | tf_op jit(solution)/shard_map/ppermute | solution.py:365
  40.3 12.1 %collective-permute-start.9 = (bf16[3,9,64,128]{3,2,1,0:T(8,128)(2,1)S(1)}, bf16[3,9,64,128]{3,2,1,0:T(8,128)(2,1)S(1)}, u32[]{:S(2)}, u32[]{:S(2)}) collective-permute-start(bf16[3,9,64,128]{3,2,1,0:T(8,128)(2,1)S(1)} %pad_maximum_fusion.1.refs_5_), channel_id=1, source_target_pairs={{0,1},{1,0},{2,3},{3,2},{4,5},{5,4},{6,7},{7,6},{8,9},{9,8},{10,11... | collective-permute-start | bytes 1327112 | tf_op jit(solution)/shard_map/ppermute | solution.py:349
  41.2 13.0 %collective-permute-start.15 = (bf16[3,9,64,128]{3,2,1,0:T(8,128)(2,1)S(1)}, bf16[3,9,64,128]{3,2,1,0:T(8,128)(2,1)S(1)}, u32[]{:S(2)}, u32[]{:S(2)}) collective-permute-start(bf16[3,9,64,128]{3,2,1,0:T(8,128)(2,1)S(1)} %collective-permute-done.14.refs_11_), channel_id=1, source_target_pairs={{0,1},{1,0},{2,3},{3,2},{4,5},{5,4},{6,7},{7,6},{8,9},{9,8},{10,11... | collective-permute-start | bytes 1327112 | tf_op jit(solution)/shard_map/ppermute | solution.py:349
  49.7 5.6 %collective-permute-start.13 = (bf16[3,9,64,128]{3,2,1,0:T(8,128)(2,1)S(1)}, bf16[3,9,64,128]{3,2,1,0:T(8,128)(2,1)S(1)}, u32[]{:S(2)}, u32[]{:S(2)}) collective-permute-start(bf16[3,9,64,128]{3,2,1,0:T(8,128)(2,1)S(1)} %collective-permute-done.12.refs_9_), channel_id=1, source_target_pairs={{0,1},{1,0},{2,3},{3,2},{4,5},{5,4},{6,7},{7,6},{8,9},{9,8},{10,11... | collective-permute-start | bytes 1327112 | tf_op jit(solution)/shard_map/ppermute | solution.py:349
  49.8 6.1 %collective-permute-start.11 = (bf16[3,9,64,128]{3,2,1,0:T(8,128)(2,1)S(1)}, bf16[3,9,64,128]{3,2,1,0:T(8,128)(2,1)S(1)}, u32[]{:S(2)}, u32[]{:S(2)}) collective-permute-start(bf16[3,9,64,128]{3,2,1,0:T(8,128)(2,1)S(1)} %collective-permute-done.10.refs_7_), channel_id=1, source_target_pairs={{0,1},{1,0},{2,3},{3,2},{4,5},{5,4},{6,7},{7,6},{8,9},{9,8},{10,11... | collective-permute-start | bytes 1327112 | tf_op jit(solution)/shard_map/ppermute | solution.py:349
  50.3 28.1 %collective-permute-start.17 = (bf16[16,64,512]{2,1,0:T(8,128)(2,1)S(1)}, bf16[16,64,512]{2,1,0:T(8,128)(2,1)S(1)}, u32[]{:S(2)}, u32[]{:S(2)}) collective-permute-start(bf16[16,64,512]{2,1,0:T(8,128)(2,1)S(1)} %bitcast.33), channel_id=1, source_target_pairs={{0,2},{2,0},{4,6},{6,4},{1,3},{3,1},{5,7},{7,5},{8,10},{10,8},{12,... | collective-permute-start | bytes 3145736 | tf_op jit(solution)/shard_map/ppermute | solution.py:365
  52.3 18.9 %collective-permute-start.22 = (bf16[2,16,64,128]{3,2,1,0:T(8,128)(2,1)S(1)}, bf16[2,16,64,128]{3,2,1,0:T(8,128)(2,1)}, u32[]{:S(2)}, u32[]{:S(2)}) collective-permute-start(bf16[2,16,64,128]{3,2,1,0:T(8,128)(2,1)S(1)} %pad_maximum_fusion.refs_11_), channel_id=1, source_target_pairs={{0,24},{8,16},{16,8},{24,0},{1,25},{9,17},{17,9},{25,1},{2,26},{10... | collective-permute-start | bytes 1572872 | tf_op jit(solution)/shard_map/ppermute | solution.py:369
  54.2 24.1 %collective-permute-start.21 = (bf16[2,16,64,128]{3,2,1,0:T(8,128)(2,1)S(1)}, bf16[2,16,64,128]{3,2,1,0:T(8,128)(2,1)}, u32[]{:S(2)}, u32[]{:S(2)}) collective-permute-start(bf16[2,16,64,128]{3,2,1,0:T(8,128)(2,1)S(1)} %pad_maximum_fusion.refs_11_), channel_id=1, source_target_pairs={{0,16},{8,24},{16,0},{24,8},{1,17},{9,25},{17,1},{25,9},{2,18},{10... | collective-permute-start | bytes 1572872 | tf_op jit(solution)/shard_map/ppermute | solution.py:369
  55.4 23.0 %collective-permute-start.20 = (bf16[2,16,64,128]{3,2,1,0:T(8,128)(2,1)S(1)}, bf16[2,16,64,128]{3,2,1,0:T(8,128)(2,1)}, u32[]{:S(2)}, u32[]{:S(2)}) collective-permute-start(bf16[2,16,64,128]{3,2,1,0:T(8,128)(2,1)S(1)} %pad_maximum_fusion.refs_11_), channel_id=1, source_target_pairs={{0,8},{8,0},{16,24},{24,16},{1,9},{9,1},{17,25},{25,17},{2,10},{10... | collective-permute-start | bytes 1572872 | tf_op jit(solution)/shard_map/ppermute | solution.py:369
  78.4 10.6 %collective-permute-start.26 = (bf16[16,64,512]{2,1,0:T(8,128)(2,1)S(1)}, bf16[16,64,512]{2,1,0:T(8,128)(2,1)S(1)}, u32[]{:S(2)}, u32[]{:S(2)}) collective-permute-start(bf16[16,64,512]{2,1,0:T(8,128)(2,1)S(1)} %collective-permute-done.17.refs_9_), channel_id=1, source_target_pairs={{0,1},{1,0},{2,3},{3,2},{4,5},{5,4},{6,7},{7,6},{8,9},{9,8},{10,11... | collective-permute-start | bytes 3145736 | tf_op jit(solution)/shard_map/ppermute | solution.py:349
  79.1 6.0 %collective-permute-start.25 = (f32[2,8,512]{2,1,0:T(8,128)S(1)}, f32[2,8,512]{2,1,0:T(8,128)S(1)}, u32[]{:S(2)}, u32[]{:S(2)}) collective-permute-start(f32[2,8,512]{2,1,0:T(8,128)S(1)} %pad_maximum_fusion.5.refs_3_), channel_id=1, source_target_pairs={{0,6},{2,4},{4,2},{6,0},{1,7},{3,5},{5,3},{7,1},{8,14},{10,12},{12... | collective-permute-start | bytes 98312 | tf_op jit(solution)/shard_map/ppermute | solution.py:430
  79.4 5.9 %collective-permute-start.24 = (f32[2,8,512]{2,1,0:T(8,128)S(1)}, f32[2,8,512]{2,1,0:T(8,128)S(1)}, u32[]{:S(2)}, u32[]{:S(2)}) collective-permute-start(f32[2,8,512]{2,1,0:T(8,128)S(1)} %pad_maximum_fusion.5.refs_3_), channel_id=1, source_target_pairs={{0,4},{2,6},{4,0},{6,2},{1,5},{3,7},{5,1},{7,3},{8,12},{10,14},{12... | collective-permute-start | bytes 98312 | tf_op jit(solution)/shard_map/ppermute | solution.py:430
  80.9 4.8 %collective-permute-start.23 = (f32[2,8,512]{2,1,0:T(8,128)S(1)}, f32[2,8,512]{2,1,0:T(8,128)S(1)}, u32[]{:S(2)}, u32[]{:S(2)}) collective-permute-start(f32[2,8,512]{2,1,0:T(8,128)S(1)} %pad_maximum_fusion.5.refs_3_), channel_id=1, source_target_pairs={{0,2},{2,0},{4,6},{6,4},{1,3},{3,1},{5,7},{7,5},{8,10},{10,8},{12,... | collective-permute-start | bytes 98312 | tf_op jit(solution)/shard_map/ppermute | solution.py:430
  (32 other events, 259.9 us)

commit v5 on v4

--- a/solution.py
+++ b/solution.py
@@ -234,7 +234,7 @@
     stat_ref[2:8, :] = jnp.zeros((6, channels), jnp.float32)
 
 
-def conv2_kernel(copy_plan, stat_count, rows, cols, edge_ref, hid_ref, gain_ref, *refs):
+def conv2_kernel(copy_plan, stat_count, rows, cols, hid_ref, gain_ref, *refs):
     stat_refs, refs = refs[:stat_count], refs[stat_count:]
     *sources, out_ref, weight, wide, shifted, woven, result, sems, out_sem = refs
     row_len = 2 * COL
@@ -260,7 +260,9 @@
 
     place = lax.broadcasted_iota(jnp.int32, (row_len, channels), 0)
     place = jnp.where(place >= COL, place - COL, place)
-    top, bottom, left, right = (edge_ref[i].astype(jnp.float32) for i in range(4))
+    py, px = lax.axis_index("py"), lax.axis_index("px")
+    inside = (py > 0, py < lax.axis_size("py") - 1, px > 0, px < lax.axis_size("px") - 1)
+    top, bottom, left, right = (jnp.where(one, 1.0, 0.0) for one in inside)
     keep = jnp.where(place == 0, left, jnp.where(place == cols + 1, right, 1.0))
 
     def normalise(line, _):
@@ -280,7 +282,7 @@
     for copy in copies:
         copy.wait()
 
-    step = 8
+    step = 16
     size = step * 2 * cols
 
     for part in range(rows // step):
@@ -290,15 +292,16 @@
                 acc = None
                 for row_kernel, row_offset in up_taps[row_phase]:
                     first = (line + row_offset) * (2 * cols)
-                    tap = 4 * row_kernel + 2 * col_phase
-                    product = jnp.dot(
-                        shifted[
-                            pl.ds(first, size), col_phase * channels : (col_phase + 2) * channels
-                        ],
-                        weight[tap : tap + 2].reshape(2 * channels, channels),
-                        preferred_element_type=jnp.float32,
-                    )
-                    acc = product if acc is None else acc + product
+                    for col_kernel, col_offset in up_taps[col_phase]:
+                        product = jnp.dot(
+                            shifted[
+                                pl.ds(first, size),
+                                col_offset * channels : (col_offset + 1) * channels,
+                            ],
+                            weight[4 * row_kernel + col_kernel],
+                            preferred_element_type=jnp.float32,
+                        )
+                        acc = product if acc is None else acc + product
                 for lane in range(channels // 128):
                     woven[row_phase, lane, pl.ds(col_phase, size, stride=2), :] = acc[
                         :, 128 * lane : 128 * lane + 128
@@ -334,12 +337,6 @@
     return jnp.transpose(weight, (1, 2, 0, 3)).reshape(-1, weight.shape[0], weight.shape[3])
 
 
-def paired_taps(weight):
-    rows, _, _, width = weight.shape
-    halves = weight.reshape(rows, 4, 2, 2, width)[:, :, ::-1, ::-1, :]
-    return jnp.transpose(halves, (1, 3, 2, 0, 4)).reshape(16, rows, width)
-
-
 def column_part(weight):
     width = weight.shape[2] // lax.axis_size("clip")
     return lax.dynamic_slice_in_dim(weight, lax.axis_index("clip") * width, width, axis=2)
@@ -438,7 +435,7 @@
     dims, frames, rows, cols = fsq_codes.shape
     channels = in_weight.shape[3]
     row_len = frames * COL
-    res_taps, up_taps_own = tap_major(res_weight), paired_taps(up_weight)
+    res_taps, up_taps_own = tap_major(res_weight), tap_major(up_weight)
     paired = tuple(lax.axis_size(axis) for axis in ("clip", "py", "px")) == (4, 4, 2)
     if paired:
         codes = code_gather(code_values(fsq_codes))
@@ -495,15 +492,11 @@
     else:
         up_sources, up_plan = whole_gather(up_taps_own)
         stats = [axis_gather(axis_gather(stat[None], "px", 0), "py", 0)]
-    py, px = lax.axis_index("py"), lax.axis_index("px")
-    edges = jnp.stack(
-        [py > 0, py < lax.axis_size("py") - 1, px > 0, px < lax.axis_size("px") - 1]
-    ).astype(jnp.int32)
-    step = 8
+    step = 16
     return pl.pallas_call(
         lambda *refs: conv2_kernel(up_plan, len(stats), rows, cols, *refs),
         out_shape=jax.ShapeDtypeStruct((frames, 2 * rows, 2 * cols, channels), jnp.bfloat16),
-        in_specs=[pl.BlockSpec(memory_space=pltpu.SMEM), WHOLE, WHOLE]
+        in_specs=[WHOLE, WHOLE]
         + [WHOLE] * len(stats)
         + [ANY] * len(up_sources),
         out_specs=ANY,
@@ -523,7 +516,7 @@
             transcendentals=0,
         ),
         name="conv2",
-    )(edges, hidden, second_gain.reshape(1, channels), *stats, *up_sources)
+    )(hidden, second_gain.reshape(1, channels), *stats, *up_sources)
 
 
 def solution(mesh):

time: 106 us -> 105 us (level)
  local copies, waits for them, and re-layouts: 9.04 us -> 6.38 us
  waiting for transfers between devices: 32.1 us -> 33.4 us
    reshape x2 -> x0, local copies, waits for them, and re-layouts: 3.19 us -> none  [paired_taps(): halves = weight.reshape(rows, 4, 2, 2, width)[:, :, ::-1, ::-1, :]]
    transpose x0 -> x1, local copies, waits for them, and re-layouts: none -> 1.82 us  [tap_major(): jnp.transpose(weight, (1, 2, 0, 3))]
    unnamed x51 -> x55, local copies, waits for them, and re-layouts: 2.55 us -> 2.03 us
  transfers between devices with their start and end apart: 31 -> 31, of which waited for: 13 -> 14; matrix products, arithmetic and copies ran while one was open for 10% -> 8% of each run, Pallas kernels for 14% -> 14%
where the time goes in v5:
time: 105 us
  waiting for transfers between devices  33.4 us (32%)
  Pallas kernels  31.2 us (30%)
  starting transfers between devices  28.3 us (27%)
  local copies, waits for them, and re-layouts  6.38 us (6%)
  other arithmetic  5.19 us (5%)
    ppermute x6, waiting for transfers between devices, to_clips(): lax.ppermute(piece, 'clip', xor_pairs('clip', d))  17.2 us
    pallas_call x1, Pallas kernels, local(): pl.pallas_call(lambda *refs: conv2_kernel(up_plan, len(stats), rows, cols...  16.6 us
    ppermute x9, starting transfers between devices, to_z(): return lax.ppermute(part, 'py', xor_pairs('py', bits))  15 us
    pallas_call x1, Pallas kernels, local(): pl.pallas_call(lambda *refs: conv1_kernel(res_plan, rows, cols, *refs), o...  12.9 us
    ppermute x9, waiting for transfers between devices, to_z(): return lax.ppermute(part, 'py', xor_pairs('py', bits))  9.06 us
    ppermute x6, starting transfers between devices, to_clips(): lax.ppermute(piece, 'clip', xor_pairs('clip', d))  7.11 us
    ppermute x13, waiting for transfers between devices, swap(): return lax.ppermute(piece, 'px', xor_pairs('px', 1))  5.38 us
    ppermute x3, starting transfers between devices, stat_gather(): lax.ppermute(pair, 'py', xor_pairs('py', j))  4.39 us
  transfers between devices with their start and end apart: 31, of which 14 were waited for; matrix products, arithmetic and copies ran while one was open for 8% of the time, Pallas kernels for 14%

profile of v5, /device:TPU:0, one launch (start us, length us, event | category | flops | bytes accessed | tf_op | source)
XLA Modules:
  0.0 105.1 jit_solution(15324765255453531205)
XLA Ops:
  0.0 1.1 %multiply_convert_fusion = bf16[6,2,16,32]{3,2,1,0:T(8,128)(2,1)S(1)} fusion(s32[6,2,16,32]{3,2,1,0:T(8,128)} %param.9, f32[6]{0:T(128)} %constant.90, s32[6]{0:T(128)} %constant.91), kind=kLoop, calls=%fused_computation.15 | loop fusion | flops 24576 | bytes 36912 | tf_op jit(solution)/shard_map/convert_element_type | solution.py:37
  1.2 3.1 %collective-permute-start.2 = (bf16[12,512]{1,0:T(8,128)(2,1)S(1)}, bf16[12,512]{1,0:T(8,128)(2,1)S(1)}, u32[]{:S(2)}, u32[]{:S(2)}) collective-permute-start(bf16[12,512]{1,0:T(8,128)(2,1)S(1)} %reshape.85), channel_id=1, source_target_pairs={{0,2},{2,0},{4,6},{6,4},{1,3},{3,1},{5,7},{7,5},{8,10},{10,8},{12,... | collective-permute-start | bytes 36872 | tf_op jit(solution)/shard_map/ppermute | solution.py:362
  4.3 2.6 %collective-permute-start.1 = (bf16[12,512]{1,0:T(8,128)(2,1)S(1)}, bf16[12,512]{1,0:T(8,128)(2,1)S(1)}, u32[]{:S(2)}, u32[]{:S(2)}) collective-permute-start(bf16[12,512]{1,0:T(8,128)(2,1)S(1)} %reshape.85), channel_id=1, source_target_pairs={{0,4},{2,6},{4,0},{6,2},{1,5},{3,7},{5,1},{7,3},{8,12},{10,14},{12... | collective-permute-start | bytes 36872 | tf_op jit(solution)/shard_map/ppermute | solution.py:362
  7.8 3.9 %collective-permute-start.8 = (bf16[9,64,128]{2,1,0:T(8,128)(2,1)S(1)}, bf16[9,64,128]{2,1,0:T(8,128)(2,1)S(1)}, u32[]{:S(2)}, u32[]{:S(2)}) collective-permute-start(bf16[9,64,128]{2,1,0:T(8,128)(2,1)S(1)} %constant_dynamic-slice_fusion), channel_id=1, source_target_pairs={{0,6},{2,4},{4,2},{6,0},{1,7},{3,5},{5,3},{7,1},{8,14},{10,12},{12... | collective-permute-start | bytes 442376 | tf_op jit(solution)/shard_map/ppermute | solution.py:362
  11.7 1.0 add_bitcast_fusion.refs_1_
  12.7 1.8 %copy.13 = bf16[4,4,64,512]{3,2,1,0:T(8,128)(2,1)S(1)} copy(bf16[4,4,64,512]{3,1,0,2:T(4,128)(2,1)} %bitcast.30) | data formatting | bytes 2097152 | tf_op jit(solution)/shard_map/transpose | solution.py:337
  15.6 1.0 broadcast_select_fusion.5
  21.1 1.7 %prep.1.refs_2_ = f32[16,512]{1,0:T(8,128)S(1)} custom-call(f32[8,8832]{1,0:T(8,128)S(1)} %pad_convert_fusion.refs_0_, bf16[80,640]{1,0:T(8,128)(2,1)S(1)} %add_bitcast_fusion.refs_1_, f32[1,512]{1,0:T(1,128)S(1)} %bitcast.25), custom_call_target="tpu_custom_call" | custom-call | tf_op jit(solution)/shard_map/prep/pallas_call | solution.py:179
  23.4 2.4 %collective-permute-start.18 = (bf16[16,64,128]{2,1,0:T(8,128)(2,1)S(1)}, bf16[16,64,128]{2,1,0:T(8,128)(2,1)S(1)}, u32[]{:S(2)}, u32[]{:S(2)}) collective-permute-start(bf16[16,64,128]{2,1,0:T(8,128)(2,1)S(1)} %constant_dynamic-slice_fusion.1), channel_id=1, source_target_pairs={{0,4},{2,6},{4,0},{6,2},{1,5},{3,7},{5,1},{7,3},{8,12},{10,14},{12... | collective-permute-start | bytes 786440 | tf_op jit(solution)/shard_map/ppermute | solution.py:362
  25.8 2.5 %collective-permute-start.14 = (bf16[3,9,64,128]{3,2,1,0:T(8,128)(2,1)S(1)}, bf16[3,9,64,128]{3,2,1,0:T(8,128)(2,1)S(1)}, u32[]{:S(2)}, u32[]{:S(2)}) collective-permute-start(bf16[3,9,64,128]{3,2,1,0:T(8,128)(2,1)S(1)} %pad_maximum_fusion.1.refs_5_), channel_id=1, source_target_pairs={{0,24},{8,16},{16,8},{24,0},{1,25},{9,17},{17,9},{25,1},{2,26},{10... | collective-permute-start | bytes 1327112 | tf_op jit(solution)/shard_map/ppermute | solution.py:366
  29.4 9.0 %collective-permute-done.18 = bf16[16,64,128]{2,1,0:T(8,128)(2,1)S(1)} collective-permute-done((bf16[16,64,128]{2,1,0:T(8,128)(2,1)S(1)}, bf16[16,64,128]{2,1,0:T(8,128)(2,1)S(1)}, u32[]{:S(2)}, u32[]{:S(2)}) %collective-permute-start.18) | collective-permute-done | bytes 262176 | tf_op jit(solution)/shard_map/ppermute | solution.py:362
  38.8 1.1 %collective-permute-done.14.refs_11_ = bf16[3,9,64,128]{3,2,1,0:T(8,128)(2,1)S(1)} collective-permute-done((bf16[3,9,64,128]{3,2,1,0:T(8,128)(2,1)S(1)}, bf16[3,9,64,128]{3,2,1,0:T(8,128)(2,1)S(1)}, u32[]{:S(2)}, u32[]{:S(2)}) %collective-permute-start.14) | collective-permute-done | bytes 442400 | tf_op jit(solution)/shard_map/ppermute | solution.py:366
  39.9 8.4 %collective-permute-done.12.refs_9_ = bf16[3,9,64,128]{3,2,1,0:T(8,128)(2,1)S(1)} collective-permute-done((bf16[3,9,64,128]{3,2,1,0:T(8,128)(2,1)S(1)}, bf16[3,9,64,128]{3,2,1,0:T(8,128)(2,1)S(1)}, u32[]{:S(2)}, u32[]{:S(2)}) %collective-permute-start.12) | collective-permute-done | bytes 442400 | tf_op jit(solution)/shard_map/ppermute | solution.py:366
  48.8 2.0 %collective-permute-start.17 = (bf16[16,64,512]{2,1,0:T(8,128)(2,1)S(1)}, bf16[16,64,512]{2,1,0:T(8,128)(2,1)S(1)}, u32[]{:S(2)}, u32[]{:S(2)}) collective-permute-start(bf16[16,64,512]{2,1,0:T(8,128)(2,1)S(1)} %bitcast.28), channel_id=1, source_target_pairs={{0,2},{2,0},{4,6},{6,4},{1,3},{3,1},{5,7},{7,5},{8,10},{10,8},{12,... | collective-permute-start | bytes 3145736 | tf_op jit(solution)/shard_map/ppermute | solution.py:362
  50.9 1.8 %collective-permute-start.22 = (bf16[2,16,64,128]{3,2,1,0:T(8,128)(2,1)S(1)}, bf16[2,16,64,128]{3,2,1,0:T(8,128)(2,1)S(1)}, u32[]{:S(2)}, u32[]{:S(2)}) collective-permute-start(bf16[2,16,64,128]{3,2,1,0:T(8,128)(2,1)S(1)} %pad_maximum_fusion.refs_10_), channel_id=1, source_target_pairs={{0,24},{8,16},{16,8},{24,0},{1,25},{9,17},{17,9},{25,1},{2,26},{10... | collective-permute-start | bytes 1572872 | tf_op jit(solution)/shard_map/ppermute | solution.py:366
  52.7 1.2 %collective-permute-start.21 = (bf16[2,16,64,128]{3,2,1,0:T(8,128)(2,1)S(1)}, bf16[2,16,64,128]{3,2,1,0:T(8,128)(2,1)S(1)}, u32[]{:S(2)}, u32[]{:S(2)}) collective-permute-start(bf16[2,16,64,128]{3,2,1,0:T(8,128)(2,1)S(1)} %pad_maximum_fusion.refs_10_), channel_id=1, source_target_pairs={{0,16},{8,24},{16,0},{24,8},{1,17},{9,25},{17,1},{25,9},{2,18},{10... | collective-permute-start | bytes 1572872 | tf_op jit(solution)/shard_map/ppermute | solution.py:366
  54.8 12.9 %conv1.1 = (bf16[1440,512]{1,0:T(8,128)(2,1)}, f32[8,512]{1,0:T(8,128)}) custom-call(f32[8,1792]{1,0:T(8,128)} %pad_convert_fusion.1.refs_0_, bf16[80,640]{1,0:T(8,128)(2,1)} %copy-done, f32[16,512]{1,0:T(8,128)} %copy-done.1, bf16[9,64,512]{2,1,0:T(8,128)(2,1)} %bitcast.38, bf16[9,64,512]{2,1,0:T(8,128)(2,1)} %collective-permute-done.4.refs_4_, ...), custom_call_target="tpu_custom_call" | custom-call | flops 6794772480 | bytes 12582912 | tf_op jit(solution)/shard_map/conv1/pallas_call | solution.py:461
  67.8 1.4 %collective-permute-done.16 = f32[8,512]{1,0:T(8,128)S(1)} collective-permute-done((f32[8,512]{1,0:T(8,128)}, f32[8,512]{1,0:T(8,128)S(1)}, u32[]{:S(2)}, u32[]{:S(2)}) %collective-permute-start.16) | collective-permute-done | bytes 16416 | tf_op jit(solution)/shard_map/ppermute | solution.py:346
  69.2 7.6 %collective-permute-done.21.refs_14_ = bf16[2,16,64,128]{3,2,1,0:T(8,128)(2,1)S(1)} collective-permute-done((bf16[2,16,64,128]{3,2,1,0:T(8,128)(2,1)S(1)}, bf16[2,16,64,128]{3,2,1,0:T(8,128)(2,1)S(1)}, u32[]{:S(2)}, u32[]{:S(2)}) %collective-permute-start.21) | collective-permute-done | bytes 524320 | tf_op jit(solution)/shard_map/ppermute | solution.py:366
  77.9 1.5 %collective-permute-start.24 = (f32[2,8,512]{2,1,0:T(8,128)S(1)}, f32[2,8,512]{2,1,0:T(8,128)S(1)}, u32[]{:S(2)}, u32[]{:S(2)}) collective-permute-start(f32[2,8,512]{2,1,0:T(8,128)S(1)} %pad_maximum_fusion.5.refs_2_), channel_id=1, source_target_pairs={{0,4},{2,6},{4,0},{6,2},{1,5},{3,7},{5,1},{7,3},{8,12},{10,14},{12... | collective-permute-start | bytes 98312 | tf_op jit(solution)/shard_map/ppermute | solution.py:427
  79.4 2.6 %collective-permute-start.23 = (f32[2,8,512]{2,1,0:T(8,128)S(1)}, f32[2,8,512]{2,1,0:T(8,128)S(1)}, u32[]{:S(2)}, u32[]{:S(2)}) collective-permute-start(f32[2,8,512]{2,1,0:T(8,128)S(1)} %pad_maximum_fusion.5.refs_2_), channel_id=1, source_target_pairs={{0,2},{2,0},{4,6},{6,4},{1,3},{3,1},{5,7},{7,5},{8,10},{10,8},{12,... | collective-permute-start | bytes 98312 | tf_op jit(solution)/shard_map/ppermute | solution.py:427
  82.1 1.6 %collective-permute-done.25.refs_5_ = f32[2,8,512]{2,1,0:T(8,128)S(1)} collective-permute-done((f32[2,8,512]{2,1,0:T(8,128)S(1)}, f32[2,8,512]{2,1,0:T(8,128)S(1)}, u32[]{:S(2)}, u32[]{:S(2)}) %collective-permute-start.25) | collective-permute-done | bytes 32800 | tf_op jit(solution)/shard_map/ppermute | solution.py:427
  84.3 1.3 %collective-permute-done.28.refs_13_ = bf16[2,16,64,128]{3,2,1,0:T(8,128)(2,1)S(1)} collective-permute-done((bf16[2,16,64,128]{3,2,1,0:T(8,128)(2,1)S(1)}, bf16[2,16,64,128]{3,2,1,0:T(8,128)(2,1)S(1)}, u32[]{:S(2)}, u32[]{:S(2)}) %collective-permute-start.28) | collective-permute-done | bytes 524320 | tf_op jit(solution)/shard_map/ppermute | solution.py:346
  88.4 16.6 %conv2.1 = bf16[2,32,64,512]{3,2,1,0:T(8,128)(2,1)} custom-call(bf16[1440,512]{1,0:T(8,128)(2,1)} %get-tuple-element.26.refs_0_, f32[1,512]{1,0:T(1,128)} %bitcast.42, f32[2,8,512]{2,1,0:T(8,128)} %copy-done.8, f32[2,8,512]{2,1,0:T(8,128)} %copy-done.26, f32[2,8,512]{2,1,0:T(8,128)} %copy-done.25, f32[2,8,512]{2,1,0:T(8,128)} %copy-done.24, ...), custom_call_target="tpu_custom_call" | custom-call | flops 8589934592 | bytes 16777216 | tf_op jit(solution)/shard_map/conv2/pallas_call | solution.py:496
  (131 shorter events, 14.4 us)
Async XLA Ops:
  1.2 14.3 %collective-permute-start.2 = (bf16[12,512]{1,0:T(8,128)(2,1)S(1)}, bf16[12,512]{1,0:T(8,128)(2,1)S(1)}, u32[]{:S(2)}, u32[]{:S(2)}) collective-permute-start(bf16[12,512]{1,0:T(8,128)(2,1)S(1)} %reshape.85), channel_id=1, source_target_pairs={{0,2},{2,0},{4,6},{6,4},{1,3},{3,1},{5,7},{7,5},{8,10},{10,8},{12,... | collective-permute-start | bytes 36872 | tf_op jit(solution)/shard_map/ppermute | solution.py:362
  4.3 10.3 %collective-permute-start.1 = (bf16[12,512]{1,0:T(8,128)(2,1)S(1)}, bf16[12,512]{1,0:T(8,128)(2,1)S(1)}, u32[]{:S(2)}, u32[]{:S(2)}) collective-permute-start(bf16[12,512]{1,0:T(8,128)(2,1)S(1)} %reshape.85), channel_id=1, source_target_pairs={{0,4},{2,6},{4,0},{6,2},{1,5},{3,7},{5,1},{7,3},{8,12},{10,14},{12... | collective-permute-start | bytes 36872 | tf_op jit(solution)/shard_map/ppermute | solution.py:362
  6.8 8.4 %collective-permute-start = (bf16[12,512]{1,0:T(8,128)(2,1)S(1)}, bf16[12,512]{1,0:T(8,128)(2,1)S(1)}, u32[]{:S(2)}, u32[]{:S(2)}) collective-permute-start(bf16[12,512]{1,0:T(8,128)(2,1)S(1)} %reshape.85), channel_id=1, source_target_pairs={{0,6},{2,4},{4,2},{6,0},{1,7},{3,5},{5,3},{7,1},{8,14},{10,12},{12... | collective-permute-start | bytes 36872 | tf_op jit(solution)/shard_map/ppermute | solution.py:362
  7.8 15.6 %collective-permute-start.8 = (bf16[9,64,128]{2,1,0:T(8,128)(2,1)S(1)}, bf16[9,64,128]{2,1,0:T(8,128)(2,1)S(1)}, u32[]{:S(2)}, u32[]{:S(2)}) collective-permute-start(bf16[9,64,128]{2,1,0:T(8,128)(2,1)S(1)} %constant_dynamic-slice_fusion), channel_id=1, source_target_pairs={{0,6},{2,4},{4,2},{6,0},{1,7},{3,5},{5,3},{7,1},{8,14},{10,12},{12... | collective-permute-start | bytes 442376 | tf_op jit(solution)/shard_map/ppermute | solution.py:362
  11.7 11.7 %collective-permute-start.7 = (bf16[9,64,128]{2,1,0:T(8,128)(2,1)S(1)}, bf16[9,64,128]{2,1,0:T(8,128)(2,1)S(1)}, u32[]{:S(2)}, u32[]{:S(2)}) collective-permute-start(bf16[9,64,128]{2,1,0:T(8,128)(2,1)S(1)} %constant_dynamic-slice_fusion), channel_id=1, source_target_pairs={{0,4},{2,6},{4,0},{6,2},{1,5},{3,7},{5,1},{7,3},{8,12},{10,14},{12... | collective-permute-start | bytes 442376 | tf_op jit(solution)/shard_map/ppermute | solution.py:362
  14.6 8.8 %collective-permute-start.6 = (bf16[9,64,128]{2,1,0:T(8,128)(2,1)S(1)}, bf16[9,64,128]{2,1,0:T(8,128)(2,1)S(1)}, u32[]{:S(2)}, u32[]{:S(2)}) collective-permute-start(bf16[9,64,128]{2,1,0:T(8,128)(2,1)S(1)} %constant_dynamic-slice_fusion), channel_id=1, source_target_pairs={{0,2},{2,0},{4,6},{6,4},{1,3},{3,1},{5,7},{7,5},{8,10},{10,8},{12,... | collective-permute-start | bytes 442376 | tf_op jit(solution)/shard_map/ppermute | solution.py:362
  17.2 3.3 %collective-permute-start.4 = (bf16[9,64,512]{2,1,0:T(8,128)(2,1)S(1)}, bf16[9,64,512]{2,1,0:T(8,128)(2,1)}, u32[]{:S(2)}, u32[]{:S(2)}) collective-permute-start(bf16[9,64,512]{2,1,0:T(8,128)(2,1)S(1)} %bitcast.39), channel_id=1, source_target_pairs={{0,1},{1,0},{2,3},{3,2},{4,5},{5,4},{6,7},{7,6},{8,9},{9,8},{10,11... | collective-permute-start | bytes 1769480 | tf_op jit(solution)/shard_map/ppermute | solution.py:346
  23.4 15.0 %collective-permute-start.18 = (bf16[16,64,128]{2,1,0:T(8,128)(2,1)S(1)}, bf16[16,64,128]{2,1,0:T(8,128)(2,1)S(1)}, u32[]{:S(2)}, u32[]{:S(2)}) collective-permute-start(bf16[16,64,128]{2,1,0:T(8,128)(2,1)S(1)} %constant_dynamic-slice_fusion.1), channel_id=1, source_target_pairs={{0,4},{2,6},{4,0},{6,2},{1,5},{3,7},{5,1},{7,3},{8,12},{10,14},{12... | collective-permute-start | bytes 786440 | tf_op jit(solution)/shard_map/ppermute | solution.py:362
  25.8 14.0 %collective-permute-start.14 = (bf16[3,9,64,128]{3,2,1,0:T(8,128)(2,1)S(1)}, bf16[3,9,64,128]{3,2,1,0:T(8,128)(2,1)S(1)}, u32[]{:S(2)}, u32[]{:S(2)}) collective-permute-start(bf16[3,9,64,128]{3,2,1,0:T(8,128)(2,1)S(1)} %pad_maximum_fusion.1.refs_5_), channel_id=1, source_target_pairs={{0,24},{8,16},{16,8},{24,0},{1,25},{9,17},{17,9},{25,1},{2,26},{10... | collective-permute-start | bytes 1327112 | tf_op jit(solution)/shard_map/ppermute | solution.py:366
  28.3 20.0 %collective-permute-start.12 = (bf16[3,9,64,128]{3,2,1,0:T(8,128)(2,1)S(1)}, bf16[3,9,64,128]{3,2,1,0:T(8,128)(2,1)S(1)}, u32[]{:S(2)}, u32[]{:S(2)}) collective-permute-start(bf16[3,9,64,128]{3,2,1,0:T(8,128)(2,1)S(1)} %pad_maximum_fusion.1.refs_5_), channel_id=1, source_target_pairs={{0,16},{8,24},{16,0},{24,8},{1,17},{9,25},{17,1},{25,9},{2,18},{10... | collective-permute-start | bytes 1327112 | tf_op jit(solution)/shard_map/ppermute | solution.py:366
  28.8 19.6 %collective-permute-start.10 = (bf16[3,9,64,128]{3,2,1,0:T(8,128)(2,1)S(1)}, bf16[3,9,64,128]{3,2,1,0:T(8,128)(2,1)S(1)}, u32[]{:S(2)}, u32[]{:S(2)}) collective-permute-start(bf16[3,9,64,128]{3,2,1,0:T(8,128)(2,1)S(1)} %pad_maximum_fusion.1.refs_5_), channel_id=1, source_target_pairs={{0,8},{8,0},{16,24},{24,16},{1,9},{9,1},{17,25},{25,17},{2,10},{10... | collective-permute-start | bytes 1327112 | tf_op jit(solution)/shard_map/ppermute | solution.py:366
  38.4 10.4 %collective-permute-start.19 = (bf16[16,64,128]{2,1,0:T(8,128)(2,1)S(1)}, bf16[16,64,128]{2,1,0:T(8,128)(2,1)S(1)}, u32[]{:S(2)}, u32[]{:S(2)}) collective-permute-start(bf16[16,64,128]{2,1,0:T(8,128)(2,1)S(1)} %collective-permute-done.18), channel_id=1, source_target_pairs={{0,2},{2,0},{4,6},{6,4},{1,3},{3,1},{5,7},{7,5},{8,10},{10,8},{12,... | collective-permute-start | bytes 786440 | tf_op jit(solution)/shard_map/ppermute | solution.py:362
  38.8 12.1 %collective-permute-start.9 = (bf16[3,9,64,128]{3,2,1,0:T(8,128)(2,1)S(1)}, bf16[3,9,64,128]{3,2,1,0:T(8,128)(2,1)S(1)}, u32[]{:S(2)}, u32[]{:S(2)}) collective-permute-start(bf16[3,9,64,128]{3,2,1,0:T(8,128)(2,1)S(1)} %pad_maximum_fusion.1.refs_5_), channel_id=1, source_target_pairs={{0,1},{1,0},{2,3},{3,2},{4,5},{5,4},{6,7},{7,6},{8,9},{9,8},{10,11... | collective-permute-start | bytes 1327112 | tf_op jit(solution)/shard_map/ppermute | solution.py:346
  39.9 12.9 %collective-permute-start.15 = (bf16[3,9,64,128]{3,2,1,0:T(8,128)(2,1)S(1)}, bf16[3,9,64,128]{3,2,1,0:T(8,128)(2,1)S(1)}, u32[]{:S(2)}, u32[]{:S(2)}) collective-permute-start(bf16[3,9,64,128]{3,2,1,0:T(8,128)(2,1)S(1)} %collective-permute-done.14.refs_11_), channel_id=1, source_target_pairs={{0,1},{1,0},{2,3},{3,2},{4,5},{5,4},{6,7},{7,6},{8,9},{9,8},{10,11... | collective-permute-start | bytes 1327112 | tf_op jit(solution)/shard_map/ppermute | solution.py:346
  48.3 5.6 %collective-permute-start.13 = (bf16[3,9,64,128]{3,2,1,0:T(8,128)(2,1)S(1)}, bf16[3,9,64,128]{3,2,1,0:T(8,128)(2,1)S(1)}, u32[]{:S(2)}, u32[]{:S(2)}) collective-permute-start(bf16[3,9,64,128]{3,2,1,0:T(8,128)(2,1)S(1)} %collective-permute-done.12.refs_9_), channel_id=1, source_target_pairs={{0,1},{1,0},{2,3},{3,2},{4,5},{5,4},{6,7},{7,6},{8,9},{9,8},{10,11... | collective-permute-start | bytes 1327112 | tf_op jit(solution)/shard_map/ppermute | solution.py:346
  48.4 6.1 %collective-permute-start.11 = (bf16[3,9,64,128]{3,2,1,0:T(8,128)(2,1)S(1)}, bf16[3,9,64,128]{3,2,1,0:T(8,128)(2,1)}, u32[]{:S(2)}, u32[]{:S(2)}) collective-permute-start(bf16[3,9,64,128]{3,2,1,0:T(8,128)(2,1)S(1)} %collective-permute-done.10.refs_7_), channel_id=1, source_target_pairs={{0,1},{1,0},{2,3},{3,2},{4,5},{5,4},{6,7},{7,6},{8,9},{9,8},{10,11... | collective-permute-start | bytes 1327112 | tf_op jit(solution)/shard_map/ppermute | solution.py:346
  48.8 28.0 %collective-permute-start.17 = (bf16[16,64,512]{2,1,0:T(8,128)(2,1)S(1)}, bf16[16,64,512]{2,1,0:T(8,128)(2,1)S(1)}, u32[]{:S(2)}, u32[]{:S(2)}) collective-permute-start(bf16[16,64,512]{2,1,0:T(8,128)(2,1)S(1)} %bitcast.28), channel_id=1, source_target_pairs={{0,2},{2,0},{4,6},{6,4},{1,3},{3,1},{5,7},{7,5},{8,10},{10,8},{12,... | collective-permute-start | bytes 3145736 | tf_op jit(solution)/shard_map/ppermute | solution.py:362
  50.9 18.2 %collective-permute-start.22 = (bf16[2,16,64,128]{3,2,1,0:T(8,128)(2,1)S(1)}, bf16[2,16,64,128]{3,2,1,0:T(8,128)(2,1)S(1)}, u32[]{:S(2)}, u32[]{:S(2)}) collective-permute-start(bf16[2,16,64,128]{3,2,1,0:T(8,128)(2,1)S(1)} %pad_maximum_fusion.refs_10_), channel_id=1, source_target_pairs={{0,24},{8,16},{16,8},{24,0},{1,25},{9,17},{17,9},{25,1},{2,26},{10... | collective-permute-start | bytes 1572872 | tf_op jit(solution)/shard_map/ppermute | solution.py:366
  52.7 24.0 %collective-permute-start.21 = (bf16[2,16,64,128]{3,2,1,0:T(8,128)(2,1)S(1)}, bf16[2,16,64,128]{3,2,1,0:T(8,128)(2,1)S(1)}, u32[]{:S(2)}, u32[]{:S(2)}) collective-permute-start(bf16[2,16,64,128]{3,2,1,0:T(8,128)(2,1)S(1)} %pad_maximum_fusion.refs_10_), channel_id=1, source_target_pairs={{0,16},{8,24},{16,0},{24,8},{1,17},{9,25},{17,1},{25,9},{2,18},{10... | collective-permute-start | bytes 1572872 | tf_op jit(solution)/shard_map/ppermute | solution.py:366
  53.9 22.9 %collective-permute-start.20 = (bf16[2,16,64,128]{3,2,1,0:T(8,128)(2,1)S(1)}, bf16[2,16,64,128]{3,2,1,0:T(8,128)(2,1)S(1)}, u32[]{:S(2)}, u32[]{:S(2)}) collective-permute-start(bf16[2,16,64,128]{3,2,1,0:T(8,128)(2,1)S(1)} %pad_maximum_fusion.refs_10_), channel_id=1, source_target_pairs={{0,8},{8,0},{16,24},{24,16},{1,9},{9,1},{17,25},{25,17},{2,10},{10... | collective-permute-start | bytes 1572872 | tf_op jit(solution)/shard_map/ppermute | solution.py:366
  76.9 10.3 %collective-permute-start.26 = (bf16[16,64,512]{2,1,0:T(8,128)(2,1)S(1)}, bf16[16,64,512]{2,1,0:T(8,128)(2,1)S(1)}, u32[]{:S(2)}, u32[]{:S(2)}) collective-permute-start(bf16[16,64,512]{2,1,0:T(8,128)(2,1)S(1)} %collective-permute-done.17.refs_8_), channel_id=1, source_target_pairs={{0,1},{1,0},{2,3},{3,2},{4,5},{5,4},{6,7},{7,6},{8,9},{9,8},{10,11... | collective-permute-start | bytes 3145736 | tf_op jit(solution)/shard_map/ppermute | solution.py:346
  77.7 6.0 %collective-permute-start.25 = (f32[2,8,512]{2,1,0:T(8,128)S(1)}, f32[2,8,512]{2,1,0:T(8,128)S(1)}, u32[]{:S(2)}, u32[]{:S(2)}) collective-permute-start(f32[2,8,512]{2,1,0:T(8,128)S(1)} %pad_maximum_fusion.5.refs_2_), channel_id=1, source_target_pairs={{0,6},{2,4},{4,2},{6,0},{1,7},{3,5},{5,3},{7,1},{8,14},{10,12},{12... | collective-permute-start | bytes 98312 | tf_op jit(solution)/shard_map/ppermute | solution.py:427
  77.9 5.9 %collective-permute-start.24 = (f32[2,8,512]{2,1,0:T(8,128)S(1)}, f32[2,8,512]{2,1,0:T(8,128)S(1)}, u32[]{:S(2)}, u32[]{:S(2)}) collective-permute-start(f32[2,8,512]{2,1,0:T(8,128)S(1)} %pad_maximum_fusion.5.refs_2_), channel_id=1, source_target_pairs={{0,4},{2,6},{4,0},{6,2},{1,5},{3,7},{5,1},{7,3},{8,12},{10,14},{12... | collective-permute-start | bytes 98312 | tf_op jit(solution)/shard_map/ppermute | solution.py:427
  79.4 4.8 %collective-permute-start.23 = (f32[2,8,512]{2,1,0:T(8,128)S(1)}, f32[2,8,512]{2,1,0:T(8,128)S(1)}, u32[]{:S(2)}, u32[]{:S(2)}) collective-permute-start(f32[2,8,512]{2,1,0:T(8,128)S(1)} %pad_maximum_fusion.5.refs_2_), channel_id=1, source_target_pairs={{0,2},{2,0},{4,6},{6,4},{1,3},{3,1},{5,7},{7,5},{8,10},{10,8},{12,... | collective-permute-start | bytes 98312 | tf_op jit(solution)/shard_map/ppermute | solution.py:427
  (34 other events, 273.7 us)
